TPU v7x, 256 devices: a whole 4x4x8 slice. The times are simulated.
256 devices in a mesh: dev: 64 (over x, z, core), tp: 4 (over y).
Axes of the slice: x: 4, y: 4, z: 8, core: 2. Of those that a mesh axis runs over, the one named last changes fastest.
Arguments:
- hidden: bfloat16 [512, 2, 7168], P('dev', None, 'tp'), may hold values from -6 to 6
- queries: bfloat16 [512, 2, 128, 576], P(('dev', 'tp'))
- latent_cache: bfloat16 [512, 256, 576], P(('dev', 'tp'))
- new_latent: bfloat16 [512, 2, 576], P(('dev', 'tp')), may hold values from -6 to 6
- lengths: int32 [512], P(('dev', 'tp')), may hold values from 17 to 256
- value_proj: bfloat16 [128, 512, 128], P('dev'), may hold values from -0.25 to 0.25
- out_proj: bfloat16 [16384, 7168], P('dev', 'tp'), may hold values from -0.046875 to 0.046875
- norm_gain: float32 [7168], P('tp'), may hold values from 0.1 to 1.9
- w_gate: bfloat16 [64, 7168, 1024], P('dev', None, 'tp'), may hold values from -0.0625 to 0.0625
- w_up: bfloat16 [64, 7168, 1024], P('dev', None, 'tp'), may hold values from -0.0625 to 0.0625
- w_down: bfloat16 [64, 1024, 7168], P('dev', 'tp'), may hold values from -0.1875 to 0.1875
- routes: int32 [512, 2, 8], P('dev'), may hold values from 0 to 63, all different within a row; in each aligned block of 16 rows (0 to 15, 16 to 31, ..., all dimensions but the last counted through in order) at most 4 rows name the same one
- route_gates: bfloat16 [512, 2, 8], P('dev'), may hold values from 0.049804688 to 0.44921875
Outputs:
- layer_out: bfloat16 [512, 2, 7168], P('dev', None, 'tp')
Inputs may be any that keep to these rules, and one draw needn't show every extreme that they name: `routes`: among the 8 rows of one dev index, both steps taken together, no expert is named more than 4 times, a bound that some block reaches.
All inputs are finite; a program needn't handle non-finite values.
Results may differ from a plain program's by a relative error of at most 0.014.
Values may be sent and summed in bfloat16 or wider, within the bound.
No kernel may reach another device: no remote copies, remote signals or barrier semaphores. Data moves between devices by JAX's collectives and lax.ppermute only.
A program may use at most 128 MiB of HBM per device.

v0:
```python
import jax
import jax.numpy as jnp
from jax import lax
from jax.sharding import PartitionSpec as P

D = 7168
LAT = 512
ROPE = 64
VDIM = 128
TOP = 8
STEPS = 2
CTX = 256


NEGATIVE = -1e30


def fold_block(running, scores, allowed, values):
    running_max, running_sum, weighted_sum = running
    masked = jnp.where(allowed, scores, NEGATIVE)
    new_max = jnp.maximum(running_max, jnp.max(masked, axis=-1))
    factor = jnp.exp(running_max - new_max)
    weights = jnp.where(allowed, jnp.exp(scores - new_max[..., None]), 0.0)
    running_sum = running_sum * factor + jnp.sum(weights, axis=-1)
    weighted_sum = weighted_sum * factor[..., None] + jnp.einsum(
        "shc,cl->shl", weights.astype(jnp.bfloat16), values, preferred_element_type=jnp.float32
    )
    return (new_max, running_sum, weighted_sum)


def attend_one(query_row, latent_rows, new_rows, row_length, block_count):
    block_width = min(128, latent_rows.shape[0])
    score_scale = (VDIM + ROPE) ** (-0.5)
    step_total, head_total = (query_row.shape[0], query_row.shape[1])
    initial = (
        jnp.full((step_total, head_total), NEGATIVE, jnp.float32),
        jnp.zeros((step_total, head_total), jnp.float32),
        jnp.zeros((step_total, head_total, LAT), jnp.float32),
    )

    def block_step(block_index, running):
        key_block = lax.dynamic_slice_in_dim(latent_rows, block_index * block_width, block_width, 0)
        scores = (
            jnp.einsum("shk,ck->shc", query_row, key_block, preferred_element_type=jnp.float32)
            * score_scale
        )
        allowed = block_index * block_width + jnp.arange(block_width) < row_length
        return fold_block(running, scores, allowed[None, None, :], key_block[:, :LAT])

    running = lax.fori_loop(0, block_count, block_step, initial)
    scores = (
        jnp.einsum("shk,ck->shc", query_row, new_rows, preferred_element_type=jnp.float32)
        * score_scale
    )
    allowed = jnp.arange(step_total)[None, :] <= jnp.arange(step_total)[:, None]
    final_max, final_sum, final_weighted = fold_block(
        running, scores, allowed[:, None, :], new_rows[:, :LAT]
    )
    return (final_weighted / final_sum[..., None]).astype(jnp.bfloat16)


def on_device(
    hidden,
    queries,
    latent_cache,
    new_latent,
    lengths,
    value_proj,
    out_proj,
    norm_gain,
    w_gate,
    w_up,
    w_down,
    routes,
    route_gates,
):
    own_rows = queries.shape[0]
    block_width = min(128, CTX)

    def block_total(length_values):
        return (length_values + block_width - 1) // block_width

    context = jnp.stack(
        [
            attend_one(
                queries[row_number],
                latent_cache[row_number],
                new_latent[row_number],
                lengths[row_number],
                block_total(lengths[row_number]),
            )
            for row_number in range(own_rows)
        ]
    )
    spread = lax.all_to_all(context, "dev", split_axis=2, concat_axis=0, tiled=True)
    projected = jnp.einsum(
        "nshl,hlv->nshv", spread, value_proj, preferred_element_type=jnp.float32
    ).astype(jnp.bfloat16)
    projected = projected.reshape(projected.shape[0], STEPS, -1)
    gathered = lax.all_gather(projected, "tp", axis=0, tiled=True)
    tp_count = lax.axis_size("tp")
    dev_count = lax.axis_size("dev")
    ordered = gathered.reshape(tp_count, dev_count, own_rows, STEPS, -1).transpose(1, 0, 2, 3, 4)
    ordered = ordered.reshape(dev_count * tp_count * own_rows * STEPS, -1)
    attention = lax.psum_scatter(
        jnp.dot(ordered, out_proj, preferred_element_type=jnp.float32),
        "dev",
        scatter_dimension=0,
        tiled=True,
    ).astype(jnp.bfloat16)
    residual = hidden.astype(jnp.float32) + attention.reshape(hidden.shape).astype(jnp.float32)
    squares = lax.psum(jnp.sum(residual * residual, axis=-1), "tp")
    normed = (residual * lax.rsqrt(squares / D + 1e-06)[..., None] * norm_gain).astype(jnp.bfloat16)
    token_count = hidden.shape[0] * STEPS
    pair_ids = routes.reshape(-1)
    pair_count = pair_ids.shape[0]
    expert_count = dev_count * w_gate.shape[0]
    capacity = 2 * token_count * TOP // expert_count
    ordinal = jnp.arange(pair_count)
    earlier = (pair_ids[:, None] == pair_ids[None, :]) & (ordinal[None, :] < ordinal[:, None])
    slot_index = jnp.sum(earlier.astype(jnp.int32), axis=1)
    target = pair_ids * capacity + slot_index
    placed = (target[:, None] == jnp.arange(expert_count * capacity)[None, :]).astype(jnp.float32)
    token_owner = ((ordinal // TOP)[:, None] == jnp.arange(token_count)[None, :]).astype(
        jnp.float32
    )
    spread_matrix = jnp.einsum(
        "pe,pt->et", placed, token_owner, precision=lax.Precision.HIGHEST
    ).astype(jnp.bfloat16)
    gate_values = route_gates.reshape(-1).astype(jnp.float32)
    combine_matrix = jnp.einsum(
        "pt,pe->te", token_owner, placed * gate_values[:, None], precision=lax.Precision.HIGHEST
    ).astype(jnp.bfloat16)
    flat_normed = normed.reshape(token_count, -1)
    gate_local, up_local, down_local = (w_gate[0], w_up[0], w_down[0])
    full_tokens = lax.all_gather(flat_normed, "tp", axis=1, tiled=True)
    outgoing_tokens = jnp.dot(spread_matrix, full_tokens, preferred_element_type=jnp.float32)
    outgoing_tokens = outgoing_tokens.astype(jnp.bfloat16).reshape(expert_count, capacity, -1)
    arrived = lax.all_to_all(outgoing_tokens, "dev", split_axis=0, concat_axis=0, tiled=True)
    sources = arrived.shape[0]
    slots_here = arrived.shape[1]
    flat_tokens = arrived.reshape(sources * slots_here, -1)
    gate_sum = jnp.dot(flat_tokens, gate_local, preferred_element_type=jnp.float32)
    up_sum = jnp.dot(flat_tokens, up_local, preferred_element_type=jnp.float32)
    activation = (jax.nn.silu(gate_sum) * up_sum).astype(jnp.bfloat16)
    partial_out = jnp.dot(activation, down_local, preferred_element_type=jnp.float32)
    partial_out = partial_out.reshape(sources, slots_here, -1)
    summed = lax.psum_scatter(
        partial_out.astype(jnp.bfloat16), "tp", scatter_dimension=2, tiled=True
    )
    returned_rows = lax.all_to_all(summed, "dev", split_axis=0, concat_axis=0, tiled=True)
    expert_mix = jnp.dot(
        combine_matrix,
        returned_rows.reshape(expert_count * capacity, -1),
        preferred_element_type=jnp.float32,
    )
    layer_out = (residual + expert_mix.reshape(residual.shape)).astype(jnp.bfloat16)
    return layer_out


def solution(mesh):
    in_specs = (
        P("dev", None, "tp"),
        P(("dev", "tp"), None, None, None),
        P(("dev", "tp"), None, None),
        P(("dev", "tp"), None, None),
        P(("dev", "tp")),
        P("dev", None, None),
        P("dev", "tp"),
        P("tp"),
        P("dev", None, "tp"),
        P("dev", None, "tp"),
        P("dev", "tp", None),
        P("dev", None, None),
        P("dev", None, None),
    )
    out_specs = P("dev", None, "tp")
    return jax.shard_map(
        on_device, mesh=mesh, in_specs=in_specs, out_specs=out_specs, check_vma=False
    )
```

profile of v0, /device:TPU:1, one launch (start us, length us, event | category | flops | bytes accessed | tf_op | source)
XLA Modules:
  0.0 449.0 jit_solution(18396351511817903357)
XLA Ops:
  6.5 1.4 fusion.55
  9.2 1.1 slice_bitcast_fusion.2
  10.3 1.1 convolution_multiply_fusion.2
  11.5 0.7 slice_bitcast_fusion.9
  12.2 1.1 slice_bitcast_fusion.3
  13.4 1.4 while.28
  13.4 0.6 add_compare_fusion.4
  14.9 1.6 while.29
  14.9 0.7 add_compare_fusion.5
  17.6 0.5 copy.78
  18.1 32.1 %all_to_all.28 = bf16[2,2,128,512]{3,1,0,2:T(2,128)(2,1)S(1)} all-to-all(bf16[2,2,128,512]{3,1,0,2:T(2,128)(2,1)S(1)} %copy.78), channel_id=1, replica_groups=mesh['dev'=64,'tp'=4] {'dev'}, dimensions={2} | all-to-all | bytes 1048576 | tf_op jit(solution)/shard_map/all_to_all | solution.py:95
  51.2 11.9 %all_gather.6 = bf16[512,2,256]{0,2,1:T(8,128)(2,1)S(1)} all-gather(bf16[128,2,256]{0,2,1:T(8,128)(2,1)S(1)} %bitcast.124), channel_id=1, replica_groups=mesh['dev'=64,'tp'=4] {'tp'}, dimensions={0}, use_global_device_ids=true | all-gather | bytes 655360 | tf_op jit(solution)/shard_map/all_gather | solution.py:100
  63.1 0.4 copy.82
  64.1 4.1 fusion.56
  68.3 0.6 copy-done.5
  69.5 142.3 %reduce-scatter.3.cloned.1.call-done = f32[16,1792]{1,0:T(8,128)} async-done(((f32[1024,1792]{1,0:T(8,128)}), f32[16,1792]{1,0:T(8,128)}) %reduce-scatter.3.cloned.1.call-update) | async-done | bytes 114704 | tf_op jit(solution)/shard_map/reduce_scatter | solution.py:105
  211.7 0.9 convert_convert_fusion
  212.8 8.4 %psum.7 = f32[8,2]{0,1:T(2,128)S(1)} all-reduce(f32[8,2]{0,1:T(2,128)S(1)} %multiply_reduce_fusion), channel_id=1, replica_groups=mesh['dev'=64,'tp'=4] {'tp'}, use_global_device_ids=true, to_apply=%region_15.16 | all-reduce | flops 16 | bytes 128 | tf_op jit(solution)/shard_map/psum | solution.py:112
  221.4 9.3 %all_gather.7 = bf16[16,7168]{1,0:T(8,128)(2,1)S(1)} all-gather(bf16[16,1792]{1,0:T(8,128)(2,1)S(1)} %reshape.99), channel_id=1, replica_groups=mesh['dev'=64,'tp'=4] {'tp'}, dimensions={1}, use_global_device_ids=true | all-gather | bytes 286720 | tf_op jit(solution)/shard_map/all_gather | solution.py:136
  230.7 3.0 convolution_convert_fusion.1
  233.7 7.0 %reshape.100 = bf16[64,4,7168]{2,1,0:T(4,128)(2,1)} reshape(bf16[256,7168]{1,0:T(8,128)(2,1)} %convolution_convert_fusion.1) | data formatting | bytes 7340032 | tf_op jit(solution)/shard_map/reshape | solution.py:138
  240.7 102.4 %all_to_all.29 = bf16[64,4,7168]{2,1,0:T(4,128)(2,1)} all-to-all(bf16[64,4,7168]{2,1,0:T(4,128)(2,1)} %reshape.100), channel_id=1, replica_groups=mesh['dev'=64,'tp'=4] {'dev'}, dimensions={0} | all-to-all | bytes 7340032 | tf_op jit(solution)/shard_map/all_to_all | solution.py:139
  343.1 6.7 %reshape.101 = bf16[256,7168]{1,0:T(8,128)(2,1)} reshape(bf16[64,4,7168]{2,1,0:T(4,128)(2,1)} %all_to_all.29) | data formatting | bytes 7340032 | tf_op jit(solution)/shard_map/reshape | solution.py:142
  349.9 4.4 fusion.19
  354.3 0.9 copy-done.9
  355.2 1.1 fusion.31
  356.4 5.0 %convolution_convert_fusion = bf16[64,4,7168]{2,0,1:T(8,128)(2,1)} fusion(bf16[1,256,7168]{2,1,0:T(8,128)(2,1)} %param.27, bf16[64,4,256]{2,1,0:T(4,128)(2,1)S(1)} %dot_general.67), kind=kOutput, calls=%fused_computation.36 | convolution fusion | flops 941359104 | bytes 7471104 | tf_op jit(solution)/shard_map/dot_general | solution.py:146
  361.3 40.5 %reduce-scatter.5.cloned.1.call-done = bf16[64,4,1792]{2,0,1:T(8,128)(2,1)} async-done(((bf16[64,4,7168]{2,0,1:T(8,128)(2,1)}), bf16[64,4,1792]{2,0,1:T(8,128)(2,1)}) %reduce-scatter.5.cloned.1.call-update) | async-done | bytes 917520 | tf_op jit(solution)/shard_map/reduce_scatter | solution.py:148
  401.9 2.8 copy.87
  404.7 10.6 %all-to-all-start.2 = ((bf16[64,4,1792]{2,1,0:T(4,128)(2,1)}), bf16[64,4,1792]{2,1,0:T(4,128)(2,1)S(1)}, u32[]{:S(2)}, u32[]{:S(2)}) async-start(bf16[64,4,1792]{2,1,0:T(4,128)(2,1)} %copy.87), calls=%async_computation.4 | async-start | bytes 1835008 | tf_op jit(solution)/shard_map/all_to_all | solution.py:151
  415.7 25.3 %all-to-all-done.2 = bf16[64,4,1792]{2,1,0:T(4,128)(2,1)S(1)} async-done(((bf16[64,4,1792]{2,1,0:T(4,128)(2,1)}), bf16[64,4,1792]{2,1,0:T(4,128)(2,1)S(1)}, u32[]{:S(2)}, u32[]{:S(2)}) %all-to-all-start.2) | async-done | bytes 917536 | tf_op jit(solution)/shard_map/all_to_all | solution.py:151
  441.5 0.7 copy.89
  (71 shorter events, 6.0 us)
Async XLA Ops:
  6.5 57.6 %copy-start = (bf16[256,1792]{1,0:T(8,128)(2,1)S(1)}, bf16[256,1792]{1,0:T(8,128)(2,1)}, u32[]{:S(2)}) copy-start(bf16[256,1792]{1,0:T(8,128)(2,1)} %param.23) | copy-start | bytes 2752516
  6.5 205.2 %reduce-scatter.3.cloned.1.call-start = ((), (), s32[]{:S(2)}) async-start(), calls=%async_computation.5 | async-start | bytes 7454720 | tf_op jit(solution)/shard_map/reduce_scatter | solution.py:105
  14.9 1.6 copy-start.2
  14.9 1.6 copy-start.7
  17.2 33.7 %copy-start.4 = (bf16[2,512,128]{2,1,0:T(8,128)(2,1)S(1)}, bf16[2,512,128]{2,1,0:T(8,128)(2,1)}, u32[]{:S(2)}) copy-start(bf16[2,512,128]{2,1,0:T(8,128)(2,1)} %param.22) | copy-start | bytes 786436
  68.2 0.7 copy-start.5
  68.2 144.5 %copy-start.3 = (bf16[8,2,1792]{2,1,0:T(2,128)(2,1)S(1)}, bf16[8,2,1792]{2,1,0:T(2,128)(2,1)}, u32[]{:S(2)}) copy-start(bf16[8,2,1792]{2,1,0:T(2,128)(2,1)} %param.17) | copy-start | bytes 172036
  68.2 153.0 %copy-start.6 = (f32[1792]{0:T(1024)S(1)}, f32[1792]{0:T(1024)}, u32[]{:S(2)}) copy-start(f32[1792]{0:T(1024)} %param.24) | copy-start | bytes 21508
  68.3 333.6 %reduce-scatter.5.cloned.1.call-start = ((), (), s32[]{:S(2)}) async-start(), calls=%async_computation.6 | async-start | bytes 4587520 | tf_op jit(solution)/shard_map/reduce_scatter | solution.py:148
  349.9 4.4 copy-start.1
  349.9 5.3 %copy-start.9 = (bf16[1,7168,256]{2,1,0:T(8,128)(2,1)S(1)}, bf16[1,7168,256]{2,1,0:T(8,128)(2,1)}, u32[]{:S(2)}) copy-start(bf16[1,7168,256]{2,1,0:T(8,128)(2,1)} %param.26) | copy-start | bytes 11010052
  361.3 54.0 %copy-start.8 = (bf16[8,2,8]{2,1,0:T(2,128)(2,1)S(1)}, bf16[8,2,8]{2,1,0:T(2,128)(2,1)}, u32[]{:S(2)}) copy-start(bf16[8,2,8]{2,1,0:T(2,128)(2,1)} %param.29) | copy-start | bytes 772
  404.7 36.4 %all-to-all-start.2 = ((bf16[64,4,1792]{2,1,0:T(4,128)(2,1)}), bf16[64,4,1792]{2,1,0:T(4,128)(2,1)S(1)}, u32[]{:S(2)}, u32[]{:S(2)}) async-start(bf16[64,4,1792]{2,1,0:T(4,128)(2,1)} %copy.87), calls=%async_computation.4 | async-start | bytes 1835008 | tf_op jit(solution)/shard_map/all_to_all | solution.py:151
Sparse Core Ops, SparseCore 0:
  68.4 143.3 reduce-scatter.2
  361.5 40.3 reduce-scatter.4
where the time goes:
time: 450 us; the launch traced here: 449 us
  waiting for transfers between devices  208 us (46%)
  blocking collectives  164 us (36%)
  local copies, waits for them, and re-layouts  25.9 us (6%)
  matrix products  21.9 us (5%)
  between operations  15.1 us (3%)
  starting transfers between devices  10.6 us (2%)
    reduce_scatter x1, waiting for transfers between devices, on_device(): lax.psum_scatter(jnp.dot(ordered, out_proj, preferred_element_type=jnp.fl...  142 us
    all_to_all x1, blocking collectives, on_device(): lax.all_to_all(outgoing_tokens, 'dev', split_axis=0, concat_axis=0, tiled...  102 us
    reduce_scatter x1, waiting for transfers between devices, on_device(): lax.psum_scatter(partial_out.astype(jnp.bfloat16), 'tp', scatter_dimensio...  40.5 us
    all_to_all x1, blocking collectives, on_device(): lax.all_to_all(context, 'dev', split_axis=2, concat_axis=0, tiled=True)  32.1 us
    all_to_all x1, waiting for transfers between devices, on_device(): lax.all_to_all(summed, 'dev', split_axis=0, concat_axis=0, tiled=True)  25.3 us
    all_gather x1, blocking collectives, on_device(): gathered = lax.all_gather(projected, 'tp', axis=0, tiled=True)  11.9 us
    all_to_all x1, starting transfers between devices, on_device(): lax.all_to_all(summed, 'dev', split_axis=0, concat_axis=0, tiled=True)  10.6 us
    all_gather x1, blocking collectives, on_device(): full_tokens = lax.all_gather(flat_normed, 'tp', axis=1, tiled=True)  9.3 us
  transfers between devices with their start and end apart: 3, of which 3 were waited for; matrix products, arithmetic and copies ran while one was open for 0% of the time, Pallas kernels for 0%

commit v1 on v0

v1 whole, which is shorter than its diff:
```python
import jax
import jax.numpy as jnp
from jax import lax
from jax.sharding import Mesh, PartitionSpec as P

EPS = 1e-06
CAP = 4
NC = 2
F32 = jnp.float32
BF16 = jnp.bfloat16
CHIPS = ("x", "z")


def swap(value):
    return lax.ppermute(value, "c", [(0, 1), (1, 0)])


def send_y(value, distance):
    size = lax.axis_size("y")
    return lax.ppermute(value, "y", [(i, (i + distance) % size) for i in range(size)])


def in_core_order(core, own, other, axis=0):
    first = jnp.where(core == 0, own, other)
    second = jnp.where(core == 0, other, own)
    return jnp.concatenate([first, second], axis=axis)


def attend(queries, cache, new_latent, lengths, lat, scale):
    steps = queries.shape[1]
    scores = jnp.einsum("nshk,nck->nshc", queries, cache, preferred_element_type=F32) * scale
    fresh = jnp.einsum("nshk,njk->nshj", queries, new_latent, preferred_element_type=F32) * scale
    seen = jnp.arange(cache.shape[1])[None, :] < lengths[:, None]
    scores = jnp.where(seen[:, None, None, :], scores, -jnp.inf)
    known = jnp.arange(steps)[None, :] <= jnp.arange(steps)[:, None]
    fresh = jnp.where(known[None, :, None, :], fresh, -jnp.inf)
    top = jnp.maximum(jnp.max(scores, axis=-1), jnp.max(fresh, axis=-1))[..., None]
    scores = jnp.exp(scores - top)
    fresh = jnp.exp(fresh - top)
    total = (jnp.sum(scores, axis=-1) + jnp.sum(fresh, axis=-1))[..., None]
    old_part = jnp.einsum(
        "nshc,ncl->nshl", (scores / total).astype(BF16), cache[:, :, :lat], preferred_element_type=F32
    )
    new_part = jnp.einsum(
        "nshj,njl->nshl", (fresh / total).astype(BF16), new_latent[:, :, :lat], preferred_element_type=F32
    )
    return (old_part + new_part).astype(BF16)


def slots_of(ids):
    flat = ids.reshape(-1)
    order = jnp.arange(flat.shape[0])
    earlier = (flat[:, None] == flat[None, :]) & (order[None, :] < order[:, None])
    return jnp.sum(earlier.astype(jnp.int32), axis=1).reshape(ids.shape)


def on_device(
    hidden,
    queries,
    latent_cache,
    new_latent,
    lengths,
    value_proj,
    out_proj,
    norm_gain,
    w_gate,
    w_up,
    w_down,
    routes,
    route_gates,
):
    core = lax.axis_index("c")
    y = lax.axis_index("y")
    ny = lax.axis_size("y")
    chips = lax.axis_size("x") * lax.axis_size("z")
    rows, steps, heads, kv = queries.shape
    heads_core, lat, vdim = value_proj.shape
    rope = kv - lat
    cols = hidden.shape[2]
    half = cols // NC
    width = cols * ny
    own_tokens = rows * steps
    group = own_tokens * ny
    heads_chip = heads_core * NC

    def half_of(value, which):
        return lax.dynamic_slice_in_dim(value, which * half, half, value.ndim - 1)

    vp = in_core_order(core, value_proj, swap(value_proj))
    op = in_core_order(core, half_of(out_proj, core), swap(half_of(out_proj, 1 - core)))
    flat_hidden = hidden.reshape(group, cols)
    chip_hidden = in_core_order(
        core, half_of(flat_hidden, core)[None], swap(half_of(flat_hidden, 1 - core))[None]
    )
    ids = routes.reshape(group, -1)
    gates = route_gates.reshape(group, -1)
    chip_ids = in_core_order(core, ids[None], swap(ids)[None])
    chip_gates = in_core_order(core, gates[None], swap(gates)[None]).astype(F32)

    context = attend(queries, latent_cache, new_latent, lengths, lat, (vdim + rope) ** (-0.5))
    context = context.reshape(own_tokens, chips, heads_chip, lat).transpose(1, 0, 2, 3)
    context = lax.all_to_all(context, CHIPS, 0, 0, tiled=True)
    values = jnp.einsum("nthl,hlv->nthv", context, vp, preferred_element_type=F32).astype(BF16)
    values = values.reshape(chips, own_tokens, heads_chip * vdim)

    blocks = [values] + [send_y(values, d) for d in range(1, ny)]
    mine = jnp.stack(blocks, axis=1)
    both = jnp.stack([mine, swap(mine)], axis=1)

    down_own = w_down[0]

    def down_block(block):
        return lax.dynamic_slice_in_dim(down_own, (block % ny) * cols, cols, 1)

    near = (1, ny - 1)
    early = [send_y(down_block(y + d), d) for d in near]
    both, *early = lax.optimization_barrier((both, *early))
    partial_sums = jnp.dot(
        both.reshape(-1, heads_chip * vdim), op, preferred_element_type=F32
    ).astype(BF16)
    partial_sums = partial_sums.reshape(chips, NC * group, half)
    arrived = lax.all_to_all(partial_sums, CHIPS, 0, 0, tiled=True)
    attention = jnp.sum(arrived.astype(F32), axis=0).astype(BF16)
    attention = attention.reshape(NC, ny, own_tokens, half)
    core_order = (jnp.arange(NC) + core) % NC
    y_order = (y - jnp.arange(ny)) % ny
    attention = attention[core_order][:, y_order].reshape(NC, group, half)
    residual = chip_hidden.astype(F32) + attention.astype(F32)
    gain = half_of(norm_gain, core)
    scaled = (residual * gain).astype(BF16).reshape(NC * group, half)
    other_half = swap(lax.dynamic_index_in_dim(residual, 1 - core, 0, keepdims=False))
    own_half = lax.dynamic_index_in_dim(residual, core, 0, keepdims=False)
    full_residual = in_core_order(core, own_half, other_half, axis=1)

    chip_slots = jnp.stack([slots_of(chip_ids[0]), slots_of(chip_ids[1])])
    group_of = jnp.arange(NC)[:, None, None]
    row_of = (chip_ids * NC + group_of) * CAP + chip_slots
    row_of = row_of.reshape(NC * group, -1)
    row_count = chips * NC * NC * CAP
    named = row_of[:, :, None] == jnp.arange(row_count)[None, None, :]
    spread = jnp.sum(named.astype(F32), axis=1).astype(BF16)
    combine = jnp.sum(named.astype(F32) * chip_gates.reshape(NC * group, -1)[:, :, None], axis=1)
    combine = combine.astype(BF16).reshape(NC * group, chips, NC, NC * CAP)
    combine = lax.dynamic_index_in_dim(combine, core, 2, keepdims=False)
    outgoing = lax.dot_general(
        spread, scaled, (((0,), (0,)), ((), ())), preferred_element_type=F32
    ).astype(BF16)
    outgoing = outgoing.reshape(chips, NC * NC * CAP, half)
    tokens = lax.all_to_all(outgoing, CHIPS, 0, 0, tiled=True)
    tokens = tokens.reshape(chips, NC, NC * CAP, half)
    kept = lax.dynamic_index_in_dim(tokens, core, 1, keepdims=False)
    received = swap(lax.dynamic_index_in_dim(tokens, 1 - core, 1, keepdims=False))
    slots = chips * NC * CAP
    tokens = in_core_order(core, kept.reshape(slots, half), received.reshape(slots, half), axis=1)

    gate_w, up_w, down_own, _ = lax.optimization_barrier((w_gate[0], w_up[0], down_own, mine))

    def up_block(block):
        start = (block % ny) * cols
        return jnp.concatenate(
            [
                lax.dynamic_slice_in_dim(gate_w, start, cols, 0),
                lax.dynamic_slice_in_dim(up_w, start, cols, 0),
            ],
            axis=1,
        )

    up_parts = [up_block(y)] + [send_y(up_block(y + d), d) for d in range(1, ny)]
    down_parts = {0: down_block(y), **dict(zip(near, early))}
    for d in range(1, ny):
        if d not in near:
            down_parts[d] = send_y(down_block(y + d), d)

    column_gain = norm_gain
    shares = jnp.sum(jnp.square(tokens.astype(F32) / column_gain), axis=1)
    squares = shares
    for d in range(1, ny):
        squares = squares + send_y(shares, d)
    row_scale = lax.rsqrt(squares / width + EPS)[:, None]
    sums = jnp.dot(tokens, up_parts[0], preferred_element_type=F32)
    for d in range(1, ny):
        part = jnp.dot(tokens, up_parts[d], preferred_element_type=F32).astype(BF16)
        sums = sums + send_y(part, -d).astype(F32)
    sums = sums * row_scale
    units = sums.shape[1] // 2
    act = (jax.nn.silu(sums[:, :units]) * sums[:, units:]).astype(BF16)
    result = jnp.dot(act, down_parts[0], preferred_element_type=F32)
    for d in range(1, ny):
        result = result + jnp.dot(send_y(act, d), down_parts[d], preferred_element_type=F32)
    result = result.astype(BF16).reshape(chips, NC * CAP, cols)

    returned = lax.all_to_all(result, CHIPS, 0, 0, tiled=True).reshape(slots, cols)
    mixture = jnp.dot(
        combine.reshape(NC * group, slots), returned, preferred_element_type=F32
    ).reshape(NC, group, cols)
    mixture_own = lax.dynamic_index_in_dim(mixture, core, 0, keepdims=False)
    mixture_other = swap(lax.dynamic_index_in_dim(mixture, 1 - core, 0, keepdims=False))
    layer_out = full_residual + (mixture_own + mixture_other)
    return layer_out.astype(BF16).reshape(hidden.shape)


def split_mesh(mesh, nz):
    dev_count, y_count = mesh.devices.shape
    nx = dev_count // (NC * nz)
    return Mesh(mesh.devices.reshape(nx, nz, NC, y_count), ("x", "z", "c", "y"))


def solution(mesh, nz=8):
    dev = ("x", "z", "c")
    both = ("x", "z", "c", "y")
    in_specs = (
        P(dev, None, "y"),
        P(both, None, None, None),
        P(both, None, None),
        P(both, None, None),
        P(both),
        P(dev, None, None),
        P(dev, "y"),
        P("y"),
        P(dev, None, "y"),
        P(dev, None, "y"),
        P(dev, "y", None),
        P(dev, None, None),
        P(dev, None, None),
    )
    return jax.shard_map(
        on_device,
        mesh=split_mesh(mesh, nz),
        in_specs=in_specs,
        out_specs=P(dev, None, "y"),
        check_vma=False,
    )
```

time: 450 us -> 310 us (0.69)
  blocking collectives: 164 us -> 0 us
  starting transfers between devices: 10.6 us -> 114 us
  waiting for transfers between devices: 208 us -> 146 us
  between operations: 15.1 us -> 0.65 us
  other arithmetic: 3.01 us -> 12 us
  local copies, waits for them, and re-layouts: 25.9 us -> 17.5 us
    reduce_scatter x2 -> x0, waiting for transfers between devices: 183 us -> none  [the longest x1 142 us: on_device(): lax.psum_scatter(jnp.dot(ordered, out_proj, preferred_element_type=jnp.fl...]
    all_to_all x2 -> x0, blocking collectives: 135 us -> none  [the longest x1 102 us: on_device(): lax.all_to_all(outgoing_tokens, 'dev', split_axis=0, concat_axis=0, tiled...]
    ppermute x0 -> x27, starting transfers between devices: none -> 77.8 us  [the longest x18 52.5 us: send_y(): lax.ppermute(value, 'y', [(i, (i + distance) % size) for i in range(size)])]
    ppermute x0 -> x27, waiting for transfers between devices: none -> 62.5 us  [the longest x18 58.4 us: send_y(): lax.ppermute(value, 'y', [(i, (i + distance) % size) for i in range(size)])]
    all_to_all x1 -> x4, waiting for transfers between devices: 25.3 us -> 83.7 us  [the longest x1 40 us: on_device(): arrived = lax.all_to_all(partial_sums, CHIPS, 0, 0, tiled=True)]
    all_to_all x1 -> x4, starting transfers between devices: 10.6 us -> 35.8 us  [the longest x1 11.9 us: on_device(): context = lax.all_to_all(context, CHIPS, 0, 0, tiled=True)]
    all_gather x2 -> x0, blocking collectives: 21.2 us -> none  [the longest x1 11.9 us: on_device(): gathered = lax.all_gather(projected, 'tp', axis=0, tiled=True)]
    reshape x6 -> x7, local copies, waits for them, and re-layouts: 14.3 us -> 2.99 us  [the longest x2 1.33 us: on_device(): context.reshape(own_tokens, chips, heads_chip, lat).transpose(1, 0, 2, 3)]
  transfers between devices with their start and end apart: 3 -> 31, of which waited for: 3 -> 16; matrix products, arithmetic and copies ran while one was open for 0% -> 10% of each run, Pallas kernels for 0% -> 0%
where the time goes in v1:
time: 310 us; the launch traced here: 309 us
  waiting for transfers between devices  146 us (47%)
  starting transfers between devices  114 us (37%)
  matrix products  18.5 us (6%)
  local copies, waits for them, and re-layouts  17.5 us (6%)
  other arithmetic  12 us (4%)
    ppermute x18, waiting for transfers between devices, send_y(): lax.ppermute(value, 'y', [(i, (i + distance) % size) for i in range(size)])  58.4 us
    ppermute x18, starting transfers between devices, send_y(): lax.ppermute(value, 'y', [(i, (i + distance) % size) for i in range(size)])  52.5 us
    all_to_all x1, waiting for transfers between devices, on_device(): arrived = lax.all_to_all(partial_sums, CHIPS, 0, 0, tiled=True)  40 us
    ppermute x9, starting transfers between devices, swap(): return lax.ppermute(value, 'c', [(0, 1), (1, 0)])  25.3 us
    all_to_all x1, waiting for transfers between devices, on_device(): lax.all_to_all(result, CHIPS, 0, 0, tiled=True).reshape(slots, cols)  19.1 us
    all_to_all x1, waiting for transfers between devices, on_device(): tokens = lax.all_to_all(outgoing, CHIPS, 0, 0, tiled=True)  12.5 us
    all_to_all x1, waiting for transfers between devices, on_device(): context = lax.all_to_all(context, CHIPS, 0, 0, tiled=True)  12.1 us
    all_to_all x1, starting transfers between devices, on_device(): context = lax.all_to_all(context, CHIPS, 0, 0, tiled=True)  11.9 us
  transfers between devices with their start and end apart: 31, of which 16 were waited for; matrix products, arithmetic and copies ran while one was open for 10% of the time, Pallas kernels for 0%

profile of v1, /device:TPU:1, one launch (start us, length us, event | category | flops | bytes accessed | tf_op | source)
XLA Modules:
  0.0 308.6 jit_solution(17597881427562965982)
XLA Ops:
  6.0 11.9 %all-to-all-start = ((bf16[32,4,4,512]{3,1,2,0:T(4,128)(2,1)}), bf16[32,4,4,512]{3,1,2,0:T(4,128)(2,1)S(1)}, u32[]{:S(2)}, u32[]{:S(2)}) async-start(bf16[32,4,4,512]{3,1,2,0:T(4,128)(2,1)} %bitcast.133), calls=%async_computation | async-start | bytes 1048576 | tf_op jit(solution)/shard_map/all_to_all | solution.py:102
  20.1 12.1 %all-to-all-done = bf16[32,4,4,512]{3,1,2,0:T(4,128)(2,1)S(1)} async-done(((bf16[32,4,4,512]{3,1,2,0:T(4,128)(2,1)}), bf16[32,4,4,512]{3,1,2,0:T(4,128)(2,1)S(1)}, u32[]{:S(2)}, u32[]{:S(2)}) %all-to-all-start) | async-done | bytes 524320 | tf_op jit(solution)/shard_map/all_to_all | solution.py:102
  33.3 2.7 collective-permute-start.4
  36.0 2.8 dynamic-slice_bitcast_fusion
  38.9 2.7 collective-permute-start.7
  42.9 4.6 %collective-permute-start.8 = (bf16[256,896]{1,0:T(8,128)(2,1)}, bf16[256,896]{1,0:T(8,128)(2,1)}, u32[]{:S(2)}, u32[]{:S(2)}) collective-permute-start(bf16[256,896]{1,0:T(8,128)(2,1)} %constant_dynamic-slice_fusion.10), channel_id=1, source_target_pairs={{0,4},{4,0},{1,5},{5,1},{2,6},{6,2},{3,7},{7,3},{8,12},{12,8},{9,1... | collective-permute-start | bytes 1376264 | tf_op jit(solution)/shard_map/ppermute | solution.py:15
  47.7 12.1 %collective-permute-done.3 = bf16[32,4,512]{2,0,1:T(8,128)(2,1)S(1)} collective-permute-done((bf16[32,4,512]{2,0,1:T(8,128)(2,1)}, bf16[32,4,512]{2,0,1:T(8,128)(2,1)S(1)}, u32[]{:S(2)}, u32[]{:S(2)}) %collective-permute-start.3) | collective-permute-done | bytes 131104 | tf_op jit(solution)/shard_map/ppermute | solution.py:20
  59.8 2.7 collective-permute-done.2
  62.6 1.9 fusion.61
  64.5 6.2 %collective-permute-start.5 = (bf16[32,4,4,512]{3,0,2,1:T(8,128)(2,1)}, bf16[32,4,4,512]{3,0,2,1:T(8,128)(2,1)}, u32[]{:S(2)}, u32[]{:S(2)}) collective-permute-start(bf16[32,4,4,512]{3,0,2,1:T(8,128)(2,1)} %get-tuple-element.34), channel_id=1, source_target_pairs={{0,4},{4,0},{1,5},{5,1},{2,6},{6,2},{3,7},{7,3},{8,12},{12,8},{9,1... | collective-permute-start | bytes 1572872 | tf_op jit(solution)/shard_map/ppermute | solution.py:15
  70.7 2.1 broadcast_select_fusion.1
  77.0 3.5 %convolution_convert_fusion = bf16[1024,896]{1,0:T(8,128)(2,1)} fusion(bf16[1024,512]{1,0:T(8,128)(2,1)S(1)} %reshape.256, bf16[256,896]{1,0:T(8,128)(2,1)} %get-tuple-element.32, bf16[256,896]{1,0:T(8,128)(2,1)S(1)} %copy-done.11), kind=kOutput, calls=%fused_computation.15 | convolution fusion | flops 942276608 | bytes 3801088 | tf_op jit(solution)/shard_map/dot_general | solution.py:118
  80.5 7.7 %all-to-all-start.1 = ((bf16[32,32,896]{2,1,0:T(8,128)(2,1)}), bf16[32,32,896]{2,1,0:T(8,128)(2,1)S(1)}, u32[]{:S(2)}, u32[]{:S(2)}) async-start(bf16[32,32,896]{2,1,0:T(8,128)(2,1)} %bitcast.140), calls=%async_computation.1 | async-start | bytes 3670016 | tf_op jit(solution)/shard_map/all_to_all | solution.py:122
  91.7 40.0 %all-to-all-done.1 = bf16[32,32,896]{2,1,0:T(8,128)(2,1)S(1)} async-done(((bf16[32,32,896]{2,1,0:T(8,128)(2,1)}), bf16[32,32,896]{2,1,0:T(8,128)(2,1)S(1)}, u32[]{:S(2)}, u32[]{:S(2)}) %all-to-all-start.1) | async-done | bytes 1835040 | tf_op jit(solution)/shard_map/all_to_all | solution.py:122
  134.7 7.4 %all-to-all-start.2 = ((bf16[32,16,896]{2,1,0:T(8,128)(2,1)}), bf16[32,16,896]{2,1,0:T(8,128)(2,1)S(1)}, u32[]{:S(2)}, u32[]{:S(2)}) async-start(bf16[32,16,896]{2,1,0:T(8,128)(2,1)} %bitcast.38), calls=%async_computation.2 | async-start | bytes 1835008 | tf_op jit(solution)/shard_map/all_to_all | solution.py:149
  142.1 4.9 %constant_dynamic-slice_fusion.5 = (bf16[1792,256]{1,0:T(8,128)(2,1)S(1)}, bf16[1792,256]{1,0:T(8,128)(2,1)S(1)}, bf16[1792,256]{1,0:T(8,128)(2,1)S(1)}, bf16[17...) fusion(bf16[7168,256]{1,0:T(8,128)(2,1)} %bitcast.138, ...), kind=kLoop, calls=%fused_computation.100 | loop fusion | bytes 14680080 | tf_op jit(solution)/shard_map/dynamic_slice | solution.py:163
  151.5 12.5 %all-to-all-done.2 = bf16[32,16,896]{2,1,0:T(8,128)(2,1)S(1)} async-done(((bf16[32,16,896]{2,1,0:T(8,128)(2,1)}), bf16[32,16,896]{2,1,0:T(8,128)(2,1)S(1)}, u32[]{:S(2)}, u32[]{:S(2)}) %all-to-all-start.2) | async-done | bytes 917536 | tf_op jit(solution)/shard_map/all_to_all | solution.py:149
  164.1 5.1 %collective-permute-start.12 = (bf16[32,8,896]{2,1,0:T(8,128)(2,1)S(1)}, bf16[32,8,896]{2,1,0:T(8,128)(2,1)}, u32[]{:S(2)}, u32[]{:S(2)}) collective-permute-start(bf16[32,8,896]{2,1,0:T(8,128)(2,1)S(1)} %dynamic-slice_bitcast_fusion.2), channel_id=1, source_target_pairs={{0,4},{4,0},{1,5},{5,1},{2,6},{6,2},{3,7},{7,3},{8,12},{12,8},{9,1... | collective-permute-start | bytes 1376264 | tf_op jit(solution)/shard_map/ppermute | solution.py:15
  172.8 16.6 %collective-permute-done.17 = bf16[1792,512]{1,0:T(8,128)(2,1)} collective-permute-done((bf16[1792,512]{1,0:T(8,128)(2,1)}, bf16[1792,512]{1,0:T(8,128)(2,1)}, u32[]{:S(2)}, u32[]{:S(2)}) %collective-permute-start.17) | collective-permute-done | bytes 1835040 | tf_op jit(solution)/shard_map/ppermute | solution.py:20
  189.4 2.1 convolution_convert_fusion.2
  192.4 35.6 %collective-permute-start.18 = (bf16[256,512]{1,0:T(8,128)(2,1)S(1)}, bf16[256,512]{1,0:T(8,128)(2,1)S(1)}, u32[]{:S(2)}, u32[]{:S(2)}) collective-permute-start(bf16[256,512]{1,0:T(8,128)(2,1)S(1)} %convolution_convert_fusion.2), channel_id=1, source_target_pairs={{0,1},{1,2},{2,3},{3,0},{4,5},{5,6},{6,7},{7,4},{8,9},{9,10},{10,1... | collective-permute-start | bytes 786440 | tf_op jit(solution)/shard_map/ppermute | solution.py:20
  228.0 2.1 convolution_convert_fusion.3
  230.2 2.8 collective-permute-done.13
  234.6 2.1 convolution_convert_fusion.4
  238.6 4.2 %collective-permute-done.16 = bf16[256,512]{1,0:T(8,128)(2,1)S(1)} collective-permute-done((bf16[256,512]{1,0:T(8,128)(2,1)S(1)}, bf16[256,512]{1,0:T(8,128)(2,1)S(1)}, u32[]{:S(2)}, u32[]{:S(2)}) %collective-permute-start.16) | collective-permute-done | bytes 262176 | tf_op jit(solution)/shard_map/ppermute | solution.py:20
  242.8 2.5 collective-permute-done.14
  246.1 4.0 %collective-permute-start.25 = (bf16[256,256]{1,0:T(8,128)(2,1)S(1)}, bf16[256,256]{1,0:T(8,128)(2,1)S(1)}, u32[]{:S(2)}, u32[]{:S(2)}) collective-permute-start(bf16[256,256]{1,0:T(8,128)(2,1)S(1)} %fusion.37), channel_id=1, source_target_pairs={{0,3},{1,0},{2,1},{3,2},{4,7},{5,4},{6,5},{7,6},{8,11},{9,8},{10,9... | collective-permute-start | bytes 393224 | tf_op jit(solution)/shard_map/ppermute | solution.py:20
  251.9 16.7 %collective-permute-done.22 = bf16[256,256]{1,0:T(8,128)(2,1)S(1)} collective-permute-done((bf16[256,256]{1,0:T(8,128)(2,1)S(1)}, bf16[256,256]{1,0:T(8,128)(2,1)S(1)}, u32[]{:S(2)}, u32[]{:S(2)}) %collective-permute-start.22) | collective-permute-done | bytes 131104 | tf_op jit(solution)/shard_map/ppermute | solution.py:20
  270.8 9.0 %all-to-all-start.3 = ((bf16[32,8,1792]{2,1,0:T(8,128)(2,1)}), bf16[32,8,1792]{2,1,0:T(8,128)(2,1)S(1)}, u32[]{:S(2)}, u32[]{:S(2)}) async-start(bf16[32,8,1792]{2,1,0:T(8,128)(2,1)} %fusion.2), calls=%async_computation.3 | async-start | bytes 1835008 | tf_op jit(solution)/shard_map/all_to_all | solution.py:192
  280.2 2.1 collective-permute-start.9
  282.2 19.1 %all-to-all-done.3 = bf16[32,8,1792]{2,1,0:T(8,128)(2,1)S(1)} async-done(((bf16[32,8,1792]{2,1,0:T(8,128)(2,1)}), bf16[32,8,1792]{2,1,0:T(8,128)(2,1)S(1)}, u32[]{:S(2)}, u32[]{:S(2)}) %all-to-all-start.3) | async-done | bytes 917536 | tf_op jit(solution)/shard_map/all_to_all | solution.py:192
  301.6 5.3 %collective-permute-start.26 = (f32[16,1792]{1,0:T(8,128)S(1)}, f32[16,1792]{1,0:T(8,128)S(1)}, u32[]{:S(2)}, u32[]{:S(2)}) collective-permute-start(f32[16,1792]{1,0:T(8,128)S(1)} %dynamic-slice_bitcast_fusion.3), channel_id=1, source_target_pairs={{0,4},{4,0},{1,5},{5,1},{2,6},{6,2},{3,7},{7,3},{8,12},{12,8},{9,1... | collective-permute-start | bytes 344072 | tf_op jit(solution)/shard_map/ppermute | solution.py:15
  (166 shorter events, 40.8 us)
Async XLA Ops:
  6.0 26.2 %all-to-all-start = ((bf16[32,4,4,512]{3,1,2,0:T(4,128)(2,1)}), bf16[32,4,4,512]{3,1,2,0:T(4,128)(2,1)S(1)}, u32[]{:S(2)}, u32[]{:S(2)}) async-start(bf16[32,4,4,512]{3,1,2,0:T(4,128)(2,1)} %bitcast.133), calls=%async_computation | async-start | bytes 1048576 | tf_op jit(solution)/shard_map/all_to_all | solution.py:102
  17.9 2.2 collective-permute-start.1
  33.3 9.6 %collective-permute-start.4 = (bf16[32,4,512]{2,0,1:T(8,128)(2,1)}, bf16[32,4,512]{2,0,1:T(8,128)(2,1)S(1)}, u32[]{:S(2)}, u32[]{:S(2)}) collective-permute-start(bf16[32,4,512]{2,0,1:T(8,128)(2,1)} %copy_bitcast_fusion.1), channel_id=1, source_target_pairs={{0,3},{1,0},{2,1},{3,2},{4,7},{5,4},{6,5},{7,6},{8,11},{9,8},{10,9... | collective-permute-start | bytes 393224 | tf_op jit(solution)/shard_map/ppermute | solution.py:20
  38.9 35.1 %collective-permute-start.6 = (bf16[256,1792]{1,0:T(8,128)(2,1)}, bf16[256,1792]{1,0:T(8,128)(2,1)S(1)}, u32[]{:S(2)}, u32[]{:S(2)}) collective-permute-start(bf16[256,1792]{1,0:T(8,128)(2,1)} %get-tuple-element.28), channel_id=1, source_target_pairs={{0,1},{1,2},{2,3},{3,0},{4,5},{5,6},{6,7},{7,4},{8,9},{9,10},{10,1... | collective-permute-start | bytes 2752520 | tf_op jit(solution)/shard_map/ppermute | solution.py:20
  38.9 36.1 %collective-permute-start.7 = (bf16[256,1792]{1,0:T(8,128)(2,1)}, bf16[256,1792]{1,0:T(8,128)(2,1)S(1)}, u32[]{:S(2)}, u32[]{:S(2)}) collective-permute-start(bf16[256,1792]{1,0:T(8,128)(2,1)} %get-tuple-element.27), channel_id=1, source_target_pairs={{0,3},{1,0},{2,1},{3,2},{4,7},{5,4},{6,5},{7,6},{8,11},{9,8},{10,9... | collective-permute-start | bytes 2752520 | tf_op jit(solution)/shard_map/ppermute | solution.py:20
  41.5 18.3 %collective-permute-start.3 = (bf16[32,4,512]{2,0,1:T(8,128)(2,1)}, bf16[32,4,512]{2,0,1:T(8,128)(2,1)S(1)}, u32[]{:S(2)}, u32[]{:S(2)}) collective-permute-start(bf16[32,4,512]{2,0,1:T(8,128)(2,1)} %copy_bitcast_fusion.1), channel_id=1, source_target_pairs={{0,2},{1,3},{2,0},{3,1},{4,6},{5,7},{6,4},{7,5},{8,10},{9,11},{10,... | collective-permute-start | bytes 393224 | tf_op jit(solution)/shard_map/ppermute | solution.py:20
  41.5 21.0 %collective-permute-start.2 = (bf16[32,4,512]{2,0,1:T(8,128)(2,1)}, bf16[32,4,512]{2,0,1:T(8,128)(2,1)}, u32[]{:S(2)}, u32[]{:S(2)}) collective-permute-start(bf16[32,4,512]{2,0,1:T(8,128)(2,1)} %copy_bitcast_fusion.1), channel_id=1, source_target_pairs={{0,1},{1,2},{2,3},{3,0},{4,5},{5,6},{6,7},{7,4},{8,9},{9,10},{10,1... | collective-permute-start | bytes 393224 | tf_op jit(solution)/shard_map/ppermute | solution.py:20
  42.9 27.8 %collective-permute-start.8 = (bf16[256,896]{1,0:T(8,128)(2,1)}, bf16[256,896]{1,0:T(8,128)(2,1)}, u32[]{:S(2)}, u32[]{:S(2)}) collective-permute-start(bf16[256,896]{1,0:T(8,128)(2,1)} %constant_dynamic-slice_fusion.10), channel_id=1, source_target_pairs={{0,4},{4,0},{1,5},{5,1},{2,6},{6,2},{3,7},{7,3},{8,12},{12,8},{9,1... | collective-permute-start | bytes 1376264 | tf_op jit(solution)/shard_map/ppermute | solution.py:15
  64.5 8.4 %collective-permute-start.5 = (bf16[32,4,4,512]{3,0,2,1:T(8,128)(2,1)}, bf16[32,4,4,512]{3,0,2,1:T(8,128)(2,1)}, u32[]{:S(2)}, u32[]{:S(2)}) collective-permute-start(bf16[32,4,4,512]{3,0,2,1:T(8,128)(2,1)} %get-tuple-element.34), channel_id=1, source_target_pairs={{0,4},{4,0},{1,5},{5,1},{2,6},{6,2},{3,7},{7,3},{8,12},{12,8},{9,1... | collective-permute-start | bytes 1572872 | tf_op jit(solution)/shard_map/ppermute | solution.py:15
  80.5 51.3 %all-to-all-start.1 = ((bf16[32,32,896]{2,1,0:T(8,128)(2,1)}), bf16[32,32,896]{2,1,0:T(8,128)(2,1)S(1)}, u32[]{:S(2)}, u32[]{:S(2)}) async-start(bf16[32,32,896]{2,1,0:T(8,128)(2,1)} %bitcast.140), calls=%async_computation.1 | async-start | bytes 3670016 | tf_op jit(solution)/shard_map/all_to_all | solution.py:122
  88.2 3.5 %collective-permute-start = (bf16[16,896]{1,0:T(8,128)(2,1)S(1)}, bf16[16,896]{1,0:T(8,128)(2,1)S(1)}, u32[]{:S(2)}, u32[]{:S(2)}) collective-permute-start(bf16[16,896]{1,0:T(8,128)(2,1)S(1)} %constant_dynamic-slice_fusion.11), channel_id=1, source_target_pairs={{0,4},{4,0},{1,5},{5,1},{2,6},{6,2},{3,7},{7,3},{8,12},{12,8},{9,1... | collective-permute-start | bytes 86024 | tf_op jit(solution)/shard_map/ppermute | solution.py:15
  88.7 1.2 collective-permute-start.11
  89.0 1.2 collective-permute-start.10
  134.7 29.3 %all-to-all-start.2 = ((bf16[32,16,896]{2,1,0:T(8,128)(2,1)}), bf16[32,16,896]{2,1,0:T(8,128)(2,1)S(1)}, u32[]{:S(2)}, u32[]{:S(2)}) async-start(bf16[32,16,896]{2,1,0:T(8,128)(2,1)} %bitcast.38), calls=%async_computation.2 | async-start | bytes 1835008 | tf_op jit(solution)/shard_map/all_to_all | solution.py:149
  148.4 41.0 %collective-permute-start.17 = (bf16[1792,512]{1,0:T(8,128)(2,1)}, bf16[1792,512]{1,0:T(8,128)(2,1)}, u32[]{:S(2)}, u32[]{:S(2)}) collective-permute-start(bf16[1792,512]{1,0:T(8,128)(2,1)} %pad_maximum_fusion.2), channel_id=1, source_target_pairs={{0,3},{1,0},{2,1},{3,2},{4,7},{5,4},{6,5},{7,6},{8,11},{9,8},{10,9... | collective-permute-start | bytes 5505032 | tf_op jit(solution)/shard_map/ppermute | solution.py:20
  149.8 42.5 %collective-permute-start.15 = (bf16[1792,512]{1,0:T(8,128)(2,1)}, bf16[1792,512]{1,0:T(8,128)(2,1)}, u32[]{:S(2)}, u32[]{:S(2)}) collective-permute-start(bf16[1792,512]{1,0:T(8,128)(2,1)} %pad_maximum_fusion.1), channel_id=1, source_target_pairs={{0,2},{1,3},{2,0},{3,1},{4,6},{5,7},{6,4},{7,5},{8,10},{9,11},{10,... | collective-permute-start | bytes 5505032 | tf_op jit(solution)/shard_map/ppermute | solution.py:20
  150.6 82.4 %collective-permute-start.13 = (bf16[1792,512]{1,0:T(8,128)(2,1)S(1)}, bf16[1792,512]{1,0:T(8,128)(2,1)}, u32[]{:S(2)}, u32[]{:S(2)}) collective-permute-start(bf16[1792,512]{1,0:T(8,128)(2,1)S(1)} %pad_maximum_fusion), channel_id=1, source_target_pairs={{0,1},{1,2},{2,3},{3,0},{4,5},{5,6},{6,7},{7,4},{8,9},{9,10},{10,1... | collective-permute-start | bytes 5505032 | tf_op jit(solution)/shard_map/ppermute | solution.py:20
  164.1 6.6 %collective-permute-start.12 = (bf16[32,8,896]{2,1,0:T(8,128)(2,1)S(1)}, bf16[32,8,896]{2,1,0:T(8,128)(2,1)}, u32[]{:S(2)}, u32[]{:S(2)}) collective-permute-start(bf16[32,8,896]{2,1,0:T(8,128)(2,1)S(1)} %dynamic-slice_bitcast_fusion.2), channel_id=1, source_target_pairs={{0,4},{4,0},{1,5},{5,1},{2,6},{6,2},{3,7},{7,3},{8,12},{12,8},{9,1... | collective-permute-start | bytes 1376264 | tf_op jit(solution)/shard_map/ppermute | solution.py:15
  172.2 64.5 %collective-permute-start.21 = (f32[256]{0:T(256)S(1)}, f32[256]{0:T(256)S(1)}, u32[]{:S(2)}, u32[]{:S(2)}) collective-permute-start(f32[256]{0:T(256)S(1)} %multiply_reduce_fusion), channel_id=1, source_target_pairs={{0,3},{1,0},{2,1},{3,2},{4,7},{5,4},{6,5},{7,6},{8,11},{9,8},{10,9... | collective-permute-start | bytes 3080 | tf_op jit(solution)/shard_map/ppermute | solution.py:20
  172.3 64.9 %collective-permute-start.20 = (f32[256]{0:T(256)S(1)}, f32[256]{0:T(256)S(1)}, u32[]{:S(2)}, u32[]{:S(2)}) collective-permute-start(f32[256]{0:T(256)S(1)} %multiply_reduce_fusion), channel_id=1, source_target_pairs={{0,2},{1,3},{2,0},{3,1},{4,6},{5,7},{6,4},{7,5},{8,10},{9,11},{10,... | collective-permute-start | bytes 3080 | tf_op jit(solution)/shard_map/ppermute | solution.py:20
  189.4 49.2 %collective-permute-start.19 = (f32[256]{0:T(256)S(1)}, f32[256]{0:T(256)S(1)}, u32[]{:S(2)}, u32[]{:S(2)}) collective-permute-start(f32[256]{0:T(256)S(1)} %multiply_reduce_fusion), channel_id=1, source_target_pairs={{0,1},{1,2},{2,3},{3,0},{4,5},{5,6},{6,7},{7,4},{8,9},{9,10},{10,1... | collective-permute-start | bytes 3080 | tf_op jit(solution)/shard_map/ppermute | solution.py:20
  192.4 46.2 %collective-permute-start.18 = (bf16[256,512]{1,0:T(8,128)(2,1)S(1)}, bf16[256,512]{1,0:T(8,128)(2,1)S(1)}, u32[]{:S(2)}, u32[]{:S(2)}) collective-permute-start(bf16[256,512]{1,0:T(8,128)(2,1)S(1)} %convolution_convert_fusion.2), channel_id=1, source_target_pairs={{0,1},{1,2},{2,3},{3,0},{4,5},{5,6},{6,7},{7,4},{8,9},{9,10},{10,1... | collective-permute-start | bytes 786440 | tf_op jit(solution)/shard_map/ppermute | solution.py:20
  232.9 9.9 %collective-permute-start.16 = (bf16[256,512]{1,0:T(8,128)(2,1)S(1)}, bf16[256,512]{1,0:T(8,128)(2,1)S(1)}, u32[]{:S(2)}, u32[]{:S(2)}) collective-permute-start(bf16[256,512]{1,0:T(8,128)(2,1)S(1)} %convolution_convert_fusion.3), channel_id=1, source_target_pairs={{0,2},{1,3},{2,0},{3,1},{4,6},{5,7},{6,4},{7,5},{8,10},{9,11},{10,... | collective-permute-start | bytes 786440 | tf_op jit(solution)/shard_map/ppermute | solution.py:20
  236.7 8.6 %collective-permute-start.14 = (bf16[256,512]{1,0:T(8,128)(2,1)S(1)}, bf16[256,512]{1,0:T(8,128)(2,1)S(1)}, u32[]{:S(2)}, u32[]{:S(2)}) collective-permute-start(bf16[256,512]{1,0:T(8,128)(2,1)S(1)} %convolution_convert_fusion.4), channel_id=1, source_target_pairs={{0,3},{1,0},{2,1},{3,2},{4,7},{5,4},{6,5},{7,6},{8,11},{9,8},{10,9... | collective-permute-start | bytes 786440 | tf_op jit(solution)/shard_map/ppermute | solution.py:20
  237.2 32.3 %collective-permute-start.24 = (bf16[256,1792]{1,0:T(8,128)(2,1)S(1)}, bf16[256,1792]{1,0:T(8,128)(2,1)S(1)}, u32[]{:S(2)}, u32[]{:S(2)}) collective-permute-start(bf16[256,1792]{1,0:T(8,128)(2,1)S(1)} %constant_dynamic-slice_fusion), channel_id=1, source_target_pairs={{0,2},{1,3},{2,0},{3,1},{4,6},{5,7},{6,4},{7,5},{8,10},{9,11},{10,... | collective-permute-start | bytes 2752520 | tf_op jit(solution)/shard_map/ppermute | solution.py:20
  246.1 22.9 %collective-permute-start.25 = (bf16[256,256]{1,0:T(8,128)(2,1)S(1)}, bf16[256,256]{1,0:T(8,128)(2,1)S(1)}, u32[]{:S(2)}, u32[]{:S(2)}) collective-permute-start(bf16[256,256]{1,0:T(8,128)(2,1)S(1)} %fusion.37), channel_id=1, source_target_pairs={{0,3},{1,0},{2,1},{3,2},{4,7},{5,4},{6,5},{7,6},{8,11},{9,8},{10,9... | collective-permute-start | bytes 393224 | tf_op jit(solution)/shard_map/ppermute | solution.py:20
  250.1 18.5 %collective-permute-start.22 = (bf16[256,256]{1,0:T(8,128)(2,1)S(1)}, bf16[256,256]{1,0:T(8,128)(2,1)S(1)}, u32[]{:S(2)}, u32[]{:S(2)}) collective-permute-start(bf16[256,256]{1,0:T(8,128)(2,1)S(1)} %fusion.37), channel_id=1, source_target_pairs={{0,1},{1,2},{2,3},{3,0},{4,5},{5,6},{6,7},{7,4},{8,9},{9,10},{10,1... | collective-permute-start | bytes 393224 | tf_op jit(solution)/shard_map/ppermute | solution.py:20
  250.5 18.9 %collective-permute-start.23 = (bf16[256,256]{1,0:T(8,128)(2,1)S(1)}, bf16[256,256]{1,0:T(8,128)(2,1)S(1)}, u32[]{:S(2)}, u32[]{:S(2)}) collective-permute-start(bf16[256,256]{1,0:T(8,128)(2,1)S(1)} %fusion.37), channel_id=1, source_target_pairs={{0,2},{1,3},{2,0},{3,1},{4,6},{5,7},{6,4},{7,5},{8,10},{9,11},{10,... | collective-permute-start | bytes 393224 | tf_op jit(solution)/shard_map/ppermute | solution.py:20
  270.8 30.5 %all-to-all-start.3 = ((bf16[32,8,1792]{2,1,0:T(8,128)(2,1)}), bf16[32,8,1792]{2,1,0:T(8,128)(2,1)S(1)}, u32[]{:S(2)}, u32[]{:S(2)}) async-start(bf16[32,8,1792]{2,1,0:T(8,128)(2,1)} %fusion.2), calls=%async_computation.3 | async-start | bytes 1835008 | tf_op jit(solution)/shard_map/all_to_all | solution.py:192
  279.8 28.8 %copy-start.1 = (bf16[2,2,128,576]{2,3,1,0:T(8,128)(2,1)S(1)}, bf16[2,2,128,576]{2,3,1,0:T(8,128)(2,1)}, u32[]{:S(2)}) copy-start(bf16[2,2,128,576]{2,3,1,0:T(8,128)(2,1)} %param.14) | copy-start | bytes 1769476
  280.2 26.8 %collective-permute-start.9 = (f32[16,896]{1,0:T(8,128)S(1)}, f32[16,896]{1,0:T(8,128)S(1)}, u32[]{:S(2)}, u32[]{:S(2)}) collective-permute-start(f32[16,896]{1,0:T(8,128)S(1)} %dynamic-slice_bitcast_fusion.4), channel_id=1, source_target_pairs={{0,4},{4,0},{1,5},{5,1},{2,6},{6,2},{3,7},{7,3},{8,12},{12,8},{9,1... | collective-permute-start | bytes 172040 | tf_op jit(solution)/shard_map/ppermute | solution.py:15
  301.6 6.3 %collective-permute-start.26 = (f32[16,1792]{1,0:T(8,128)S(1)}, f32[16,1792]{1,0:T(8,128)S(1)}, u32[]{:S(2)}, u32[]{:S(2)}) collective-permute-start(f32[16,1792]{1,0:T(8,128)S(1)} %dynamic-slice_bitcast_fusion.3), channel_id=1, source_target_pairs={{0,4},{4,0},{1,5},{5,1},{2,6},{6,2},{3,7},{7,3},{8,12},{12,8},{9,1... | collective-permute-start | bytes 344072 | tf_op jit(solution)/shard_map/ppermute | solution.py:15
  (19 other events, 153.2 us)

commit v2 on v1

--- a/solution.py
+++ b/solution.py
@@ -78,13 +78,43 @@
     rope = kv - lat
     cols = hidden.shape[2]
     half = cols // NC
+    units = w_gate.shape[2]
     width = cols * ny
     own_tokens = rows * steps
     group = own_tokens * ny
     heads_chip = heads_core * NC
+    slots = chips * NC * CAP
+    near = (1, ny - 1)
+    far = tuple(d for d in range(1, ny) if d not in near)
 
     def half_of(value, which):
         return lax.dynamic_slice_in_dim(value, which * half, half, value.ndim - 1)
+
+    def after(value, done):
+        return lax.optimization_barrier((value, done))[0]
+
+    def over_chips(value):
+        return lax.all_to_all(value, CHIPS, 0, 0, tiled=True)
+
+    def down_block(block):
+        return lax.dynamic_slice_in_dim(w_down[0], (block % ny) * cols, cols, 1)
+
+    def row_block(weight, block):
+        return lax.dynamic_slice_in_dim(weight[0], (block % ny) * cols, cols, 0)
+
+    def up_block(block):
+        return jnp.concatenate([row_block(w_gate, block), row_block(w_up, block)], axis=1)
+
+    def half_block(block, which):
+        start = (block % ny) * cols + which * half
+        return jnp.concatenate(
+            [lax.dynamic_slice_in_dim(weight[0], start, half, 0) for weight in (w_gate, w_up)],
+            axis=1,
+        )
+
+    down_parts = {d: send_y(down_block(y + d), d) for d in near}
+    near_up = {d: up_block(y + d) for d in near}
+    far_gain = {d: send_y(norm_gain, d) for d in far}
 
     vp = in_core_order(core, value_proj, swap(value_proj))
     op = in_core_order(core, half_of(out_proj, core), swap(half_of(out_proj, 1 - core)))
@@ -99,97 +129,92 @@
 
     context = attend(queries, latent_cache, new_latent, lengths, lat, (vdim + rope) ** (-0.5))
     context = context.reshape(own_tokens, chips, heads_chip, lat).transpose(1, 0, 2, 3)
-    context = lax.all_to_all(context, CHIPS, 0, 0, tiled=True)
+    context = over_chips(context)
+    context, down_parts, near_up, vp, op, far_gain = lax.optimization_barrier(
+        (context, down_parts, near_up, vp, op, far_gain)
+    )
     values = jnp.einsum("nthl,hlv->nthv", context, vp, preferred_element_type=F32).astype(BF16)
-    values = values.reshape(chips, own_tokens, heads_chip * vdim)
-
-    blocks = [values] + [send_y(values, d) for d in range(1, ny)]
-    mine = jnp.stack(blocks, axis=1)
-    both = jnp.stack([mine, swap(mine)], axis=1)
-
-    down_own = w_down[0]
-
-    def down_block(block):
-        return lax.dynamic_slice_in_dim(down_own, (block % ny) * cols, cols, 1)
-
-    near = (1, ny - 1)
-    early = [send_y(down_block(y + d), d) for d in near]
-    both, *early = lax.optimization_barrier((both, *early))
-    partial_sums = jnp.dot(
-        both.reshape(-1, heads_chip * vdim), op, preferred_element_type=F32
+
+    values = jnp.concatenate([values] + [send_y(values, d) for d in range(1, ny)], axis=1)
+    up_parts = {d: send_y(block, d) for d, block in after(near_up, values).items()}
+    values = values.reshape(chips, group, heads_chip * vdim)
+    values = jnp.concatenate([values, swap(values)], axis=1)
+    sums = jnp.dot(
+        values.reshape(-1, heads_chip * vdim), op, preferred_element_type=F32
     ).astype(BF16)
-    partial_sums = partial_sums.reshape(chips, NC * group, half)
-    arrived = lax.all_to_all(partial_sums, CHIPS, 0, 0, tiled=True)
-    attention = jnp.sum(arrived.astype(F32), axis=0).astype(BF16)
-    attention = attention.reshape(NC, ny, own_tokens, half)
-    core_order = (jnp.arange(NC) + core) % NC
+    sums = over_chips(sums.reshape(chips, NC * group, half))
+    sums = jnp.sum(sums.astype(F32), axis=0).astype(BF16).astype(F32)
+
+    core_order = (core + jnp.arange(NC)) % NC
     y_order = (y - jnp.arange(ny)) % ny
-    attention = attention[core_order][:, y_order].reshape(NC, group, half)
-    residual = chip_hidden.astype(F32) + attention.astype(F32)
+    token = jnp.arange(own_tokens)
+    place = core_order[:, None, None] * group + y_order[None, :, None] * own_tokens + token
+    place = place.reshape(-1)
+    placed_hidden = chip_hidden.reshape(NC * group, half)[place].astype(F32)
     gain = half_of(norm_gain, core)
-    scaled = (residual * gain).astype(BF16).reshape(NC * group, half)
-    other_half = swap(lax.dynamic_index_in_dim(residual, 1 - core, 0, keepdims=False))
-    own_half = lax.dynamic_index_in_dim(residual, core, 0, keepdims=False)
-    full_residual = in_core_order(core, own_half, other_half, axis=1)
 
     chip_slots = jnp.stack([slots_of(chip_ids[0]), slots_of(chip_ids[1])])
     group_of = jnp.arange(NC)[:, None, None]
     row_of = (chip_ids * NC + group_of) * CAP + chip_slots
     row_of = row_of.reshape(NC * group, -1)
-    row_count = chips * NC * NC * CAP
-    named = row_of[:, :, None] == jnp.arange(row_count)[None, None, :]
-    spread = jnp.sum(named.astype(F32), axis=1).astype(BF16)
-    combine = jnp.sum(named.astype(F32) * chip_gates.reshape(NC * group, -1)[:, :, None], axis=1)
-    combine = combine.astype(BF16).reshape(NC * group, chips, NC, NC * CAP)
+    row_ids = jnp.arange(chips * NC * NC * CAP)[None, None, :]
+    named = row_of[:, :, None] == row_ids
+    weighted = named.astype(F32) * chip_gates.reshape(NC * group, -1)[:, :, None]
+    combine = jnp.sum(weighted, axis=1).astype(BF16).reshape(NC * group, chips, NC, NC * CAP)
     combine = lax.dynamic_index_in_dim(combine, core, 2, keepdims=False)
+    spread = jnp.sum((row_of[place][:, :, None] == row_ids).astype(F32), axis=1).astype(BF16)
+
+    residual = placed_hidden + sums
+    scaled = (residual * gain).astype(BF16)
+    far_down = {d: send_y(after(down_block(y + d), up_parts), d) for d in far}
     outgoing = lax.dot_general(
         spread, scaled, (((0,), (0,)), ((), ())), preferred_element_type=F32
     ).astype(BF16)
-    outgoing = outgoing.reshape(chips, NC * NC * CAP, half)
-    tokens = lax.all_to_all(outgoing, CHIPS, 0, 0, tiled=True)
+    tokens = over_chips(outgoing.reshape(chips, NC * NC * CAP, half))
     tokens = tokens.reshape(chips, NC, NC * CAP, half)
-    kept = lax.dynamic_index_in_dim(tokens, core, 1, keepdims=False)
+    kept = lax.dynamic_index_in_dim(tokens, core, 1, keepdims=False).reshape(slots, half)
     received = swap(lax.dynamic_index_in_dim(tokens, 1 - core, 1, keepdims=False))
-    slots = chips * NC * CAP
-    tokens = in_core_order(core, kept.reshape(slots, half), received.reshape(slots, half), axis=1)
-
-    gate_w, up_w, down_own, _ = lax.optimization_barrier((w_gate[0], w_up[0], down_own, mine))
-
-    def up_block(block):
-        start = (block % ny) * cols
-        return jnp.concatenate(
-            [
-                lax.dynamic_slice_in_dim(gate_w, start, cols, 0),
-                lax.dynamic_slice_in_dim(up_w, start, cols, 0),
-            ],
-            axis=1,
-        )
-
-    up_parts = [up_block(y)] + [send_y(up_block(y + d), d) for d in range(1, ny)]
-    down_parts = {0: down_block(y), **dict(zip(near, early))}
-    for d in range(1, ny):
-        if d not in near:
-            down_parts[d] = send_y(down_block(y + d), d)
-
-    column_gain = norm_gain
-    shares = jnp.sum(jnp.square(tokens.astype(F32) / column_gain), axis=1)
-    squares = shares
-    for d in range(1, ny):
-        squares = squares + send_y(shares, d)
-    row_scale = lax.rsqrt(squares / width + EPS)[:, None]
-    sums = jnp.dot(tokens, up_parts[0], preferred_element_type=F32)
-    for d in range(1, ny):
-        part = jnp.dot(tokens, up_parts[d], preferred_element_type=F32).astype(BF16)
-        sums = sums + send_y(part, -d).astype(F32)
-    sums = sums * row_scale
-    units = sums.shape[1] // 2
+    received = received.reshape(slots, half)
+    kept, far_down = lax.optimization_barrier((kept, far_down))
+    far_tokens = {d: (send_y(kept, d), send_y(received, d)) for d in far}
+    down_parts.update(far_down)
+    down_parts[0] = down_block(y)
+    tokens = in_core_order(core, kept, received, axis=1)
+
+    residual = residual.reshape(NC, group, half)
+    full_residual = in_core_order(core, residual[0], swap(residual[1]), axis=1)
+    back = (y - jnp.arange(ny)) % ny
+    full_residual = full_residual.reshape(ny, own_tokens, cols)[back].reshape(group, cols)
+
+    def share(part, gains):
+        return jnp.sum(jnp.square(part.astype(F32) / gains), axis=1, keepdims=True)
+
+    own_share = share(tokens, norm_gain)
+    coarse = lax.reduce_precision(own_share, 8, 7)
+    lanes = jnp.arange(128)[None, :]
+    share_lanes = jnp.where(lanes == 0, coarse, jnp.where(lanes == 1, own_share - coarse, 0.0))
+    squares = own_share
+    sums = jnp.dot(tokens, up_block(y), preferred_element_type=F32)
+    for d in near:
+        part = jnp.dot(tokens, up_parts[d], preferred_element_type=F32)
+        part = jnp.concatenate([part.astype(BF16), share_lanes.astype(BF16)], axis=1)
+        part = send_y(part, -d).astype(F32)
+        sums = sums + part[:, : 2 * units]
+        squares = squares + part[:, 2 * units : 2 * units + 1]
+        squares = squares + part[:, 2 * units + 1 : 2 * units + 2]
+    for d in far:
+        for part, which in zip(far_tokens[d], (core, 1 - core)):
+            sums = sums + jnp.dot(part, half_block(y - d, which), preferred_element_type=F32)
+            squares = squares + share(part, half_of(far_gain[d], which))
+    sums = sums * lax.rsqrt(squares / width + EPS)
     act = (jax.nn.silu(sums[:, :units]) * sums[:, units:]).astype(BF16)
-    result = jnp.dot(act, down_parts[0], preferred_element_type=F32)
-    for d in range(1, ny):
-        result = result + jnp.dot(send_y(act, d), down_parts[d], preferred_element_type=F32)
+    acts = {0: act, **{d: send_y(act, d) for d in near + far}}
+    result = sum(
+        jnp.dot(acts[d], down_parts[d], preferred_element_type=F32) for d in (0,) + near + far
+    )
     result = result.astype(BF16).reshape(chips, NC * CAP, cols)
 
-    returned = lax.all_to_all(result, CHIPS, 0, 0, tiled=True).reshape(slots, cols)
+    returned = over_chips(result).reshape(slots, cols)
     mixture = jnp.dot(
         combine.reshape(NC * group, slots), returned, preferred_element_type=F32
     ).reshape(NC, group, cols)

time: 310 us -> 225 us (0.73)
  starting transfers between devices: 114 us -> 71.7 us
  waiting for transfers between devices: 146 us -> 108 us
  other arithmetic: 12 us -> 8.35 us
    ppermute x18 -> x16, waiting for transfers between devices: 58.4 us -> 26.8 us  [send_y(): lax.ppermute(value, 'y', [(i, (i + distance) % size) for i in range(size)])]
    ppermute x18 -> x16, starting transfers between devices: 52.5 us -> 23.1 us  [send_y(): lax.ppermute(value, 'y', [(i, (i + distance) % size) for i in range(size)])]
    all_to_all x4, starting transfers between devices: 35.8 us -> 28 us  [over_chips(): return lax.all_to_all(value, CHIPS, 0, 0, tiled=True)]
    all_to_all x4, waiting for transfers between devices: 83.7 us -> 77.1 us  [over_chips(): return lax.all_to_all(value, CHIPS, 0, 0, tiled=True)]
    ppermute x9, starting transfers between devices: 25.3 us -> 20.6 us  [swap(): return lax.ppermute(value, 'c', [(0, 1), (1, 0)])]
    dot_general x9 -> x10, matrix products: 13.2 us -> 15.5 us  [the longest x4 6.27 us: on_device(): jnp.dot(acts[d], down_parts[d], preferred_element_type=F32)]
  transfers between devices with their start and end apart: 31 -> 29, of which waited for: 16 -> 16; matrix products, arithmetic and copies ran while one was open for 10% -> 14% of each run, Pallas kernels for 0% -> 0%
where the time goes in v2:
time: 225 us; the launch traced here: 224 us
  waiting for transfers between devices  108 us (48%)
  starting transfers between devices  71.7 us (32%)
  matrix products  19.1 us (8%)
  local copies, waits for them, and re-layouts  16.7 us (7%)
  other arithmetic  8.35 us (4%)
    all_to_all x4, waiting for transfers between devices, over_chips(): return lax.all_to_all(value, CHIPS, 0, 0, tiled=True)  77.1 us
    all_to_all x4, starting transfers between devices, over_chips(): return lax.all_to_all(value, CHIPS, 0, 0, tiled=True)  28 us
    ppermute x16, waiting for transfers between devices, send_y(): lax.ppermute(value, 'y', [(i, (i + distance) % size) for i in range(size)])  26.8 us
    ppermute x16, starting transfers between devices, send_y(): lax.ppermute(value, 'y', [(i, (i + distance) % size) for i in range(size)])  23.1 us
    ppermute x9, starting transfers between devices, swap(): return lax.ppermute(value, 'c', [(0, 1), (1, 0)])  20.6 us
    dot_general x4, matrix products, on_device(): jnp.dot(acts[d], down_parts[d], preferred_element_type=F32)  6.27 us
    dot_general x2, matrix products, on_device(): part = jnp.dot(tokens, up_parts[d], preferred_element_type=F32)  4.72 us
  transfers between devices with their start and end apart: 29, of which 16 were waited for; matrix products, arithmetic and copies ran while one was open for 14% of the time, Pallas kernels for 0%

profile of v2, /device:TPU:1, one launch (start us, length us, event | category | flops | bytes accessed | tf_op | source)
XLA Modules:
  0.0 224.4 jit_solution(9654375426550088758)
XLA Ops:
  0.0 3.5 %dynamic-slice_bitcast_fusion.2 = (bf16[256,1792]{1,0:T(8,128)(2,1)}, bf16[256,1792]{1,0:T(8,128)(2,1)}, bf16[256,1792]{1,0:T(8,128)(2,1)}) fusion(bf16[1,256,7168]{2,1,0:T(8,128)(2,1)} %param.23, s32[]{:T(128)S(6)} %select_n.285, s32[]{:T(128)S(6)} %select_n.263, s32[]{:T(128)S(6)} %select_n.261), kind=kLoop, calls=%fused_computation.52 | loop fusion | bytes 5505036 | tf_op jit(solution)/shard_map/dynamic_slice | solution.py:100
  3.5 2.1 collective-permute-start.1
  7.9 2.9 %collective-permute-start.4 = (bf16[256,896]{1,0:T(8,128)(2,1)}, bf16[256,896]{1,0:T(8,128)(2,1)}, u32[]{:S(2)}, u32[]{:S(2)}) collective-permute-start(bf16[256,896]{1,0:T(8,128)(2,1)} %constant_dynamic-slice_fusion.1), channel_id=1, source_target_pairs={{0,4},{4,0},{1,5},{5,1},{2,6},{6,2},{3,7},{7,3},{8,12},{12,8},{9,1... | collective-permute-start | bytes 1376264 | tf_op jit(solution)/shard_map/ppermute | solution.py:15
  14.0 9.3 %all-to-all-start = ((bf16[32,4,4,512]{3,1,2,0:T(4,128)(2,1)}), bf16[32,4,4,512]{3,1,2,0:T(4,128)(2,1)S(1)}, u32[]{:S(2)}, u32[]{:S(2)}) async-start(bf16[32,4,4,512]{3,1,2,0:T(4,128)(2,1)} %bitcast.142), calls=%async_computation | async-start | bytes 1048576 | tf_op jit(solution)/shard_map/all_to_all | solution.py:97
  23.7 1.7 collective-permute-start.5
  25.4 3.9 %dynamic-slice_bitcast_fusion = (bf16[1792,256]{1,0:T(8,128)(2,1)S(1)}, bf16[1792,256]{1,0:T(8,128)(2,1)S(1)}, bf16[1792,256]{1,0:T(8,128)(2,1)S(1)}, bf16[1792,...) fusion(bf16[1,7168,256]{2,1,0:T(8,128)(2,1)} %param.22, s32[]{:T(128)S(6)} %select_n.290, ...), kind=kLoop, calls=%fused_computation.50 | loop fusion | bytes 11010060 | tf_op jit(solution)/shard_map/dynamic_slice | solution.py:103
  34.5 3.7 %all-to-all-done = bf16[32,4,4,512]{3,1,2,0:T(4,128)(2,1)S(1)} async-done(((bf16[32,4,4,512]{3,1,2,0:T(4,128)(2,1)}), bf16[32,4,4,512]{3,1,2,0:T(4,128)(2,1)S(1)}, u32[]{:S(2)}, u32[]{:S(2)}) %all-to-all-start) | async-done | bytes 524320 | tf_op jit(solution)/shard_map/all_to_all | solution.py:97
  38.8 2.6 %collective-permute-start.7 = (bf16[32,4,4,128]{3,0,1,2:T(8,128)(2,1)S(1)}, bf16[32,4,4,128]{3,0,1,2:T(8,128)(2,1)S(1)}, u32[]{:S(2)}, u32[]{:S(2)}) collective-permute-start(bf16[32,4,4,128]{3,0,1,2:T(8,128)(2,1)S(1)} %fusion.24), channel_id=1, source_target_pairs={{0,2},{1,3},{2,0},{3,1},{4,6},{5,7},{6,4},{7,5},{8,10},{9,11},{10,... | collective-permute-start | bytes 393224 | tf_op jit(solution)/shard_map/ppermute | solution.py:20
  46.8 4.1 %collective-permute-start.9 = (bf16[32,16,512]{2,1,0:T(8,128)(2,1)S(1)}, bf16[32,16,512]{2,1,0:T(8,128)(2,1)S(1)}, u32[]{:S(2)}, u32[]{:S(2)}) collective-permute-start(bf16[32,16,512]{2,1,0:T(8,128)(2,1)S(1)} %reshape.340), channel_id=1, source_target_pairs={{0,4},{4,0},{1,5},{5,1},{2,6},{6,2},{3,7},{7,3},{8,12},{12,8},{9,1... | collective-permute-start | bytes 1572872 | tf_op jit(solution)/shard_map/ppermute | solution.py:15
  52.5 2.6 %convolution_convert_fusion = bf16[1024,896]{1,0:T(8,128)(2,1)} fusion(bf16[1024,512]{1,0:T(8,128)(2,1)S(1)} %bitcast.146, bf16[512,896]{1,0:T(8,128)(2,1)S(1)} %copy-done.6), kind=kOutput, calls=%fused_computation.15 | convolution fusion | flops 940441600 | bytes 3801088 | tf_op jit(solution)/shard_map/dot_general | solution.py:142
  55.0 6.7 %all-to-all-start.1 = ((bf16[32,32,896]{2,1,0:T(8,128)(2,1)}), bf16[32,32,896]{2,1,0:T(8,128)(2,1)S(1)}, u32[]{:S(2)}, u32[]{:S(2)}) async-start(bf16[32,32,896]{2,1,0:T(8,128)(2,1)} %bitcast.145), calls=%async_computation.1 | async-start | bytes 3670016 | tf_op jit(solution)/shard_map/all_to_all | solution.py:97
  66.8 1.6 collective-permute-start.14
  69.1 35.7 %all-to-all-done.1 = bf16[32,32,896]{2,1,0:T(8,128)(2,1)S(1)} async-done(((bf16[32,32,896]{2,1,0:T(8,128)(2,1)}), bf16[32,32,896]{2,1,0:T(8,128)(2,1)S(1)}, u32[]{:S(2)}, u32[]{:S(2)}) %all-to-all-start.1) | async-done | bytes 1835040 | tf_op jit(solution)/shard_map/all_to_all | solution.py:97
  106.5 7.4 %all-to-all-start.2 = ((bf16[32,16,896]{2,1,0:T(8,128)(2,1)}), bf16[32,16,896]{2,1,0:T(8,128)(2,1)S(1)}, u32[]{:S(2)}, u32[]{:S(2)}) async-start(bf16[32,16,896]{2,1,0:T(8,128)(2,1)} %bitcast.35), calls=%async_computation.2 | async-start | bytes 1835008 | tf_op jit(solution)/shard_map/all_to_all | solution.py:97
  113.9 1.8 collective-permute-start.15
  115.7 20.1 %all-to-all-done.2 = bf16[32,16,896]{2,1,0:T(8,128)(2,1)S(1)} async-done(((bf16[32,16,896]{2,1,0:T(8,128)(2,1)}), bf16[32,16,896]{2,1,0:T(8,128)(2,1)S(1)}, u32[]{:S(2)}, u32[]{:S(2)}) %all-to-all-start.2) | async-done | bytes 917536 | tf_op jit(solution)/shard_map/all_to_all | solution.py:97
  136.6 5.3 %collective-permute-start.16 = (bf16[32,8,896]{2,1,0:T(8,128)(2,1)}, bf16[32,8,896]{2,1,0:T(8,128)(2,1)S(1)}, u32[]{:S(2)}, u32[]{:S(2)}) collective-permute-start(bf16[32,8,896]{2,1,0:T(8,128)(2,1)} %get-tuple-element.49), channel_id=1, source_target_pairs={{0,4},{4,0},{1,5},{5,1},{2,6},{6,2},{3,7},{7,3},{8,12},{12,8},{9,1... | collective-permute-start | bytes 1376264 | tf_op jit(solution)/shard_map/ppermute | solution.py:15
  141.9 1.6 dynamic-slice_bitcast_fusion.11
  143.5 1.7 collective-permute-start.19
  146.9 2.4 %convolution_convert_fusion.2 = bf16[256,512]{0,1:T(8,128)(2,1)S(1)} fusion(bf16[1792,512]{1,0:T(8,128)(2,1)} %collective-permute-done.14, bf16[256,896]{1,0:T(8,128)(2,1)S(1)} %get-tuple-element.47, bf16[256,896]{1,0:T(8,128)(2,1)S(1)} %get-tuple-element.46), kind=kOutput, calls=%fused_computation.26 | convolution fusion | flops 471728128 | bytes 3014656 | tf_op jit(solution)/shard_map/dot_general | solution.py:199
  149.4 2.4 %convolution_convert_fusion.3 = bf16[256,512]{0,1:T(8,128)(2,1)S(1)} fusion(bf16[1792,512]{1,0:T(8,128)(2,1)} %collective-permute-done.13, bf16[256,896]{1,0:T(8,128)(2,1)S(1)} %get-tuple-element.47, bf16[256,896]{1,0:T(8,128)(2,1)S(1)} %get-tuple-element.46), kind=kOutput, calls=%fused_computation.27 | convolution fusion | flops 471728128 | bytes 3014656 | tf_op jit(solution)/shard_map/dot_general | solution.py:199
  151.8 2.5 %collective-permute-start.17 = (bf16[256,640]{0,1:T(8,128)(2,1)S(1)}, bf16[256,640]{0,1:T(8,128)(2,1)S(1)}, u32[]{:S(2)}, u32[]{:S(2)}) collective-permute-start(bf16[256,640]{0,1:T(8,128)(2,1)S(1)} %get-tuple-element.56), channel_id=1, source_target_pairs={{0,3},{1,0},{2,1},{3,2},{4,7},{5,4},{6,5},{7,6},{8,11},{9,8},{10,9... | collective-permute-start | bytes 983048 | tf_op jit(solution)/shard_map/ppermute | solution.py:20
  154.3 2.9 %collective-permute-done.19 = bf16[256,896]{1,0:T(8,128)(2,1)S(1)} collective-permute-done((bf16[256,896]{1,0:T(8,128)(2,1)S(1)}, bf16[256,896]{1,0:T(8,128)(2,1)S(1)}, u32[]{:S(2)}, u32[]{:S(2)}) %collective-permute-start.19) | collective-permute-done | bytes 458784 | tf_op jit(solution)/shard_map/ppermute | solution.py:20
  157.9 16.2 %collective-permute-done.17 = bf16[256,640]{0,1:T(8,128)(2,1)S(1)} collective-permute-done((bf16[256,640]{0,1:T(8,128)(2,1)S(1)}, bf16[256,640]{0,1:T(8,128)(2,1)S(1)}, u32[]{:S(2)}, u32[]{:S(2)}) %collective-permute-start.17) | collective-permute-done | bytes 327712 | tf_op jit(solution)/shard_map/ppermute | solution.py:20
  177.7 1.6 fusion.36
  179.4 2.6 %collective-permute-start.23 = (bf16[256,256]{0,1:T(8,128)(2,1)S(1)}, bf16[256,256]{0,1:T(8,128)(2,1)S(1)}, u32[]{:S(2)}, u32[]{:S(2)}) collective-permute-start(bf16[256,256]{0,1:T(8,128)(2,1)S(1)} %fusion.46), channel_id=1, source_target_pairs={{0,2},{1,3},{2,0},{3,1},{4,6},{5,7},{6,4},{7,5},{8,10},{9,11},{10,... | collective-permute-start | bytes 393224 | tf_op jit(solution)/shard_map/ppermute | solution.py:20
  182.4 4.0 %collective-permute-done.23 = bf16[256,256]{0,1:T(8,128)(2,1)S(1)} collective-permute-done((bf16[256,256]{0,1:T(8,128)(2,1)S(1)}, bf16[256,256]{0,1:T(8,128)(2,1)S(1)}, u32[]{:S(2)}, u32[]{:S(2)}) %collective-permute-start.23) | collective-permute-done | bytes 131104 | tf_op jit(solution)/shard_map/ppermute | solution.py:20
  186.4 1.6 fusion.80
  188.1 2.6 %fusion.2 = bf16[32,8,1792]{2,1,0:T(8,128)(2,1)} fusion(f32[256,1792]{1,0:T(8,128)S(1)} %fusion.80, f32[256,1792]{1,0:T(8,128)S(1)} %convolution_add_fusion.1, bf16[256,256]{0,1:T(8,128)(2,1)S(1)} %collective-permute-done.22, bf16[256,1792]{1,0:T(8,128)(2,1)} %collective-permute-done.2), kind=kOutput, calls=%fused_computation.7 | convolution fusion | flops 236257280 | bytes 5636096 | tf_op jit(solution)/shard_map/dot_general | solution.py:213
  190.6 4.6 %all-to-all-start.3 = ((bf16[32,8,1792]{2,1,0:T(8,128)(2,1)}), bf16[32,8,1792]{2,1,0:T(8,128)(2,1)S(1)}, u32[]{:S(2)}, u32[]{:S(2)}) async-start(bf16[32,8,1792]{2,1,0:T(8,128)(2,1)} %fusion.2), calls=%async_computation.3 | async-start | bytes 1835008 | tf_op jit(solution)/shard_map/all_to_all | solution.py:97
  199.5 17.6 %all-to-all-done.3 = bf16[32,8,1792]{2,1,0:T(8,128)(2,1)S(1)} async-done(((bf16[32,8,1792]{2,1,0:T(8,128)(2,1)}), bf16[32,8,1792]{2,1,0:T(8,128)(2,1)S(1)}, u32[]{:S(2)}, u32[]{:S(2)}) %all-to-all-start.3) | async-done | bytes 917536 | tf_op jit(solution)/shard_map/all_to_all | solution.py:97
  217.5 5.3 %collective-permute-start.24 = (f32[16,1792]{1,0:T(8,128)S(1)}, f32[16,1792]{1,0:T(8,128)S(1)}, u32[]{:S(2)}, u32[]{:S(2)}) collective-permute-start(f32[16,1792]{1,0:T(8,128)S(1)} %dynamic-slice_bitcast_fusion.15), channel_id=1, source_target_pairs={{0,4},{4,0},{1,5},{5,1},{2,6},{6,2},{3,7},{7,3},{8,12},{12,8},{9,1... | collective-permute-start | bytes 344072 | tf_op jit(solution)/shard_map/ppermute | solution.py:15
  (163 shorter events, 39.5 us)
Async XLA Ops:
  3.5 31.0 %collective-permute-start.1 = (bf16[256,1792]{1,0:T(8,128)(2,1)}, bf16[256,1792]{1,0:T(8,128)(2,1)S(1)}, u32[]{:S(2)}, u32[]{:S(2)}) collective-permute-start(bf16[256,1792]{1,0:T(8,128)(2,1)} %get-tuple-element.43), channel_id=1, source_target_pairs={{0,1},{1,2},{2,3},{3,0},{4,5},{5,6},{6,7},{7,4},{8,9},{9,10},{10,1... | collective-permute-start | bytes 2752520 | tf_op jit(solution)/shard_map/ppermute | solution.py:20
  5.6 28.9 %collective-permute-start.2 = (bf16[256,1792]{1,0:T(8,128)(2,1)}, bf16[256,1792]{1,0:T(8,128)(2,1)}, u32[]{:S(2)}, u32[]{:S(2)}) collective-permute-start(bf16[256,1792]{1,0:T(8,128)(2,1)} %get-tuple-element.42), channel_id=1, source_target_pairs={{0,3},{1,0},{2,1},{3,2},{4,7},{5,4},{6,5},{7,6},{8,11},{9,8},{10,9... | collective-permute-start | bytes 2752520 | tf_op jit(solution)/shard_map/ppermute | solution.py:20
  7.9 24.3 %collective-permute-start.4 = (bf16[256,896]{1,0:T(8,128)(2,1)}, bf16[256,896]{1,0:T(8,128)(2,1)}, u32[]{:S(2)}, u32[]{:S(2)}) collective-permute-start(bf16[256,896]{1,0:T(8,128)(2,1)} %constant_dynamic-slice_fusion.1), channel_id=1, source_target_pairs={{0,4},{4,0},{1,5},{5,1},{2,6},{6,2},{3,7},{7,3},{8,12},{12,8},{9,1... | collective-permute-start | bytes 1376264 | tf_op jit(solution)/shard_map/ppermute | solution.py:15
  12.7 11.1 %copy-start.11 = (f32[1792]{0:T(1024)S(1)}, f32[1792]{0:T(1024)}, u32[]{:S(2)}) copy-start(f32[1792]{0:T(1024)} %param.20) | copy-start | bytes 21508
  14.0 24.2 %all-to-all-start = ((bf16[32,4,4,512]{3,1,2,0:T(4,128)(2,1)}), bf16[32,4,4,512]{3,1,2,0:T(4,128)(2,1)S(1)}, u32[]{:S(2)}, u32[]{:S(2)}) async-start(bf16[32,4,4,512]{3,1,2,0:T(4,128)(2,1)} %bitcast.142), calls=%async_computation | async-start | bytes 1048576 | tf_op jit(solution)/shard_map/all_to_all | solution.py:97
  23.4 8.7 %collective-permute-start.3 = (bf16[2,512,128]{2,1,0:T(8,128)(2,1)S(1)}, bf16[2,512,128]{2,1,0:T(8,128)(2,1)S(1)}, u32[]{:S(2)}, u32[]{:S(2)}) collective-permute-start(bf16[2,512,128]{2,1,0:T(8,128)(2,1)S(1)} %copy-done.9), channel_id=1, source_target_pairs={{0,4},{4,0},{1,5},{5,1},{2,6},{6,2},{3,7},{7,3},{8,12},{12,8},{9,1... | collective-permute-start | bytes 786440 | tf_op jit(solution)/shard_map/ppermute | solution.py:15
  23.7 10.8 %collective-permute-start.5 = (f32[1792]{0:T(1024)S(1)}, f32[1792]{0:T(1024)S(1)}, u32[]{:S(2)}, u32[]{:S(2)}) collective-permute-start(f32[1792]{0:T(1024)S(1)} %copy-done.11), channel_id=1, source_target_pairs={{0,2},{1,3},{2,0},{3,1},{4,6},{5,7},{6,4},{7,5},{8,10},{9,11},{10,... | collective-permute-start | bytes 21512 | tf_op jit(solution)/shard_map/ppermute | solution.py:20
  34.5 12.2 %copy-start.3 = (bf16[256,1792]{1,0:T(8,128)(2,1)}, bf16[256,1792]{1,0:T(8,128)(2,1)S(1)}, u32[]{:S(2)}) copy-start(bf16[256,1792]{1,0:T(8,128)(2,1)S(1)} %collective-permute-done.1) | copy-start | bytes 2752516
  38.7 5.1 %collective-permute-start.6 = (bf16[32,4,4,128]{3,0,1,2:T(8,128)(2,1)S(1)}, bf16[32,4,4,128]{3,0,1,2:T(8,128)(2,1)S(1)}, u32[]{:S(2)}, u32[]{:S(2)}) collective-permute-start(bf16[32,4,4,128]{3,0,1,2:T(8,128)(2,1)S(1)} %fusion.24), channel_id=1, source_target_pairs={{0,1},{1,2},{2,3},{3,0},{4,5},{5,6},{6,7},{7,4},{8,9},{9,10},{10,1... | collective-permute-start | bytes 393224 | tf_op jit(solution)/shard_map/ppermute | solution.py:20
  38.8 6.4 %collective-permute-start.7 = (bf16[32,4,4,128]{3,0,1,2:T(8,128)(2,1)S(1)}, bf16[32,4,4,128]{3,0,1,2:T(8,128)(2,1)S(1)}, u32[]{:S(2)}, u32[]{:S(2)}) collective-permute-start(bf16[32,4,4,128]{3,0,1,2:T(8,128)(2,1)S(1)} %fusion.24), channel_id=1, source_target_pairs={{0,2},{1,3},{2,0},{3,1},{4,6},{5,7},{6,4},{7,5},{8,10},{9,11},{10,... | collective-permute-start | bytes 393224 | tf_op jit(solution)/shard_map/ppermute | solution.py:20
  41.5 4.6 %collective-permute-start.8 = (bf16[32,4,4,128]{3,0,1,2:T(8,128)(2,1)S(1)}, bf16[32,4,4,128]{3,0,1,2:T(8,128)(2,1)S(1)}, u32[]{:S(2)}, u32[]{:S(2)}) collective-permute-start(bf16[32,4,4,128]{3,0,1,2:T(8,128)(2,1)S(1)} %fusion.24), channel_id=1, source_target_pairs={{0,3},{1,0},{2,1},{3,2},{4,7},{5,4},{6,5},{7,6},{8,11},{9,8},{10,9... | collective-permute-start | bytes 393224 | tf_op jit(solution)/shard_map/ppermute | solution.py:20
  46.8 5.6 %collective-permute-start.9 = (bf16[32,16,512]{2,1,0:T(8,128)(2,1)S(1)}, bf16[32,16,512]{2,1,0:T(8,128)(2,1)S(1)}, u32[]{:S(2)}, u32[]{:S(2)}) collective-permute-start(bf16[32,16,512]{2,1,0:T(8,128)(2,1)S(1)} %reshape.340), channel_id=1, source_target_pairs={{0,4},{4,0},{1,5},{5,1},{2,6},{6,2},{3,7},{7,3},{8,12},{12,8},{9,1... | collective-permute-start | bytes 1572872 | tf_op jit(solution)/shard_map/ppermute | solution.py:15
  55.0 49.7 %all-to-all-start.1 = ((bf16[32,32,896]{2,1,0:T(8,128)(2,1)}), bf16[32,32,896]{2,1,0:T(8,128)(2,1)S(1)}, u32[]{:S(2)}, u32[]{:S(2)}) async-start(bf16[32,32,896]{2,1,0:T(8,128)(2,1)} %bitcast.145), calls=%async_computation.1 | async-start | bytes 3670016 | tf_op jit(solution)/shard_map/all_to_all | solution.py:97
  61.8 6.5 %collective-permute-start = (bf16[16,896]{1,0:T(8,128)(2,1)S(1)}, bf16[16,896]{1,0:T(8,128)(2,1)S(1)}, u32[]{:S(2)}, u32[]{:S(2)}) collective-permute-start(bf16[16,896]{1,0:T(8,128)(2,1)S(1)} %constant_dynamic-slice_fusion.2), channel_id=1, source_target_pairs={{0,4},{4,0},{1,5},{5,1},{2,6},{6,2},{3,7},{7,3},{8,12},{12,8},{9,1... | collective-permute-start | bytes 86024 | tf_op jit(solution)/shard_map/ppermute | solution.py:15
  62.6 1.2 collective-permute-start.11
  65.6 48.2 %collective-permute-start.13 = (bf16[1792,512]{1,0:T(8,128)(2,1)}, bf16[1792,512]{1,0:T(8,128)(2,1)}, u32[]{:S(2)}, u32[]{:S(2)}) collective-permute-start(bf16[1792,512]{1,0:T(8,128)(2,1)} %pad_maximum_fusion), channel_id=1, source_target_pairs={{0,1},{1,2},{2,3},{3,0},{4,5},{5,6},{6,7},{7,4},{8,9},{9,10},{10,1... | collective-permute-start | bytes 5505032 | tf_op jit(solution)/shard_map/ppermute | solution.py:20
  66.8 47.1 %collective-permute-start.14 = (bf16[1792,512]{1,0:T(8,128)(2,1)}, bf16[1792,512]{1,0:T(8,128)(2,1)}, u32[]{:S(2)}, u32[]{:S(2)}) collective-permute-start(bf16[1792,512]{1,0:T(8,128)(2,1)} %pad_maximum_fusion.1), channel_id=1, source_target_pairs={{0,3},{1,0},{2,1},{3,2},{4,7},{5,4},{6,5},{7,6},{8,11},{9,8},{10,9... | collective-permute-start | bytes 5505032 | tf_op jit(solution)/shard_map/ppermute | solution.py:20
  106.5 29.3 %all-to-all-start.2 = ((bf16[32,16,896]{2,1,0:T(8,128)(2,1)}), bf16[32,16,896]{2,1,0:T(8,128)(2,1)S(1)}, u32[]{:S(2)}, u32[]{:S(2)}) async-start(bf16[32,16,896]{2,1,0:T(8,128)(2,1)} %bitcast.35), calls=%async_computation.2 | async-start | bytes 1835008 | tf_op jit(solution)/shard_map/all_to_all | solution.py:97
  113.9 29.6 %collective-permute-start.15 = (bf16[256,1792]{1,0:T(8,128)(2,1)S(1)}, bf16[256,1792]{1,0:T(8,128)(2,1)}, u32[]{:S(2)}, u32[]{:S(2)}) collective-permute-start(bf16[256,1792]{1,0:T(8,128)(2,1)S(1)} %copy-done.5), channel_id=1, source_target_pairs={{0,2},{1,3},{2,0},{3,1},{4,6},{5,7},{6,4},{7,5},{8,10},{9,11},{10,... | collective-permute-start | bytes 2752520 | tf_op jit(solution)/shard_map/ppermute | solution.py:20
  136.6 8.7 %collective-permute-start.16 = (bf16[32,8,896]{2,1,0:T(8,128)(2,1)}, bf16[32,8,896]{2,1,0:T(8,128)(2,1)S(1)}, u32[]{:S(2)}, u32[]{:S(2)}) collective-permute-start(bf16[32,8,896]{2,1,0:T(8,128)(2,1)} %get-tuple-element.49), channel_id=1, source_target_pairs={{0,4},{4,0},{1,5},{5,1},{2,6},{6,2},{3,7},{7,3},{8,12},{12,8},{9,1... | collective-permute-start | bytes 1376264 | tf_op jit(solution)/shard_map/ppermute | solution.py:15
  143.5 13.7 %collective-permute-start.19 = (bf16[256,896]{1,0:T(8,128)(2,1)S(1)}, bf16[256,896]{1,0:T(8,128)(2,1)S(1)}, u32[]{:S(2)}, u32[]{:S(2)}) collective-permute-start(bf16[256,896]{1,0:T(8,128)(2,1)S(1)} %get-tuple-element.26), channel_id=1, source_target_pairs={{0,2},{1,3},{2,0},{3,1},{4,6},{5,7},{6,4},{7,5},{8,10},{9,11},{10,... | collective-permute-start | bytes 1376264 | tf_op jit(solution)/shard_map/ppermute | solution.py:20
  145.3 29.1 %collective-permute-start.20 = (bf16[256,896]{1,0:T(8,128)(2,1)S(1)}, bf16[256,896]{1,0:T(8,128)(2,1)S(1)}, u32[]{:S(2)}, u32[]{:S(2)}) collective-permute-start(bf16[256,896]{1,0:T(8,128)(2,1)S(1)} %bitcast.147), channel_id=1, source_target_pairs={{0,2},{1,3},{2,0},{3,1},{4,6},{5,7},{6,4},{7,5},{8,10},{9,11},{10,... | collective-permute-start | bytes 1376264 | tf_op jit(solution)/shard_map/ppermute | solution.py:20
  151.8 22.2 %collective-permute-start.17 = (bf16[256,640]{0,1:T(8,128)(2,1)S(1)}, bf16[256,640]{0,1:T(8,128)(2,1)S(1)}, u32[]{:S(2)}, u32[]{:S(2)}) collective-permute-start(bf16[256,640]{0,1:T(8,128)(2,1)S(1)} %get-tuple-element.56), channel_id=1, source_target_pairs={{0,3},{1,0},{2,1},{3,2},{4,7},{5,4},{6,5},{7,6},{8,11},{9,8},{10,9... | collective-permute-start | bytes 983048 | tf_op jit(solution)/shard_map/ppermute | solution.py:20
  154.3 20.0 %collective-permute-start.18 = (bf16[256,640]{0,1:T(8,128)(2,1)S(1)}, bf16[256,640]{0,1:T(8,128)(2,1)S(1)}, u32[]{:S(2)}, u32[]{:S(2)}) collective-permute-start(bf16[256,640]{0,1:T(8,128)(2,1)S(1)} %get-tuple-element.57), channel_id=1, source_target_pairs={{0,1},{1,2},{2,3},{3,0},{4,5},{5,6},{6,7},{7,4},{8,9},{9,10},{10,1... | collective-permute-start | bytes 983048 | tf_op jit(solution)/shard_map/ppermute | solution.py:20
  176.3 5.6 %collective-permute-start.21 = (bf16[256,256]{0,1:T(8,128)(2,1)S(1)}, bf16[256,256]{0,1:T(8,128)(2,1)S(1)}, u32[]{:S(2)}, u32[]{:S(2)}) collective-permute-start(bf16[256,256]{0,1:T(8,128)(2,1)S(1)} %fusion.46), channel_id=1, source_target_pairs={{0,1},{1,2},{2,3},{3,0},{4,5},{5,6},{6,7},{7,4},{8,9},{9,10},{10,1... | collective-permute-start | bytes 393224 | tf_op jit(solution)/shard_map/ppermute | solution.py:20
  179.4 7.1 %collective-permute-start.23 = (bf16[256,256]{0,1:T(8,128)(2,1)S(1)}, bf16[256,256]{0,1:T(8,128)(2,1)S(1)}, u32[]{:S(2)}, u32[]{:S(2)}) collective-permute-start(bf16[256,256]{0,1:T(8,128)(2,1)S(1)} %fusion.46), channel_id=1, source_target_pairs={{0,2},{1,3},{2,0},{3,1},{4,6},{5,7},{6,4},{7,5},{8,10},{9,11},{10,... | collective-permute-start | bytes 393224 | tf_op jit(solution)/shard_map/ppermute | solution.py:20
  181.9 6.1 %collective-permute-start.22 = (bf16[256,256]{0,1:T(8,128)(2,1)S(1)}, bf16[256,256]{0,1:T(8,128)(2,1)S(1)}, u32[]{:S(2)}, u32[]{:S(2)}) collective-permute-start(bf16[256,256]{0,1:T(8,128)(2,1)S(1)} %fusion.46), channel_id=1, source_target_pairs={{0,3},{1,0},{2,1},{3,2},{4,7},{5,4},{6,5},{7,6},{8,11},{9,8},{10,9... | collective-permute-start | bytes 393224 | tf_op jit(solution)/shard_map/ppermute | solution.py:20
  190.6 26.5 %all-to-all-start.3 = ((bf16[32,8,1792]{2,1,0:T(8,128)(2,1)}), bf16[32,8,1792]{2,1,0:T(8,128)(2,1)S(1)}, u32[]{:S(2)}, u32[]{:S(2)}) async-start(bf16[32,8,1792]{2,1,0:T(8,128)(2,1)} %fusion.2), calls=%async_computation.3 | async-start | bytes 1835008 | tf_op jit(solution)/shard_map/all_to_all | solution.py:97
  195.3 2.2 %collective-permute-start.12 = (bf16[16,8]{1,0:T(8,128)(2,1)S(1)}, bf16[16,8]{1,0:T(8,128)(2,1)S(1)}, u32[]{:S(2)}, u32[]{:S(2)}) collective-permute-start(bf16[16,8]{1,0:T(8,128)(2,1)S(1)} %bitcast.159), channel_id=1, source_target_pairs={{0,4},{4,0},{1,5},{5,1},{2,6},{6,2},{3,7},{7,3},{8,12},{12,8},{9,1... | collective-permute-start | bytes 776 | tf_op jit(solution)/shard_map/ppermute | solution.py:15
  198.1 26.2 %copy-start.1 = (bf16[2,2,128,576]{2,3,1,0:T(8,128)(2,1)S(1)}, bf16[2,2,128,576]{2,3,1,0:T(8,128)(2,1)}, u32[]{:S(2)}) copy-start(bf16[2,2,128,576]{2,3,1,0:T(8,128)(2,1)} %param.14) | copy-start | bytes 1769476
  198.2 1.3 collective-permute-start.10
  217.5 6.2 %collective-permute-start.24 = (f32[16,1792]{1,0:T(8,128)S(1)}, f32[16,1792]{1,0:T(8,128)S(1)}, u32[]{:S(2)}, u32[]{:S(2)}) collective-permute-start(f32[16,1792]{1,0:T(8,128)S(1)} %dynamic-slice_bitcast_fusion.15), channel_id=1, source_target_pairs={{0,4},{4,0},{1,5},{5,1},{2,6},{6,2},{3,7},{7,3},{8,12},{12,8},{9,1... | collective-permute-start | bytes 344072 | tf_op jit(solution)/shard_map/ppermute | solution.py:15
  (13 other events, 98.6 us)

commit v3 on v2

--- a/solution.py
+++ b/solution.py
@@ -112,7 +112,7 @@
             axis=1,
         )
 
-    down_parts = {d: send_y(down_block(y + d), d) for d in near}
+    near_down = {d: send_y(down_block(y + d), d) for d in near}
     near_up = {d: up_block(y + d) for d in near}
     far_gain = {d: send_y(norm_gain, d) for d in far}
 
@@ -130,8 +130,8 @@
     context = attend(queries, latent_cache, new_latent, lengths, lat, (vdim + rope) ** (-0.5))
     context = context.reshape(own_tokens, chips, heads_chip, lat).transpose(1, 0, 2, 3)
     context = over_chips(context)
-    context, down_parts, near_up, vp, op, far_gain = lax.optimization_barrier(
-        (context, down_parts, near_up, vp, op, far_gain)
+    context, near_down, near_up, vp, op, far_gain = lax.optimization_barrier(
+        (context, near_down, near_up, vp, op, far_gain)
     )
     values = jnp.einsum("nthl,hlv->nthv", context, vp, preferred_element_type=F32).astype(BF16)
 
@@ -155,13 +155,13 @@
 
     chip_slots = jnp.stack([slots_of(chip_ids[0]), slots_of(chip_ids[1])])
     group_of = jnp.arange(NC)[:, None, None]
-    row_of = (chip_ids * NC + group_of) * CAP + chip_slots
+    row_of = ((chip_ids ^ core) * NC + group_of) * CAP + chip_slots
     row_of = row_of.reshape(NC * group, -1)
     row_ids = jnp.arange(chips * NC * NC * CAP)[None, None, :]
     named = row_of[:, :, None] == row_ids
     weighted = named.astype(F32) * chip_gates.reshape(NC * group, -1)[:, :, None]
     combine = jnp.sum(weighted, axis=1).astype(BF16).reshape(NC * group, chips, NC, NC * CAP)
-    combine = lax.dynamic_index_in_dim(combine, core, 2, keepdims=False)
+    combine = combine[:, :, 0]
     spread = jnp.sum((row_of[place][:, :, None] == row_ids).astype(F32), axis=1).astype(BF16)
 
     residual = placed_hidden + sums
@@ -172,13 +172,12 @@
     ).astype(BF16)
     tokens = over_chips(outgoing.reshape(chips, NC * NC * CAP, half))
     tokens = tokens.reshape(chips, NC, NC * CAP, half)
-    kept = lax.dynamic_index_in_dim(tokens, core, 1, keepdims=False).reshape(slots, half)
-    received = swap(lax.dynamic_index_in_dim(tokens, 1 - core, 1, keepdims=False))
-    received = received.reshape(slots, half)
+    kept, given = tokens[:, 0].reshape(slots, half), tokens[:, 1].reshape(slots, half)
+    received = swap(given)
     kept, far_down = lax.optimization_barrier((kept, far_down))
-    far_tokens = {d: (send_y(kept, d), send_y(received, d)) for d in far}
-    down_parts.update(far_down)
-    down_parts[0] = down_block(y)
+    far_tokens = {d: (send_y(kept, d), swap(send_y(given, d))) for d in far}
+    down_all = [down_block(y)] + [near_down[d] for d in near] + [far_down[d] for d in far]
+    down_all = jnp.concatenate(down_all, axis=0)
     tokens = in_core_order(core, kept, received, axis=1)
 
     residual = residual.reshape(NC, group, half)
@@ -208,10 +207,8 @@
             squares = squares + share(part, half_of(far_gain[d], which))
     sums = sums * lax.rsqrt(squares / width + EPS)
     act = (jax.nn.silu(sums[:, :units]) * sums[:, units:]).astype(BF16)
-    acts = {0: act, **{d: send_y(act, d) for d in near + far}}
-    result = sum(
-        jnp.dot(acts[d], down_parts[d], preferred_element_type=F32) for d in (0,) + near + far
-    )
+    acts = jnp.concatenate([act] + [send_y(act, d) for d in near + far], axis=1)
+    result = jnp.dot(acts, down_all, preferred_element_type=F32)
     result = result.astype(BF16).reshape(chips, NC * CAP, cols)
 
     returned = over_chips(result).reshape(slots, cols)

time: 225 us -> 224 us (level)
  matrix products: 19.1 us -> 16.8 us
    dot_general x4 -> x1, matrix products: 6.27 us -> 3.9 us  [on_device(): result = jnp.dot(acts, down_all, preferred_element_type=F32)]
    ppermute x9 -> x10, starting transfers between devices: 20.6 us -> 21.9 us  [swap(): return lax.ppermute(value, 'c', [(0, 1), (1, 0)])]
  transfers between devices with their start and end apart: 29 -> 30, of which waited for: 16 -> 18; matrix products, arithmetic and copies ran while one was open for 14% -> 13% of each run, Pallas kernels for 0% -> 0%
where the time goes in v3:
time: 224 us; the launch traced here: 223 us
  waiting for transfers between devices  108 us (48%)
  starting transfers between devices  72.9 us (33%)
  matrix products  16.8 us (8%)
  local copies, waits for them, and re-layouts  16.4 us (7%)
  other arithmetic  8.34 us (4%)
    all_to_all x4, waiting for transfers between devices, over_chips(): return lax.all_to_all(value, CHIPS, 0, 0, tiled=True)  77.3 us
    all_to_all x4, starting transfers between devices, over_chips(): return lax.all_to_all(value, CHIPS, 0, 0, tiled=True)  28 us
    ppermute x16, waiting for transfers between devices, send_y(): lax.ppermute(value, 'y', [(i, (i + distance) % size) for i in range(size)])  27.5 us
    ppermute x16, starting transfers between devices, send_y(): lax.ppermute(value, 'y', [(i, (i + distance) % size) for i in range(size)])  22.9 us
    ppermute x10, starting transfers between devices, swap(): return lax.ppermute(value, 'c', [(0, 1), (1, 0)])  21.9 us
    dot_general x2, matrix products, on_device(): part = jnp.dot(tokens, up_parts[d], preferred_element_type=F32)  4.72 us
  transfers between devices with their start and end apart: 30, of which 18 were waited for; matrix products, arithmetic and copies ran while one was open for 13% of the time, Pallas kernels for 0%

profile of v3, /device:TPU:1, one launch (start us, length us, event | category | flops | bytes accessed | tf_op | source)
XLA Modules:
  0.0 223.4 jit_solution(2071028698271486924)
XLA Ops:
  0.0 4.1 %dynamic-slice_bitcast_fusion = (bf16[256,1792]{1,0:T(8,128)(2,1)}, bf16[256,1792]{1,0:T(8,128)(2,1)}, bf16[256,1792]{1,0:T(8,128)(2,1)}, bf16[256,1792]{1,0:T(8,128)(2,1)}) fusion(bf16[1,256,7168]{2,1,0:T(8,128)(2,1)} %param.23, s32[]{:T(128)S(6)} %select_n.283, s32[]{:T(128)S(6)} %select_n.258, s32[]{:T(128)S(6)} %select_n.256, s32[]{:T(128)S(6)} %select_n.279), kind=kLoop, calls=%fused_computation.49 | loop fusion | bytes 7340048 | tf_op jit(solution)/shard_map/dynamic_slice | solution.py:100
  4.1 2.1 collective-permute-start.1
  8.6 2.8 %collective-permute-start.4 = (bf16[256,896]{1,0:T(8,128)(2,1)}, bf16[256,896]{1,0:T(8,128)(2,1)}, u32[]{:S(2)}, u32[]{:S(2)}) collective-permute-start(bf16[256,896]{1,0:T(8,128)(2,1)} %constant_dynamic-slice_fusion), channel_id=1, source_target_pairs={{0,4},{4,0},{1,5},{5,1},{2,6},{6,2},{3,7},{7,3},{8,12},{12,8},{9,1... | collective-permute-start | bytes 1376264 | tf_op jit(solution)/shard_map/ppermute | solution.py:15
  14.6 9.3 %all-to-all-start = ((bf16[32,4,4,512]{3,1,2,0:T(4,128)(2,1)}), bf16[32,4,4,512]{3,1,2,0:T(4,128)(2,1)S(1)}, u32[]{:S(2)}, u32[]{:S(2)}) async-start(bf16[32,4,4,512]{3,1,2,0:T(4,128)(2,1)} %bitcast.133), calls=%async_computation | async-start | bytes 1048576 | tf_op jit(solution)/shard_map/all_to_all | solution.py:97
  24.3 1.7 collective-permute-start.5
  26.0 3.8 %dynamic-slice_bitcast_fusion.1 = (bf16[1792,256]{1,0:T(8,128)(2,1)S(1)}, bf16[1792,256]{1,0:T(8,128)(2,1)S(1)}, bf16[1792,256]{1,0:T(8,128)(2,1)S(1)}, bf16[179...) fusion(bf16[1,7168,256]{2,1,0:T(8,128)(2,1)} %param.22, s32[]{:T(128)S(6)} %select_n.283, ...), kind=kLoop, calls=%fused_computation.52 | loop fusion | bytes 11010060 | tf_op jit(solution)/shard_map/dynamic_slice | solution.py:103
  35.1 3.7 %all-to-all-done = bf16[32,4,4,512]{3,1,2,0:T(4,128)(2,1)S(1)} async-done(((bf16[32,4,4,512]{3,1,2,0:T(4,128)(2,1)}), bf16[32,4,4,512]{3,1,2,0:T(4,128)(2,1)S(1)}, u32[]{:S(2)}, u32[]{:S(2)}) %all-to-all-start) | async-done | bytes 524320 | tf_op jit(solution)/shard_map/all_to_all | solution.py:97
  39.4 2.6 %collective-permute-start.7 = (bf16[32,4,4,128]{3,0,1,2:T(8,128)(2,1)S(1)}, bf16[32,4,4,128]{3,0,1,2:T(8,128)(2,1)S(1)}, u32[]{:S(2)}, u32[]{:S(2)}) collective-permute-start(bf16[32,4,4,128]{3,0,1,2:T(8,128)(2,1)S(1)} %fusion.30), channel_id=1, source_target_pairs={{0,2},{1,3},{2,0},{3,1},{4,6},{5,7},{6,4},{7,5},{8,10},{9,11},{10,... | collective-permute-start | bytes 393224 | tf_op jit(solution)/shard_map/ppermute | solution.py:20
  47.4 4.0 %collective-permute-start.9 = (bf16[32,16,512]{2,1,0:T(8,128)(2,1)S(1)}, bf16[32,16,512]{2,1,0:T(8,128)(2,1)S(1)}, u32[]{:S(2)}, u32[]{:S(2)}) collective-permute-start(bf16[32,16,512]{2,1,0:T(8,128)(2,1)S(1)} %reshape.334), channel_id=1, source_target_pairs={{0,4},{4,0},{1,5},{5,1},{2,6},{6,2},{3,7},{7,3},{8,12},{12,8},{9,1... | collective-permute-start | bytes 1572872 | tf_op jit(solution)/shard_map/ppermute | solution.py:15
  53.0 2.6 %convolution_convert_fusion = bf16[1024,896]{1,0:T(8,128)(2,1)} fusion(bf16[1024,512]{1,0:T(8,128)(2,1)S(1)} %bitcast.137, bf16[512,896]{1,0:T(8,128)(2,1)S(1)} %copy-done.2), kind=kOutput, calls=%fused_computation.20 | convolution fusion | flops 940441600 | bytes 3801088 | tf_op jit(solution)/shard_map/dot_general | solution.py:142
  55.6 6.7 %all-to-all-start.1 = ((bf16[32,32,896]{2,1,0:T(8,128)(2,1)}), bf16[32,32,896]{2,1,0:T(8,128)(2,1)S(1)}, u32[]{:S(2)}, u32[]{:S(2)}) async-start(bf16[32,32,896]{2,1,0:T(8,128)(2,1)} %bitcast.136), calls=%async_computation.1 | async-start | bytes 3670016 | tf_op jit(solution)/shard_map/all_to_all | solution.py:97
  67.4 1.6 collective-permute-start.14
  69.8 35.6 %all-to-all-done.1 = bf16[32,32,896]{2,1,0:T(8,128)(2,1)S(1)} async-done(((bf16[32,32,896]{2,1,0:T(8,128)(2,1)}), bf16[32,32,896]{2,1,0:T(8,128)(2,1)S(1)}, u32[]{:S(2)}, u32[]{:S(2)}) %all-to-all-start.1) | async-done | bytes 1835040 | tf_op jit(solution)/shard_map/all_to_all | solution.py:97
  107.1 7.4 %all-to-all-start.2 = ((bf16[32,16,896]{2,1,0:T(8,128)(2,1)}), bf16[32,16,896]{2,1,0:T(8,128)(2,1)S(1)}, u32[]{:S(2)}, u32[]{:S(2)}) async-start(bf16[32,16,896]{2,1,0:T(8,128)(2,1)} %bitcast.35), calls=%async_computation.2 | async-start | bytes 1835008 | tf_op jit(solution)/shard_map/all_to_all | solution.py:97
  114.5 1.8 collective-permute-start.15
  116.3 20.1 %all-to-all-done.2 = bf16[32,16,896]{2,1,0:T(8,128)(2,1)S(1)} async-done(((bf16[32,16,896]{2,1,0:T(8,128)(2,1)}), bf16[32,16,896]{2,1,0:T(8,128)(2,1)S(1)}, u32[]{:S(2)}, u32[]{:S(2)}) %all-to-all-start.2) | async-done | bytes 917536 | tf_op jit(solution)/shard_map/all_to_all | solution.py:97
  136.4 5.3 %collective-permute-start.16 = (bf16[256,896]{1,0:T(8,128)(2,1)S(1)}, bf16[256,896]{1,0:T(8,128)(2,1)S(1)}, u32[]{:S(2)}, u32[]{:S(2)}) collective-permute-start(bf16[256,896]{1,0:T(8,128)(2,1)S(1)} %get-tuple-element.49), channel_id=1, source_target_pairs={{0,4},{4,0},{1,5},{5,1},{2,6},{6,2},{3,7},{7,3},{8,12},{12,8},{9,1... | collective-permute-start | bytes 1376264 | tf_op jit(solution)/shard_map/ppermute | solution.py:15
  141.7 1.6 dynamic-slice_bitcast_fusion.10
  143.4 1.7 collective-permute-start.20
  146.8 2.4 %convolution_convert_fusion.2 = bf16[256,512]{0,1:T(8,128)(2,1)S(1)} fusion(bf16[1792,512]{1,0:T(8,128)(2,1)} %collective-permute-done.14, bf16[256,896]{1,0:T(8,128)(2,1)S(1)} %get-tuple-element.48, bf16[256,896]{1,0:T(8,128)(2,1)S(1)} %get-tuple-element.47), kind=kOutput, calls=%fused_computation.31 | convolution fusion | flops 471728128 | bytes 3014656 | tf_op jit(solution)/shard_map/dot_general | solution.py:198
  149.3 2.4 %convolution_convert_fusion.3 = bf16[256,512]{0,1:T(8,128)(2,1)S(1)} fusion(bf16[1792,512]{1,0:T(8,128)(2,1)} %collective-permute-done.13, bf16[256,896]{1,0:T(8,128)(2,1)S(1)} %get-tuple-element.48, bf16[256,896]{1,0:T(8,128)(2,1)S(1)} %get-tuple-element.47), kind=kOutput, calls=%fused_computation.32 | convolution fusion | flops 471728128 | bytes 3014656 | tf_op jit(solution)/shard_map/dot_general | solution.py:198
  151.7 2.5 %collective-permute-start.17 = (bf16[256,640]{0,1:T(8,128)(2,1)S(1)}, bf16[256,640]{0,1:T(8,128)(2,1)S(1)}, u32[]{:S(2)}, u32[]{:S(2)}) collective-permute-start(bf16[256,640]{0,1:T(8,128)(2,1)S(1)} %get-tuple-element.57), channel_id=1, source_target_pairs={{0,3},{1,0},{2,1},{3,2},{4,7},{5,4},{6,5},{7,6},{8,11},{9,8},{10,9... | collective-permute-start | bytes 983048 | tf_op jit(solution)/shard_map/ppermute | solution.py:20
  154.2 2.8 %collective-permute-done.20 = bf16[256,896]{1,0:T(8,128)(2,1)S(1)} collective-permute-done((bf16[256,896]{1,0:T(8,128)(2,1)S(1)}, bf16[256,896]{1,0:T(8,128)(2,1)S(1)}, u32[]{:S(2)}, u32[]{:S(2)}) %collective-permute-start.20) | collective-permute-done | bytes 458784 | tf_op jit(solution)/shard_map/ppermute | solution.py:20
  158.3 8.6 %collective-permute-done.19 = bf16[256,896]{1,0:T(8,128)(2,1)S(1)} collective-permute-done((bf16[256,896]{1,0:T(8,128)(2,1)S(1)}, bf16[256,896]{1,0:T(8,128)(2,1)S(1)}, u32[]{:S(2)}, u32[]{:S(2)}) %collective-permute-start.19) | collective-permute-done | bytes 458784 | tf_op jit(solution)/shard_map/ppermute | solution.py:20
  167.6 6.3 %collective-permute-done.17 = bf16[256,640]{0,1:T(8,128)(2,1)S(1)} collective-permute-done((bf16[256,640]{0,1:T(8,128)(2,1)S(1)}, bf16[256,640]{0,1:T(8,128)(2,1)S(1)}, u32[]{:S(2)}, u32[]{:S(2)}) %collective-permute-start.17) | collective-permute-done | bytes 327712 | tf_op jit(solution)/shard_map/ppermute | solution.py:20
  179.8 2.0 collective-permute-done.22
  181.8 3.9 %collective-permute-done.24 = bf16[256,256]{0,1:T(8,128)(2,1)S(1)} collective-permute-done((bf16[256,256]{0,1:T(8,128)(2,1)S(1)}, bf16[256,256]{0,1:T(8,128)(2,1)S(1)}, u32[]{:S(2)}, u32[]{:S(2)}) %collective-permute-start.24) | collective-permute-done | bytes 131104 | tf_op jit(solution)/shard_map/ppermute | solution.py:20
  185.7 3.9 %fusion.11 = bf16[32,8,1792]{2,1,0:T(8,128)(2,1)} fusion(bf16[256,1792]{1,0:T(8,128)(2,1)} %collective-permute-done.15, bf16[256,1792]{1,0:T(8,128)(2,1)} %collective-permute-done.2, bf16[256,1792]{1,0:T(8,128)(2,1)} %collective-permute-done.1, bf16[256,1792]{1,0:T(8,128)(2,1)S(1)} %copy-done.4, bf16[256,256]{0,1:T(8,128)(2,1)S(1)} %collective-permute-done.24, ...), kind=kOutput, calls=%fused_computation.12 | convolution fusion | flops 956760064 | bytes 5111808 | tf_op jit(solution)/shard_map/dot_general | solution.py:211
  189.6 4.6 %all-to-all-start.3 = ((bf16[32,8,1792]{2,1,0:T(8,128)(2,1)}), bf16[32,8,1792]{2,1,0:T(8,128)(2,1)S(1)}, u32[]{:S(2)}, u32[]{:S(2)}) async-start(bf16[32,8,1792]{2,1,0:T(8,128)(2,1)} %fusion.11), calls=%async_computation.3 | async-start | bytes 1835008 | tf_op jit(solution)/shard_map/all_to_all | solution.py:97
  194.3 1.6 collective-permute-start.12
  198.4 17.9 %all-to-all-done.3 = bf16[32,8,1792]{2,1,0:T(8,128)(2,1)S(1)} async-done(((bf16[32,8,1792]{2,1,0:T(8,128)(2,1)}), bf16[32,8,1792]{2,1,0:T(8,128)(2,1)S(1)}, u32[]{:S(2)}, u32[]{:S(2)}) %all-to-all-start.3) | async-done | bytes 917536 | tf_op jit(solution)/shard_map/all_to_all | solution.py:97
  216.6 5.2 %collective-permute-start.25 = (f32[16,1792]{1,0:T(8,128)S(1)}, f32[16,1792]{1,0:T(8,128)S(1)}, u32[]{:S(2)}, u32[]{:S(2)}) collective-permute-start(f32[16,1792]{1,0:T(8,128)S(1)} %dynamic-slice_bitcast_fusion.14), channel_id=1, source_target_pairs={{0,4},{4,0},{1,5},{5,1},{2,6},{6,2},{3,7},{7,3},{8,12},{12,8},{9,1... | collective-permute-start | bytes 344072 | tf_op jit(solution)/shard_map/ppermute | solution.py:15
  (158 shorter events, 40.2 us)
Async XLA Ops:
  0.0 11.5 %copy-start = (bf16[2,2,128,576]{2,3,1,0:T(8,128)(2,1)S(1)}, bf16[2,2,128,576]{2,3,1,0:T(8,128)(2,1)}, u32[]{:S(2)}) copy-start(bf16[2,2,128,576]{2,3,1,0:T(8,128)(2,1)} %param.14) | copy-start | bytes 1769476
  0.0 11.5 %copy-start.5 = (bf16[2,256,576]{1,2,0:T(8,128)(2,1)S(1)}, bf16[2,256,576]{1,2,0:T(8,128)(2,1)}, u32[]{:S(2)}) copy-start(bf16[2,256,576]{1,2,0:T(8,128)(2,1)} %param.15) | copy-start | bytes 1769476
  4.1 30.9 %collective-permute-start.1 = (bf16[256,1792]{1,0:T(8,128)(2,1)}, bf16[256,1792]{1,0:T(8,128)(2,1)}, u32[]{:S(2)}, u32[]{:S(2)}) collective-permute-start(bf16[256,1792]{1,0:T(8,128)(2,1)} %get-tuple-element.43), channel_id=1, source_target_pairs={{0,1},{1,2},{2,3},{3,0},{4,5},{5,6},{6,7},{7,4},{8,9},{9,10},{10,1... | collective-permute-start | bytes 2752520 | tf_op jit(solution)/shard_map/ppermute | solution.py:20
  6.3 28.8 %collective-permute-start.2 = (bf16[256,1792]{1,0:T(8,128)(2,1)}, bf16[256,1792]{1,0:T(8,128)(2,1)}, u32[]{:S(2)}, u32[]{:S(2)}) collective-permute-start(bf16[256,1792]{1,0:T(8,128)(2,1)} %get-tuple-element.42), channel_id=1, source_target_pairs={{0,3},{1,0},{2,1},{3,2},{4,7},{5,4},{6,5},{7,6},{8,11},{9,8},{10,9... | collective-permute-start | bytes 2752520 | tf_op jit(solution)/shard_map/ppermute | solution.py:20
  8.6 24.1 %collective-permute-start.4 = (bf16[256,896]{1,0:T(8,128)(2,1)}, bf16[256,896]{1,0:T(8,128)(2,1)}, u32[]{:S(2)}, u32[]{:S(2)}) collective-permute-start(bf16[256,896]{1,0:T(8,128)(2,1)} %constant_dynamic-slice_fusion), channel_id=1, source_target_pairs={{0,4},{4,0},{1,5},{5,1},{2,6},{6,2},{3,7},{7,3},{8,12},{12,8},{9,1... | collective-permute-start | bytes 1376264 | tf_op jit(solution)/shard_map/ppermute | solution.py:15
  14.6 24.2 %all-to-all-start = ((bf16[32,4,4,512]{3,1,2,0:T(4,128)(2,1)}), bf16[32,4,4,512]{3,1,2,0:T(4,128)(2,1)S(1)}, u32[]{:S(2)}, u32[]{:S(2)}) async-start(bf16[32,4,4,512]{3,1,2,0:T(4,128)(2,1)} %bitcast.133), calls=%async_computation | async-start | bytes 1048576 | tf_op jit(solution)/shard_map/all_to_all | solution.py:97
  23.9 8.7 %collective-permute-start.3 = (bf16[2,512,128]{2,1,0:T(8,128)(2,1)S(1)}, bf16[2,512,128]{2,1,0:T(8,128)(2,1)S(1)}, u32[]{:S(2)}, u32[]{:S(2)}) collective-permute-start(bf16[2,512,128]{2,1,0:T(8,128)(2,1)S(1)} %copy-done.6), channel_id=1, source_target_pairs={{0,4},{4,0},{1,5},{5,1},{2,6},{6,2},{3,7},{7,3},{8,12},{12,8},{9,1... | collective-permute-start | bytes 786440 | tf_op jit(solution)/shard_map/ppermute | solution.py:15
  24.3 10.7 %collective-permute-start.5 = (f32[1792]{0:T(1024)S(1)}, f32[1792]{0:T(1024)S(1)}, u32[]{:S(2)}, u32[]{:S(2)}) collective-permute-start(f32[1792]{0:T(1024)S(1)} %copy-done.8), channel_id=1, source_target_pairs={{0,2},{1,3},{2,0},{3,1},{4,6},{5,7},{6,4},{7,5},{8,10},{9,11},{10,... | collective-permute-start | bytes 21512 | tf_op jit(solution)/shard_map/ppermute | solution.py:20
  39.3 5.1 %collective-permute-start.6 = (bf16[32,4,4,128]{3,0,1,2:T(8,128)(2,1)S(1)}, bf16[32,4,4,128]{3,0,1,2:T(8,128)(2,1)S(1)}, u32[]{:S(2)}, u32[]{:S(2)}) collective-permute-start(bf16[32,4,4,128]{3,0,1,2:T(8,128)(2,1)S(1)} %fusion.30), channel_id=1, source_target_pairs={{0,1},{1,2},{2,3},{3,0},{4,5},{5,6},{6,7},{7,4},{8,9},{9,10},{10,1... | collective-permute-start | bytes 393224 | tf_op jit(solution)/shard_map/ppermute | solution.py:20
  39.4 6.4 %collective-permute-start.7 = (bf16[32,4,4,128]{3,0,1,2:T(8,128)(2,1)S(1)}, bf16[32,4,4,128]{3,0,1,2:T(8,128)(2,1)S(1)}, u32[]{:S(2)}, u32[]{:S(2)}) collective-permute-start(bf16[32,4,4,128]{3,0,1,2:T(8,128)(2,1)S(1)} %fusion.30), channel_id=1, source_target_pairs={{0,2},{1,3},{2,0},{3,1},{4,6},{5,7},{6,4},{7,5},{8,10},{9,11},{10,... | collective-permute-start | bytes 393224 | tf_op jit(solution)/shard_map/ppermute | solution.py:20
  42.1 4.6 %collective-permute-start.8 = (bf16[32,4,4,128]{3,0,1,2:T(8,128)(2,1)S(1)}, bf16[32,4,4,128]{3,0,1,2:T(8,128)(2,1)S(1)}, u32[]{:S(2)}, u32[]{:S(2)}) collective-permute-start(bf16[32,4,4,128]{3,0,1,2:T(8,128)(2,1)S(1)} %fusion.30), channel_id=1, source_target_pairs={{0,3},{1,0},{2,1},{3,2},{4,7},{5,4},{6,5},{7,6},{8,11},{9,8},{10,9... | collective-permute-start | bytes 393224 | tf_op jit(solution)/shard_map/ppermute | solution.py:20
  47.4 5.6 %collective-permute-start.9 = (bf16[32,16,512]{2,1,0:T(8,128)(2,1)S(1)}, bf16[32,16,512]{2,1,0:T(8,128)(2,1)S(1)}, u32[]{:S(2)}, u32[]{:S(2)}) collective-permute-start(bf16[32,16,512]{2,1,0:T(8,128)(2,1)S(1)} %reshape.334), channel_id=1, source_target_pairs={{0,4},{4,0},{1,5},{5,1},{2,6},{6,2},{3,7},{7,3},{8,12},{12,8},{9,1... | collective-permute-start | bytes 1572872 | tf_op jit(solution)/shard_map/ppermute | solution.py:15
  55.6 49.8 %all-to-all-start.1 = ((bf16[32,32,896]{2,1,0:T(8,128)(2,1)}), bf16[32,32,896]{2,1,0:T(8,128)(2,1)S(1)}, u32[]{:S(2)}, u32[]{:S(2)}) async-start(bf16[32,32,896]{2,1,0:T(8,128)(2,1)} %bitcast.136), calls=%async_computation.1 | async-start | bytes 3670016 | tf_op jit(solution)/shard_map/all_to_all | solution.py:97
  62.4 3.8 %collective-permute-start = (bf16[16,896]{1,0:T(8,128)(2,1)S(1)}, bf16[16,896]{1,0:T(8,128)(2,1)S(1)}, u32[]{:S(2)}, u32[]{:S(2)}) collective-permute-start(bf16[16,896]{1,0:T(8,128)(2,1)S(1)} %constant_dynamic-slice_fusion.1), channel_id=1, source_target_pairs={{0,4},{4,0},{1,5},{5,1},{2,6},{6,2},{3,7},{7,3},{8,12},{12,8},{9,1... | collective-permute-start | bytes 86024 | tf_op jit(solution)/shard_map/ppermute | solution.py:15
  63.2 1.2 collective-permute-start.11
  66.2 48.2 %collective-permute-start.13 = (bf16[1792,512]{1,0:T(8,128)(2,1)}, bf16[1792,512]{1,0:T(8,128)(2,1)}, u32[]{:S(2)}, u32[]{:S(2)}) collective-permute-start(bf16[1792,512]{1,0:T(8,128)(2,1)} %pad_maximum_fusion), channel_id=1, source_target_pairs={{0,1},{1,2},{2,3},{3,0},{4,5},{5,6},{6,7},{7,4},{8,9},{9,10},{10,1... | collective-permute-start | bytes 5505032 | tf_op jit(solution)/shard_map/ppermute | solution.py:20
  67.4 47.1 %collective-permute-start.14 = (bf16[1792,512]{1,0:T(8,128)(2,1)}, bf16[1792,512]{1,0:T(8,128)(2,1)}, u32[]{:S(2)}, u32[]{:S(2)}) collective-permute-start(bf16[1792,512]{1,0:T(8,128)(2,1)} %pad_maximum_fusion.1), channel_id=1, source_target_pairs={{0,3},{1,0},{2,1},{3,2},{4,7},{5,4},{6,5},{7,6},{8,11},{9,8},{10,9... | collective-permute-start | bytes 5505032 | tf_op jit(solution)/shard_map/ppermute | solution.py:20
  107.1 29.3 %all-to-all-start.2 = ((bf16[32,16,896]{2,1,0:T(8,128)(2,1)}), bf16[32,16,896]{2,1,0:T(8,128)(2,1)S(1)}, u32[]{:S(2)}, u32[]{:S(2)}) async-start(bf16[32,16,896]{2,1,0:T(8,128)(2,1)} %bitcast.35), calls=%async_computation.2 | async-start | bytes 1835008 | tf_op jit(solution)/shard_map/all_to_all | solution.py:97
  114.5 30.6 %collective-permute-start.15 = (bf16[256,1792]{1,0:T(8,128)(2,1)}, bf16[256,1792]{1,0:T(8,128)(2,1)}, u32[]{:S(2)}, u32[]{:S(2)}) collective-permute-start(bf16[256,1792]{1,0:T(8,128)(2,1)} %get-tuple-element.25), channel_id=1, source_target_pairs={{0,2},{1,3},{2,0},{3,1},{4,6},{5,7},{6,4},{7,5},{8,10},{9,11},{10,... | collective-permute-start | bytes 2752520 | tf_op jit(solution)/shard_map/ppermute | solution.py:20
  136.4 9.9 %collective-permute-start.16 = (bf16[256,896]{1,0:T(8,128)(2,1)S(1)}, bf16[256,896]{1,0:T(8,128)(2,1)S(1)}, u32[]{:S(2)}, u32[]{:S(2)}) collective-permute-start(bf16[256,896]{1,0:T(8,128)(2,1)S(1)} %get-tuple-element.49), channel_id=1, source_target_pairs={{0,4},{4,0},{1,5},{5,1},{2,6},{6,2},{3,7},{7,3},{8,12},{12,8},{9,1... | collective-permute-start | bytes 1376264 | tf_op jit(solution)/shard_map/ppermute | solution.py:15
  143.4 13.6 %collective-permute-start.20 = (bf16[256,896]{1,0:T(8,128)(2,1)S(1)}, bf16[256,896]{1,0:T(8,128)(2,1)S(1)}, u32[]{:S(2)}, u32[]{:S(2)}) collective-permute-start(bf16[256,896]{1,0:T(8,128)(2,1)S(1)} %get-tuple-element.49), channel_id=1, source_target_pairs={{0,2},{1,3},{2,0},{3,1},{4,6},{5,7},{6,4},{7,5},{8,10},{9,11},{10,... | collective-permute-start | bytes 1376264 | tf_op jit(solution)/shard_map/ppermute | solution.py:20
  145.1 21.8 %collective-permute-start.19 = (bf16[256,896]{1,0:T(8,128)(2,1)S(1)}, bf16[256,896]{1,0:T(8,128)(2,1)S(1)}, u32[]{:S(2)}, u32[]{:S(2)}) collective-permute-start(bf16[256,896]{1,0:T(8,128)(2,1)S(1)} %get-tuple-element.26), channel_id=1, source_target_pairs={{0,2},{1,3},{2,0},{3,1},{4,6},{5,7},{6,4},{7,5},{8,10},{9,11},{10,... | collective-permute-start | bytes 1376264 | tf_op jit(solution)/shard_map/ppermute | solution.py:20
  151.7 22.2 %collective-permute-start.17 = (bf16[256,640]{0,1:T(8,128)(2,1)S(1)}, bf16[256,640]{0,1:T(8,128)(2,1)S(1)}, u32[]{:S(2)}, u32[]{:S(2)}) collective-permute-start(bf16[256,640]{0,1:T(8,128)(2,1)S(1)} %get-tuple-element.57), channel_id=1, source_target_pairs={{0,3},{1,0},{2,1},{3,2},{4,7},{5,4},{6,5},{7,6},{8,11},{9,8},{10,9... | collective-permute-start | bytes 983048 | tf_op jit(solution)/shard_map/ppermute | solution.py:20
  154.2 20.0 %collective-permute-start.18 = (bf16[256,640]{0,1:T(8,128)(2,1)S(1)}, bf16[256,640]{0,1:T(8,128)(2,1)S(1)}, u32[]{:S(2)}, u32[]{:S(2)}) collective-permute-start(bf16[256,640]{0,1:T(8,128)(2,1)S(1)} %get-tuple-element.58), channel_id=1, source_target_pairs={{0,1},{1,2},{2,3},{3,0},{4,5},{5,6},{6,7},{7,4},{8,9},{9,10},{10,1... | collective-permute-start | bytes 983048 | tf_op jit(solution)/shard_map/ppermute | solution.py:20
  157.0 18.2 %collective-permute-start.21 = (bf16[256,896]{1,0:T(8,128)(2,1)S(1)}, bf16[256,896]{1,0:T(8,128)(2,1)S(1)}, u32[]{:S(2)}, u32[]{:S(2)}) collective-permute-start(bf16[256,896]{1,0:T(8,128)(2,1)S(1)} %collective-permute-done.20), channel_id=1, source_target_pairs={{0,4},{4,0},{1,5},{5,1},{2,6},{6,2},{3,7},{7,3},{8,12},{12,8},{9,1... | collective-permute-start | bytes 1376264 | tf_op jit(solution)/shard_map/ppermute | solution.py:15
  176.1 5.7 %collective-permute-start.22 = (bf16[256,256]{0,1:T(8,128)(2,1)S(1)}, bf16[256,256]{0,1:T(8,128)(2,1)S(1)}, u32[]{:S(2)}, u32[]{:S(2)}) collective-permute-start(bf16[256,256]{0,1:T(8,128)(2,1)S(1)} %fusion.55), channel_id=1, source_target_pairs={{0,1},{1,2},{2,3},{3,0},{4,5},{5,6},{6,7},{7,4},{8,9},{9,10},{10,1... | collective-permute-start | bytes 393224 | tf_op jit(solution)/shard_map/ppermute | solution.py:20
  177.3 4.5 %collective-permute-start.23 = (bf16[256,256]{0,1:T(8,128)(2,1)S(1)}, bf16[256,256]{0,1:T(8,128)(2,1)S(1)}, u32[]{:S(2)}, u32[]{:S(2)}) collective-permute-start(bf16[256,256]{0,1:T(8,128)(2,1)S(1)} %fusion.55), channel_id=1, source_target_pairs={{0,3},{1,0},{2,1},{3,2},{4,7},{5,4},{6,5},{7,6},{8,11},{9,8},{10,9... | collective-permute-start | bytes 393224 | tf_op jit(solution)/shard_map/ppermute | solution.py:20
  178.8 6.9 %collective-permute-start.24 = (bf16[256,256]{0,1:T(8,128)(2,1)S(1)}, bf16[256,256]{0,1:T(8,128)(2,1)S(1)}, u32[]{:S(2)}, u32[]{:S(2)}) collective-permute-start(bf16[256,256]{0,1:T(8,128)(2,1)S(1)} %fusion.55), channel_id=1, source_target_pairs={{0,2},{1,3},{2,0},{3,1},{4,6},{5,7},{6,4},{7,5},{8,10},{9,11},{10,... | collective-permute-start | bytes 393224 | tf_op jit(solution)/shard_map/ppermute | solution.py:20
  189.6 26.7 %all-to-all-start.3 = ((bf16[32,8,1792]{2,1,0:T(8,128)(2,1)}), bf16[32,8,1792]{2,1,0:T(8,128)(2,1)S(1)}, u32[]{:S(2)}, u32[]{:S(2)}) async-start(bf16[32,8,1792]{2,1,0:T(8,128)(2,1)} %fusion.11), calls=%async_computation.3 | async-start | bytes 1835008 | tf_op jit(solution)/shard_map/all_to_all | solution.py:97
  194.3 2.5 %collective-permute-start.12 = (bf16[16,8]{1,0:T(8,128)(2,1)S(1)}, bf16[16,8]{1,0:T(8,128)(2,1)S(1)}, u32[]{:S(2)}, u32[]{:S(2)}) collective-permute-start(bf16[16,8]{1,0:T(8,128)(2,1)S(1)} %bitcast.149), channel_id=1, source_target_pairs={{0,4},{4,0},{1,5},{5,1},{2,6},{6,2},{3,7},{7,3},{8,12},{12,8},{9,1... | collective-permute-start | bytes 776 | tf_op jit(solution)/shard_map/ppermute | solution.py:15
  197.0 1.3 collective-permute-start.10
  216.6 6.1 %collective-permute-start.25 = (f32[16,1792]{1,0:T(8,128)S(1)}, f32[16,1792]{1,0:T(8,128)S(1)}, u32[]{:S(2)}, u32[]{:S(2)}) collective-permute-start(f32[16,1792]{1,0:T(8,128)S(1)} %dynamic-slice_bitcast_fusion.14), channel_id=1, source_target_pairs={{0,4},{4,0},{1,5},{5,1},{2,6},{6,2},{3,7},{7,3},{8,12},{12,8},{9,1... | collective-permute-start | bytes 344072 | tf_op jit(solution)/shard_map/ppermute | solution.py:15
  (12 other events, 93.9 us)

commit v4 on v3

--- a/solution.py
+++ b/solution.py
@@ -186,26 +186,20 @@
     full_residual = full_residual.reshape(ny, own_tokens, cols)[back].reshape(group, cols)
 
     def share(part, gains):
-        return jnp.sum(jnp.square(part.astype(F32) / gains), axis=1, keepdims=True)
+        return jnp.sum(jnp.square(part.astype(F32) / gains), axis=1)
 
     own_share = share(tokens, norm_gain)
-    coarse = lax.reduce_precision(own_share, 8, 7)
-    lanes = jnp.arange(128)[None, :]
-    share_lanes = jnp.where(lanes == 0, coarse, jnp.where(lanes == 1, own_share - coarse, 0.0))
     squares = own_share
     sums = jnp.dot(tokens, up_block(y), preferred_element_type=F32)
     for d in near:
         part = jnp.dot(tokens, up_parts[d], preferred_element_type=F32)
-        part = jnp.concatenate([part.astype(BF16), share_lanes.astype(BF16)], axis=1)
-        part = send_y(part, -d).astype(F32)
-        sums = sums + part[:, : 2 * units]
-        squares = squares + part[:, 2 * units : 2 * units + 1]
-        squares = squares + part[:, 2 * units + 1 : 2 * units + 2]
+        sums = sums + send_y(part.astype(BF16), -d).astype(F32)
+        squares = squares + send_y(own_share, -d)
     for d in far:
         for part, which in zip(far_tokens[d], (core, 1 - core)):
             sums = sums + jnp.dot(part, half_block(y - d, which), preferred_element_type=F32)
             squares = squares + share(part, half_of(far_gain[d], which))
-    sums = sums * lax.rsqrt(squares / width + EPS)
+    sums = sums * lax.rsqrt(squares / width + EPS)[:, None]
     act = (jax.nn.silu(sums[:, :units]) * sums[:, units:]).astype(BF16)
     acts = jnp.concatenate([act] + [send_y(act, d) for d in near + far], axis=1)
     result = jnp.dot(acts, down_all, preferred_element_type=F32)

time: 224 us -> 223 us (level)
  starting transfers between devices: 72.9 us -> 80 us
  waiting for transfers between devices: 108 us -> 101 us
    all_to_all x4, waiting for transfers between devices: 77.3 us -> 73 us  [over_chips(): return lax.all_to_all(value, CHIPS, 0, 0, tiled=True)]
    ppermute x10, starting transfers between devices: 21.9 us -> 26.1 us  [swap(): return lax.ppermute(value, 'c', [(0, 1), (1, 0)])]
    ppermute x16 -> x18, starting transfers between devices: 22.9 us -> 25.8 us  [send_y(): lax.ppermute(value, 'y', [(i, (i + distance) % size) for i in range(size)])]
    ppermute x16 -> x18, waiting for transfers between devices: 27.5 us -> 24.7 us  [send_y(): lax.ppermute(value, 'y', [(i, (i + distance) % size) for i in range(size)])]
  transfers between devices with their start and end apart: 30 -> 32, of which waited for: 18 -> 18; matrix products, arithmetic and copies ran while one was open for 13% -> 12% of each run, Pallas kernels for 0% -> 0%
where the time goes in v4:
time: 223 us; the launch traced here: 222 us
  waiting for transfers between devices  101 us (45%)
  starting transfers between devices  80 us (36%)
  local copies, waits for them, and re-layouts  16.5 us (7%)
  matrix products  15.9 us (7%)
  other arithmetic  8.11 us (4%)
    all_to_all x4, waiting for transfers between devices, over_chips(): return lax.all_to_all(value, CHIPS, 0, 0, tiled=True)  73 us
    all_to_all x4, starting transfers between devices, over_chips(): return lax.all_to_all(value, CHIPS, 0, 0, tiled=True)  28 us
    ppermute x10, starting transfers between devices, swap(): return lax.ppermute(value, 'c', [(0, 1), (1, 0)])  26.1 us
    ppermute x18, starting transfers between devices, send_y(): lax.ppermute(value, 'y', [(i, (i + distance) % size) for i in range(size)])  25.8 us
    ppermute x18, waiting for transfers between devices, send_y(): lax.ppermute(value, 'y', [(i, (i + distance) % size) for i in range(size)])  24.7 us
  transfers between devices with their start and end apart: 32, of which 18 were waited for; matrix products, arithmetic and copies ran while one was open for 12% of the time, Pallas kernels for 0%

profile of v4, /device:TPU:1, one launch (start us, length us, event | category | flops | bytes accessed | tf_op | source)
XLA Modules:
  0.0 222.3 jit_solution(15439427043697628900)
XLA Ops:
  0.0 4.1 %dynamic-slice_bitcast_fusion = (bf16[256,1792]{1,0:T(8,128)(2,1)}, bf16[256,1792]{1,0:T(8,128)(2,1)}, bf16[256,1792]{1,0:T(8,128)(2,1)}, bf16[256,1792]{1,0:T(8,128)(2,1)}) fusion(bf16[1,256,7168]{2,1,0:T(8,128)(2,1)} %param.23, s32[]{:T(128)S(6)} %select_n.275, s32[]{:T(128)S(6)} %select_n.250, s32[]{:T(128)S(6)} %select_n.248, s32[]{:T(128)S(6)} %select_n.271), kind=kLoop, calls=%fused_computation.49 | loop fusion | bytes 7340048 | tf_op jit(solution)/shard_map/dynamic_slice | solution.py:100
  4.1 2.1 collective-permute-start.1
  8.6 2.8 %collective-permute-start.4 = (bf16[256,896]{1,0:T(8,128)(2,1)}, bf16[256,896]{1,0:T(8,128)(2,1)}, u32[]{:S(2)}, u32[]{:S(2)}) collective-permute-start(bf16[256,896]{1,0:T(8,128)(2,1)} %constant_dynamic-slice_fusion), channel_id=1, source_target_pairs={{0,4},{4,0},{1,5},{5,1},{2,6},{6,2},{3,7},{7,3},{8,12},{12,8},{9,1... | collective-permute-start | bytes 1376264 | tf_op jit(solution)/shard_map/ppermute | solution.py:15
  14.6 9.3 %all-to-all-start = ((bf16[32,4,4,512]{3,1,2,0:T(4,128)(2,1)}), bf16[32,4,4,512]{3,1,2,0:T(4,128)(2,1)S(1)}, u32[]{:S(2)}, u32[]{:S(2)}) async-start(bf16[32,4,4,512]{3,1,2,0:T(4,128)(2,1)} %bitcast.129), calls=%async_computation | async-start | bytes 1048576 | tf_op jit(solution)/shard_map/all_to_all | solution.py:97
  24.3 1.7 collective-permute-start.5
  26.0 3.8 %dynamic-slice_bitcast_fusion.1 = (bf16[1792,256]{1,0:T(8,128)(2,1)S(1)}, bf16[1792,256]{1,0:T(8,128)(2,1)S(1)}, bf16[1792,256]{1,0:T(8,128)(2,1)S(1)}, bf16[179...) fusion(bf16[1,7168,256]{2,1,0:T(8,128)(2,1)} %param.22, s32[]{:T(128)S(6)} %select_n.275, ...), kind=kLoop, calls=%fused_computation.52 | loop fusion | bytes 11010060 | tf_op jit(solution)/shard_map/dynamic_slice | solution.py:103
  35.1 3.7 %all-to-all-done = bf16[32,4,4,512]{3,1,2,0:T(4,128)(2,1)S(1)} async-done(((bf16[32,4,4,512]{3,1,2,0:T(4,128)(2,1)}), bf16[32,4,4,512]{3,1,2,0:T(4,128)(2,1)S(1)}, u32[]{:S(2)}, u32[]{:S(2)}) %all-to-all-start) | async-done | bytes 524320 | tf_op jit(solution)/shard_map/all_to_all | solution.py:97
  39.4 2.6 %collective-permute-start.7 = (bf16[32,4,4,128]{3,0,1,2:T(8,128)(2,1)S(1)}, bf16[32,4,4,128]{3,0,1,2:T(8,128)(2,1)S(1)}, u32[]{:S(2)}, u32[]{:S(2)}) collective-permute-start(bf16[32,4,4,128]{3,0,1,2:T(8,128)(2,1)S(1)} %fusion.30), channel_id=1, source_target_pairs={{0,2},{1,3},{2,0},{3,1},{4,6},{5,7},{6,4},{7,5},{8,10},{9,11},{10,... | collective-permute-start | bytes 393224 | tf_op jit(solution)/shard_map/ppermute | solution.py:20
  47.3 4.1 %collective-permute-start.9 = (bf16[32,16,512]{2,1,0:T(8,128)(2,1)S(1)}, bf16[32,16,512]{2,1,0:T(8,128)(2,1)S(1)}, u32[]{:S(2)}, u32[]{:S(2)}) collective-permute-start(bf16[32,16,512]{2,1,0:T(8,128)(2,1)S(1)} %reshape.317), channel_id=1, source_target_pairs={{0,4},{4,0},{1,5},{5,1},{2,6},{6,2},{3,7},{7,3},{8,12},{12,8},{9,1... | collective-permute-start | bytes 1572872 | tf_op jit(solution)/shard_map/ppermute | solution.py:15
  53.0 2.6 %convolution_convert_fusion = bf16[1024,896]{1,0:T(8,128)(2,1)} fusion(bf16[1024,512]{1,0:T(8,128)(2,1)S(1)} %bitcast.133, bf16[512,896]{1,0:T(8,128)(2,1)S(1)} %copy-done.2), kind=kOutput, calls=%fused_computation.20 | convolution fusion | flops 940441600 | bytes 3801088 | tf_op jit(solution)/shard_map/dot_general | solution.py:142
  55.6 6.7 %all-to-all-start.1 = ((bf16[32,32,896]{2,1,0:T(8,128)(2,1)}), bf16[32,32,896]{2,1,0:T(8,128)(2,1)S(1)}, u32[]{:S(2)}, u32[]{:S(2)}) async-start(bf16[32,32,896]{2,1,0:T(8,128)(2,1)} %bitcast.132), calls=%async_computation.1 | async-start | bytes 3670016 | tf_op jit(solution)/shard_map/all_to_all | solution.py:97
  69.8 35.6 %all-to-all-done.1 = bf16[32,32,896]{2,1,0:T(8,128)(2,1)S(1)} async-done(((bf16[32,32,896]{2,1,0:T(8,128)(2,1)}), bf16[32,32,896]{2,1,0:T(8,128)(2,1)S(1)}, u32[]{:S(2)}, u32[]{:S(2)}) %all-to-all-start.1) | async-done | bytes 1835040 | tf_op jit(solution)/shard_map/all_to_all | solution.py:97
  107.1 7.4 %all-to-all-start.2 = ((bf16[32,16,896]{2,1,0:T(8,128)(2,1)}), bf16[32,16,896]{2,1,0:T(8,128)(2,1)S(1)}, u32[]{:S(2)}, u32[]{:S(2)}) async-start(bf16[32,16,896]{2,1,0:T(8,128)(2,1)} %bitcast.35), calls=%async_computation.2 | async-start | bytes 1835008 | tf_op jit(solution)/shard_map/all_to_all | solution.py:97
  114.5 1.8 collective-permute-start.15
  116.3 20.1 %all-to-all-done.2 = bf16[32,16,896]{2,1,0:T(8,128)(2,1)S(1)} async-done(((bf16[32,16,896]{2,1,0:T(8,128)(2,1)}), bf16[32,16,896]{2,1,0:T(8,128)(2,1)S(1)}, u32[]{:S(2)}, u32[]{:S(2)}) %all-to-all-start.2) | async-done | bytes 917536 | tf_op jit(solution)/shard_map/all_to_all | solution.py:97
  136.4 5.3 %collective-permute-start.16 = (bf16[256,896]{1,0:T(8,128)(2,1)S(1)}, bf16[256,896]{1,0:T(8,128)(2,1)S(1)}, u32[]{:S(2)}, u32[]{:S(2)}) collective-permute-start(bf16[256,896]{1,0:T(8,128)(2,1)S(1)} %get-tuple-element.49), channel_id=1, source_target_pairs={{0,4},{4,0},{1,5},{5,1},{2,6},{6,2},{3,7},{7,3},{8,12},{12,8},{9,1... | collective-permute-start | bytes 1376264 | tf_op jit(solution)/shard_map/ppermute | solution.py:15
  143.4 1.7 collective-permute-start.20
  146.8 2.5 %collective-permute-start.22 = (f32[256]{0:T(256)S(1)}, f32[256]{0:T(256)S(1)}, u32[]{:S(2)}, u32[]{:S(2)}) collective-permute-start(f32[256]{0:T(256)S(1)} %multiply_reduce_fusion), channel_id=1, source_target_pairs={{0,3},{1,0},{2,1},{3,2},{4,7},{5,4},{6,5},{7,6},{8,11},{9,8},{10,9... | collective-permute-start | bytes 3080 | tf_op jit(solution)/shard_map/ppermute | solution.py:20
  149.2 2.1 convolution_convert_fusion.3
  151.4 2.8 %collective-permute-start.17 = (bf16[256,512]{1,0:T(8,128)(2,1)S(1)}, bf16[256,512]{1,0:T(8,128)(2,1)S(1)}, u32[]{:S(2)}, u32[]{:S(2)}) collective-permute-start(bf16[256,512]{1,0:T(8,128)(2,1)S(1)} %convolution_convert_fusion.3), channel_id=1, source_target_pairs={{0,3},{1,0},{2,1},{3,2},{4,7},{5,4},{6,5},{7,6},{8,11},{9,8},{10,9... | collective-permute-start | bytes 786440 | tf_op jit(solution)/shard_map/ppermute | solution.py:20
  154.2 2.1 convolution_convert_fusion.2
  156.3 10.5 %collective-permute-done.19 = bf16[256,896]{1,0:T(8,128)(2,1)S(1)} collective-permute-done((bf16[256,896]{1,0:T(8,128)(2,1)S(1)}, bf16[256,896]{1,0:T(8,128)(2,1)S(1)}, u32[]{:S(2)}, u32[]{:S(2)}) %collective-permute-start.19) | collective-permute-done | bytes 458784 | tf_op jit(solution)/shard_map/ppermute | solution.py:20
  170.2 2.3 %collective-permute-done.17 = bf16[256,512]{1,0:T(8,128)(2,1)S(1)} collective-permute-done((bf16[256,512]{1,0:T(8,128)(2,1)S(1)}, bf16[256,512]{1,0:T(8,128)(2,1)S(1)}, u32[]{:S(2)}, u32[]{:S(2)}) %collective-permute-start.17) | collective-permute-done | bytes 262176 | tf_op jit(solution)/shard_map/ppermute | solution.py:20
  172.5 2.5 %collective-permute-done.18 = bf16[256,512]{1,0:T(8,128)(2,1)S(1)} collective-permute-done((bf16[256,512]{1,0:T(8,128)(2,1)S(1)}, bf16[256,512]{1,0:T(8,128)(2,1)S(1)}, u32[]{:S(2)}, u32[]{:S(2)}) %collective-permute-start.18) | collective-permute-done | bytes 262176 | tf_op jit(solution)/shard_map/ppermute | solution.py:20
  176.5 2.7 %collective-permute-start.25 = (bf16[256,256]{1,0:T(8,128)(2,1)S(1)}, bf16[256,256]{1,0:T(8,128)(2,1)S(1)}, u32[]{:S(2)}, u32[]{:S(2)}) collective-permute-start(bf16[256,256]{1,0:T(8,128)(2,1)S(1)} %fusion.55), channel_id=1, source_target_pairs={{0,3},{1,0},{2,1},{3,2},{4,7},{5,4},{6,5},{7,6},{8,11},{9,8},{10,9... | collective-permute-start | bytes 393224 | tf_op jit(solution)/shard_map/ppermute | solution.py:20
  179.2 2.3 %collective-permute-done.24 = bf16[256,256]{1,0:T(8,128)(2,1)S(1)} collective-permute-done((bf16[256,256]{1,0:T(8,128)(2,1)S(1)}, bf16[256,256]{1,0:T(8,128)(2,1)S(1)}, u32[]{:S(2)}, u32[]{:S(2)}) %collective-permute-start.24) | collective-permute-done | bytes 131104 | tf_op jit(solution)/shard_map/ppermute | solution.py:20
  182.6 2.4 %collective-permute-done.26 = bf16[256,256]{1,0:T(8,128)(2,1)S(1)} collective-permute-done((bf16[256,256]{1,0:T(8,128)(2,1)S(1)}, bf16[256,256]{1,0:T(8,128)(2,1)S(1)}, u32[]{:S(2)}, u32[]{:S(2)}) %collective-permute-start.26) | collective-permute-done | bytes 131104 | tf_op jit(solution)/shard_map/ppermute | solution.py:20
  185.0 3.9 %fusion.11 = bf16[32,8,1792]{2,1,0:T(8,128)(2,1)} fusion(bf16[256,1792]{1,0:T(8,128)(2,1)} %collective-permute-done.15, bf16[256,1792]{1,0:T(8,128)(2,1)} %collective-permute-done.2, bf16[256,1792]{1,0:T(8,128)(2,1)} %collective-permute-done.1, bf16[256,1792]{1,0:T(8,128)(2,1)S(1)} %copy-done.4, bf16[256,256]{1,0:T(8,128)(2,1)S(1)} %collective-permute-done.26, ...), kind=kOutput, calls=%fused_computation.12 | convolution fusion | flops 956760064 | bytes 5111808 | tf_op jit(solution)/shard_map/dot_general | solution.py:205
  188.9 4.6 %all-to-all-start.3 = ((bf16[32,8,1792]{2,1,0:T(8,128)(2,1)}), bf16[32,8,1792]{2,1,0:T(8,128)(2,1)S(1)}, u32[]{:S(2)}, u32[]{:S(2)}) async-start(bf16[32,8,1792]{2,1,0:T(8,128)(2,1)} %fusion.11), calls=%async_computation.3 | async-start | bytes 1835008 | tf_op jit(solution)/shard_map/all_to_all | solution.py:97
  193.5 3.3 %collective-permute-start.12 = (bf16[16,8]{1,0:T(8,128)(2,1)S(1)}, bf16[16,8]{1,0:T(8,128)(2,1)S(1)}, u32[]{:S(2)}, u32[]{:S(2)}) collective-permute-start(bf16[16,8]{1,0:T(8,128)(2,1)S(1)} %bitcast.142), channel_id=1, source_target_pairs={{0,4},{4,0},{1,5},{5,1},{2,6},{6,2},{3,7},{7,3},{8,12},{12,8},{9,1... | collective-permute-start | bytes 776 | tf_op jit(solution)/shard_map/ppermute | solution.py:15
  199.4 13.6 %all-to-all-done.3 = bf16[32,8,1792]{2,1,0:T(8,128)(2,1)S(1)} async-done(((bf16[32,8,1792]{2,1,0:T(8,128)(2,1)}), bf16[32,8,1792]{2,1,0:T(8,128)(2,1)S(1)}, u32[]{:S(2)}, u32[]{:S(2)}) %all-to-all-start.3) | async-done | bytes 917536 | tf_op jit(solution)/shard_map/all_to_all | solution.py:97
  213.2 7.4 %collective-permute-start.27 = (f32[16,1792]{1,0:T(8,128)S(1)}, f32[16,1792]{1,0:T(8,128)S(1)}, u32[]{:S(2)}, u32[]{:S(2)}) collective-permute-start(f32[16,1792]{1,0:T(8,128)S(1)} %dynamic-slice_bitcast_fusion.14), channel_id=1, source_target_pairs={{0,4},{4,0},{1,5},{5,1},{2,6},{6,2},{3,7},{7,3},{8,12},{12,8},{9,1... | collective-permute-start | bytes 344072 | tf_op jit(solution)/shard_map/ppermute | solution.py:15
  (156 shorter events, 41.2 us)
Async XLA Ops:
  4.1 31.0 %collective-permute-start.1 = (bf16[256,1792]{1,0:T(8,128)(2,1)}, bf16[256,1792]{1,0:T(8,128)(2,1)}, u32[]{:S(2)}, u32[]{:S(2)}) collective-permute-start(bf16[256,1792]{1,0:T(8,128)(2,1)} %get-tuple-element.43), channel_id=1, source_target_pairs={{0,1},{1,2},{2,3},{3,0},{4,5},{5,6},{6,7},{7,4},{8,9},{9,10},{10,1... | collective-permute-start | bytes 2752520 | tf_op jit(solution)/shard_map/ppermute | solution.py:20
  6.2 28.9 %collective-permute-start.2 = (bf16[256,1792]{1,0:T(8,128)(2,1)}, bf16[256,1792]{1,0:T(8,128)(2,1)}, u32[]{:S(2)}, u32[]{:S(2)}) collective-permute-start(bf16[256,1792]{1,0:T(8,128)(2,1)} %get-tuple-element.42), channel_id=1, source_target_pairs={{0,3},{1,0},{2,1},{3,2},{4,7},{5,4},{6,5},{7,6},{8,11},{9,8},{10,9... | collective-permute-start | bytes 2752520 | tf_op jit(solution)/shard_map/ppermute | solution.py:20
  8.6 24.2 %collective-permute-start.4 = (bf16[256,896]{1,0:T(8,128)(2,1)}, bf16[256,896]{1,0:T(8,128)(2,1)}, u32[]{:S(2)}, u32[]{:S(2)}) collective-permute-start(bf16[256,896]{1,0:T(8,128)(2,1)} %constant_dynamic-slice_fusion), channel_id=1, source_target_pairs={{0,4},{4,0},{1,5},{5,1},{2,6},{6,2},{3,7},{7,3},{8,12},{12,8},{9,1... | collective-permute-start | bytes 1376264 | tf_op jit(solution)/shard_map/ppermute | solution.py:15
  14.6 24.2 %all-to-all-start = ((bf16[32,4,4,512]{3,1,2,0:T(4,128)(2,1)}), bf16[32,4,4,512]{3,1,2,0:T(4,128)(2,1)S(1)}, u32[]{:S(2)}, u32[]{:S(2)}) async-start(bf16[32,4,4,512]{3,1,2,0:T(4,128)(2,1)} %bitcast.129), calls=%async_computation | async-start | bytes 1048576 | tf_op jit(solution)/shard_map/all_to_all | solution.py:97
  23.9 8.7 %collective-permute-start.3 = (bf16[2,512,128]{2,1,0:T(8,128)(2,1)S(1)}, bf16[2,512,128]{2,1,0:T(8,128)(2,1)S(1)}, u32[]{:S(2)}, u32[]{:S(2)}) collective-permute-start(bf16[2,512,128]{2,1,0:T(8,128)(2,1)S(1)} %copy-done.6), channel_id=1, source_target_pairs={{0,4},{4,0},{1,5},{5,1},{2,6},{6,2},{3,7},{7,3},{8,12},{12,8},{9,1... | collective-permute-start | bytes 786440 | tf_op jit(solution)/shard_map/ppermute | solution.py:15
  24.3 10.8 %collective-permute-start.5 = (f32[1792]{0:T(1024)S(1)}, f32[1792]{0:T(1024)S(1)}, u32[]{:S(2)}, u32[]{:S(2)}) collective-permute-start(f32[1792]{0:T(1024)S(1)} %copy-done.8), channel_id=1, source_target_pairs={{0,2},{1,3},{2,0},{3,1},{4,6},{5,7},{6,4},{7,5},{8,10},{9,11},{10,... | collective-permute-start | bytes 21512 | tf_op jit(solution)/shard_map/ppermute | solution.py:20
  39.3 5.1 %collective-permute-start.6 = (bf16[32,4,4,128]{3,0,1,2:T(8,128)(2,1)S(1)}, bf16[32,4,4,128]{3,0,1,2:T(8,128)(2,1)S(1)}, u32[]{:S(2)}, u32[]{:S(2)}) collective-permute-start(bf16[32,4,4,128]{3,0,1,2:T(8,128)(2,1)S(1)} %fusion.30), channel_id=1, source_target_pairs={{0,1},{1,2},{2,3},{3,0},{4,5},{5,6},{6,7},{7,4},{8,9},{9,10},{10,1... | collective-permute-start | bytes 393224 | tf_op jit(solution)/shard_map/ppermute | solution.py:20
  39.4 6.4 %collective-permute-start.7 = (bf16[32,4,4,128]{3,0,1,2:T(8,128)(2,1)S(1)}, bf16[32,4,4,128]{3,0,1,2:T(8,128)(2,1)S(1)}, u32[]{:S(2)}, u32[]{:S(2)}) collective-permute-start(bf16[32,4,4,128]{3,0,1,2:T(8,128)(2,1)S(1)} %fusion.30), channel_id=1, source_target_pairs={{0,2},{1,3},{2,0},{3,1},{4,6},{5,7},{6,4},{7,5},{8,10},{9,11},{10,... | collective-permute-start | bytes 393224 | tf_op jit(solution)/shard_map/ppermute | solution.py:20
  42.0 4.6 %collective-permute-start.8 = (bf16[32,4,4,128]{3,0,1,2:T(8,128)(2,1)S(1)}, bf16[32,4,4,128]{3,0,1,2:T(8,128)(2,1)S(1)}, u32[]{:S(2)}, u32[]{:S(2)}) collective-permute-start(bf16[32,4,4,128]{3,0,1,2:T(8,128)(2,1)S(1)} %fusion.30), channel_id=1, source_target_pairs={{0,3},{1,0},{2,1},{3,2},{4,7},{5,4},{6,5},{7,6},{8,11},{9,8},{10,9... | collective-permute-start | bytes 393224 | tf_op jit(solution)/shard_map/ppermute | solution.py:20
  47.3 5.6 %collective-permute-start.9 = (bf16[32,16,512]{2,1,0:T(8,128)(2,1)S(1)}, bf16[32,16,512]{2,1,0:T(8,128)(2,1)S(1)}, u32[]{:S(2)}, u32[]{:S(2)}) collective-permute-start(bf16[32,16,512]{2,1,0:T(8,128)(2,1)S(1)} %reshape.317), channel_id=1, source_target_pairs={{0,4},{4,0},{1,5},{5,1},{2,6},{6,2},{3,7},{7,3},{8,12},{12,8},{9,1... | collective-permute-start | bytes 1572872 | tf_op jit(solution)/shard_map/ppermute | solution.py:15
  55.6 49.8 %all-to-all-start.1 = ((bf16[32,32,896]{2,1,0:T(8,128)(2,1)}), bf16[32,32,896]{2,1,0:T(8,128)(2,1)S(1)}, u32[]{:S(2)}, u32[]{:S(2)}) async-start(bf16[32,32,896]{2,1,0:T(8,128)(2,1)} %bitcast.132), calls=%async_computation.1 | async-start | bytes 3670016 | tf_op jit(solution)/shard_map/all_to_all | solution.py:97
  62.4 3.8 %collective-permute-start = (bf16[16,896]{1,0:T(8,128)(2,1)S(1)}, bf16[16,896]{1,0:T(8,128)(2,1)S(1)}, u32[]{:S(2)}, u32[]{:S(2)}) collective-permute-start(bf16[16,896]{1,0:T(8,128)(2,1)S(1)} %constant_dynamic-slice_fusion.1), channel_id=1, source_target_pairs={{0,4},{4,0},{1,5},{5,1},{2,6},{6,2},{3,7},{7,3},{8,12},{12,8},{9,1... | collective-permute-start | bytes 86024 | tf_op jit(solution)/shard_map/ppermute | solution.py:15
  63.2 1.2 collective-permute-start.11
  66.2 48.2 %collective-permute-start.13 = (bf16[1792,512]{1,0:T(8,128)(2,1)}, bf16[1792,512]{1,0:T(8,128)(2,1)}, u32[]{:S(2)}, u32[]{:S(2)}) collective-permute-start(bf16[1792,512]{1,0:T(8,128)(2,1)} %pad_maximum_fusion), channel_id=1, source_target_pairs={{0,1},{1,2},{2,3},{3,0},{4,5},{5,6},{6,7},{7,4},{8,9},{9,10},{10,1... | collective-permute-start | bytes 5505032 | tf_op jit(solution)/shard_map/ppermute | solution.py:20
  67.4 47.1 %collective-permute-start.14 = (bf16[1792,512]{1,0:T(8,128)(2,1)}, bf16[1792,512]{1,0:T(8,128)(2,1)}, u32[]{:S(2)}, u32[]{:S(2)}) collective-permute-start(bf16[1792,512]{1,0:T(8,128)(2,1)} %pad_maximum_fusion.1), channel_id=1, source_target_pairs={{0,3},{1,0},{2,1},{3,2},{4,7},{5,4},{6,5},{7,6},{8,11},{9,8},{10,9... | collective-permute-start | bytes 5505032 | tf_op jit(solution)/shard_map/ppermute | solution.py:20
  107.1 29.3 %all-to-all-start.2 = ((bf16[32,16,896]{2,1,0:T(8,128)(2,1)}), bf16[32,16,896]{2,1,0:T(8,128)(2,1)S(1)}, u32[]{:S(2)}, u32[]{:S(2)}) async-start(bf16[32,16,896]{2,1,0:T(8,128)(2,1)} %bitcast.35), calls=%async_computation.2 | async-start | bytes 1835008 | tf_op jit(solution)/shard_map/all_to_all | solution.py:97
  114.5 30.6 %collective-permute-start.15 = (bf16[256,1792]{1,0:T(8,128)(2,1)}, bf16[256,1792]{1,0:T(8,128)(2,1)}, u32[]{:S(2)}, u32[]{:S(2)}) collective-permute-start(bf16[256,1792]{1,0:T(8,128)(2,1)} %get-tuple-element.25), channel_id=1, source_target_pairs={{0,2},{1,3},{2,0},{3,1},{4,6},{5,7},{6,4},{7,5},{8,10},{9,11},{10,... | collective-permute-start | bytes 2752520 | tf_op jit(solution)/shard_map/ppermute | solution.py:20
  136.4 9.9 %collective-permute-start.16 = (bf16[256,896]{1,0:T(8,128)(2,1)S(1)}, bf16[256,896]{1,0:T(8,128)(2,1)S(1)}, u32[]{:S(2)}, u32[]{:S(2)}) collective-permute-start(bf16[256,896]{1,0:T(8,128)(2,1)S(1)} %get-tuple-element.49), channel_id=1, source_target_pairs={{0,4},{4,0},{1,5},{5,1},{2,6},{6,2},{3,7},{7,3},{8,12},{12,8},{9,1... | collective-permute-start | bytes 1376264 | tf_op jit(solution)/shard_map/ppermute | solution.py:15
  143.4 24.6 %collective-permute-start.20 = (bf16[256,896]{1,0:T(8,128)(2,1)S(1)}, bf16[256,896]{1,0:T(8,128)(2,1)S(1)}, u32[]{:S(2)}, u32[]{:S(2)}) collective-permute-start(bf16[256,896]{1,0:T(8,128)(2,1)S(1)} %get-tuple-element.49), channel_id=1, source_target_pairs={{0,2},{1,3},{2,0},{3,1},{4,6},{5,7},{6,4},{7,5},{8,10},{9,11},{10,... | collective-permute-start | bytes 1376264 | tf_op jit(solution)/shard_map/ppermute | solution.py:20
  145.1 21.7 %collective-permute-start.19 = (bf16[256,896]{1,0:T(8,128)(2,1)S(1)}, bf16[256,896]{1,0:T(8,128)(2,1)S(1)}, u32[]{:S(2)}, u32[]{:S(2)}) collective-permute-start(bf16[256,896]{1,0:T(8,128)(2,1)S(1)} %get-tuple-element.26), channel_id=1, source_target_pairs={{0,2},{1,3},{2,0},{3,1},{4,6},{5,7},{6,4},{7,5},{8,10},{9,11},{10,... | collective-permute-start | bytes 1376264 | tf_op jit(solution)/shard_map/ppermute | solution.py:20
  146.8 29.1 %collective-permute-start.22 = (f32[256]{0:T(256)S(1)}, f32[256]{0:T(256)S(1)}, u32[]{:S(2)}, u32[]{:S(2)}) collective-permute-start(f32[256]{0:T(256)S(1)} %multiply_reduce_fusion), channel_id=1, source_target_pairs={{0,3},{1,0},{2,1},{3,2},{4,7},{5,4},{6,5},{7,6},{8,11},{9,8},{10,9... | collective-permute-start | bytes 3080 | tf_op jit(solution)/shard_map/ppermute | solution.py:20
  149.2 26.6 %collective-permute-start.23 = (f32[256]{0:T(256)S(1)}, f32[256]{0:T(256)S(1)}, u32[]{:S(2)}, u32[]{:S(2)}) collective-permute-start(f32[256]{0:T(256)S(1)} %multiply_reduce_fusion), channel_id=1, source_target_pairs={{0,1},{1,2},{2,3},{3,0},{4,5},{5,6},{6,7},{7,4},{8,9},{9,10},{10,1... | collective-permute-start | bytes 3080 | tf_op jit(solution)/shard_map/ppermute | solution.py:20
  151.4 21.1 %collective-permute-start.17 = (bf16[256,512]{1,0:T(8,128)(2,1)S(1)}, bf16[256,512]{1,0:T(8,128)(2,1)S(1)}, u32[]{:S(2)}, u32[]{:S(2)}) collective-permute-start(bf16[256,512]{1,0:T(8,128)(2,1)S(1)} %convolution_convert_fusion.3), channel_id=1, source_target_pairs={{0,3},{1,0},{2,1},{3,2},{4,7},{5,4},{6,5},{7,6},{8,11},{9,8},{10,9... | collective-permute-start | bytes 786440 | tf_op jit(solution)/shard_map/ppermute | solution.py:20
  166.8 8.2 %collective-permute-start.18 = (bf16[256,512]{1,0:T(8,128)(2,1)S(1)}, bf16[256,512]{1,0:T(8,128)(2,1)S(1)}, u32[]{:S(2)}, u32[]{:S(2)}) collective-permute-start(bf16[256,512]{1,0:T(8,128)(2,1)S(1)} %convolution_convert_fusion.2), channel_id=1, source_target_pairs={{0,1},{1,2},{2,3},{3,0},{4,5},{5,6},{6,7},{7,4},{8,9},{9,10},{10,1... | collective-permute-start | bytes 786440 | tf_op jit(solution)/shard_map/ppermute | solution.py:20
  168.0 7.7 %collective-permute-start.21 = (bf16[256,896]{1,0:T(8,128)(2,1)S(1)}, bf16[256,896]{1,0:T(8,128)(2,1)S(1)}, u32[]{:S(2)}, u32[]{:S(2)}) collective-permute-start(bf16[256,896]{1,0:T(8,128)(2,1)S(1)} %collective-permute-done.20), channel_id=1, source_target_pairs={{0,4},{4,0},{1,5},{5,1},{2,6},{6,2},{3,7},{7,3},{8,12},{12,8},{9,1... | collective-permute-start | bytes 1376264 | tf_op jit(solution)/shard_map/ppermute | solution.py:15
  176.5 5.1 %collective-permute-start.24 = (bf16[256,256]{1,0:T(8,128)(2,1)S(1)}, bf16[256,256]{1,0:T(8,128)(2,1)S(1)}, u32[]{:S(2)}, u32[]{:S(2)}) collective-permute-start(bf16[256,256]{1,0:T(8,128)(2,1)S(1)} %fusion.55), channel_id=1, source_target_pairs={{0,1},{1,2},{2,3},{3,0},{4,5},{5,6},{6,7},{7,4},{8,9},{9,10},{10,1... | collective-permute-start | bytes 393224 | tf_op jit(solution)/shard_map/ppermute | solution.py:20
  176.5 6.1 %collective-permute-start.25 = (bf16[256,256]{1,0:T(8,128)(2,1)S(1)}, bf16[256,256]{1,0:T(8,128)(2,1)S(1)}, u32[]{:S(2)}, u32[]{:S(2)}) collective-permute-start(bf16[256,256]{1,0:T(8,128)(2,1)S(1)} %fusion.55), channel_id=1, source_target_pairs={{0,3},{1,0},{2,1},{3,2},{4,7},{5,4},{6,5},{7,6},{8,11},{9,8},{10,9... | collective-permute-start | bytes 393224 | tf_op jit(solution)/shard_map/ppermute | solution.py:20
  179.2 5.8 %collective-permute-start.26 = (bf16[256,256]{1,0:T(8,128)(2,1)S(1)}, bf16[256,256]{1,0:T(8,128)(2,1)S(1)}, u32[]{:S(2)}, u32[]{:S(2)}) collective-permute-start(bf16[256,256]{1,0:T(8,128)(2,1)S(1)} %fusion.55), channel_id=1, source_target_pairs={{0,2},{1,3},{2,0},{3,1},{4,6},{5,7},{6,4},{7,5},{8,10},{9,11},{10,... | collective-permute-start | bytes 393224 | tf_op jit(solution)/shard_map/ppermute | solution.py:20
  188.9 24.0 %all-to-all-start.3 = ((bf16[32,8,1792]{2,1,0:T(8,128)(2,1)}), bf16[32,8,1792]{2,1,0:T(8,128)(2,1)S(1)}, u32[]{:S(2)}, u32[]{:S(2)}) async-start(bf16[32,8,1792]{2,1,0:T(8,128)(2,1)} %fusion.11), calls=%async_computation.3 | async-start | bytes 1835008 | tf_op jit(solution)/shard_map/all_to_all | solution.py:97
  193.5 4.2 %collective-permute-start.12 = (bf16[16,8]{1,0:T(8,128)(2,1)S(1)}, bf16[16,8]{1,0:T(8,128)(2,1)S(1)}, u32[]{:S(2)}, u32[]{:S(2)}) collective-permute-start(bf16[16,8]{1,0:T(8,128)(2,1)S(1)} %bitcast.142), channel_id=1, source_target_pairs={{0,4},{4,0},{1,5},{5,1},{2,6},{6,2},{3,7},{7,3},{8,12},{12,8},{9,1... | collective-permute-start | bytes 776 | tf_op jit(solution)/shard_map/ppermute | solution.py:15
  198.0 1.3 collective-permute-start.10
  213.2 8.4 %collective-permute-start.27 = (f32[16,1792]{1,0:T(8,128)S(1)}, f32[16,1792]{1,0:T(8,128)S(1)}, u32[]{:S(2)}, u32[]{:S(2)}) collective-permute-start(f32[16,1792]{1,0:T(8,128)S(1)} %dynamic-slice_bitcast_fusion.14), channel_id=1, source_target_pairs={{0,4},{4,0},{1,5},{5,1},{2,6},{6,2},{3,7},{7,3},{8,12},{12,8},{9,1... | collective-permute-start | bytes 344072 | tf_op jit(solution)/shard_map/ppermute | solution.py:15
  (14 other events, 127.0 us)

commit v5 on v4

--- a/solution.py
+++ b/solution.py
@@ -172,10 +172,14 @@
     ).astype(BF16)
     tokens = over_chips(outgoing.reshape(chips, NC * NC * CAP, half))
     tokens = tokens.reshape(chips, NC, NC * CAP, half)
-    kept, given = tokens[:, 0].reshape(slots, half), tokens[:, 1].reshape(slots, half)
-    received = swap(given)
-    kept, far_down = lax.optimization_barrier((kept, far_down))
-    far_tokens = {d: (send_y(kept, d), swap(send_y(given, d))) for d in far}
+    tokens, far_down = lax.optimization_barrier((tokens, far_down))
+    far_arrived = {d: send_y(tokens, d) for d in far}
+
+    def split(value):
+        return value[:, 0].reshape(slots, half), swap(value[:, 1].reshape(slots, half))
+
+    kept, received = split(tokens)
+    far_tokens = {d: split(far_arrived[d]) for d in far}
     down_all = [down_block(y)] + [near_down[d] for d in near] + [far_down[d] for d in far]
     down_all = jnp.concatenate(down_all, axis=0)
     tokens = in_core_order(core, kept, received, axis=1)

time: 223 us -> 226 us (1.013)
  starting transfers between devices: 80 us -> 75.3 us
  matrix products: 15.9 us -> 19.8 us
    ppermute x18 -> x17, waiting for transfers between devices: 24.7 us -> 41.8 us  [send_y(): lax.ppermute(value, 'y', [(i, (i + distance) % size) for i in range(size)])]
    all_to_all x4, waiting for transfers between devices: 73 us -> 56.6 us  [over_chips(): return lax.all_to_all(value, CHIPS, 0, 0, tiled=True)]
    ppermute x10, starting transfers between devices: 26.1 us -> 21.5 us  [swap(): return lax.ppermute(value, 'c', [(0, 1), (1, 0)])]
    ppermute x18 -> x17, starting transfers between devices: 25.8 us -> 23.7 us  [send_y(): lax.ppermute(value, 'y', [(i, (i + distance) % size) for i in range(size)])]
  transfers between devices with their start and end apart: 32 -> 31, of which waited for: 18 -> 17; matrix products, arithmetic and copies ran while one was open for 12% -> 15% of each run, Pallas kernels for 0% -> 0%
where the time goes in v5:
time: 226 us; the launch traced here: 225 us
  waiting for transfers between devices  102 us (45%)
  starting transfers between devices  75.3 us (33%)
  matrix products  19.8 us (9%)
  local copies, waits for them, and re-layouts  18.4 us (8%)
  other arithmetic  9.23 us (4%)
    all_to_all x4, waiting for transfers between devices, over_chips(): return lax.all_to_all(value, CHIPS, 0, 0, tiled=True)  56.6 us
    ppermute x17, waiting for transfers between devices, send_y(): lax.ppermute(value, 'y', [(i, (i + distance) % size) for i in range(size)])  41.8 us
    all_to_all x4, starting transfers between devices, over_chips(): return lax.all_to_all(value, CHIPS, 0, 0, tiled=True)  30.1 us
    ppermute x17, starting transfers between devices, send_y(): lax.ppermute(value, 'y', [(i, (i + distance) % size) for i in range(size)])  23.7 us
    ppermute x10, starting transfers between devices, swap(): return lax.ppermute(value, 'c', [(0, 1), (1, 0)])  21.5 us
    dot_general x2, matrix products, on_device(): part = jnp.dot(tokens, up_parts[d], preferred_element_type=F32)  5.68 us
  transfers between devices with their start and end apart: 31, of which 17 were waited for; matrix products, arithmetic and copies ran while one was open for 15% of the time, Pallas kernels for 0%

profile of v5, /device:TPU:1, one launch (start us, length us, event | category | flops | bytes accessed | tf_op | source)
XLA Modules:
  0.0 225.3 jit_solution(10624390182799990887)
XLA Ops:
  0.0 4.0 %dynamic-slice_bitcast_fusion = (bf16[256,1792]{1,0:T(8,128)(2,1)}, bf16[256,1792]{1,0:T(8,128)(2,1)}, bf16[256,1792]{1,0:T(8,128)(2,1)}, bf16[256,1792]{1,0:T(8,128)(2,1)}) fusion(bf16[1,256,7168]{2,1,0:T(8,128)(2,1)} %param.23, s32[]{:T(128)S(6)} %select_n.275, s32[]{:T(128)S(6)} %select_n.250, s32[]{:T(128)S(6)} %select_n.248, s32[]{:T(128)S(6)} %select_n.271), kind=kLoop, calls=%fused_computation.50 | loop fusion | bytes 7340048 | tf_op jit(solution)/shard_map/dynamic_slice | solution.py:100
  4.1 2.1 collective-permute-start.1
  8.5 2.8 %collective-permute-start.4 = (bf16[256,896]{1,0:T(8,128)(2,1)}, bf16[256,896]{1,0:T(8,128)(2,1)}, u32[]{:S(2)}, u32[]{:S(2)}) collective-permute-start(bf16[256,896]{1,0:T(8,128)(2,1)} %constant_dynamic-slice_fusion), channel_id=1, source_target_pairs={{0,4},{4,0},{1,5},{5,1},{2,6},{6,2},{3,7},{7,3},{8,12},{12,8},{9,1... | collective-permute-start | bytes 1376264 | tf_op jit(solution)/shard_map/ppermute | solution.py:15
  14.6 9.3 %all-to-all-start = ((bf16[32,4,4,512]{3,1,2,0:T(4,128)(2,1)}), bf16[32,4,4,512]{3,1,2,0:T(4,128)(2,1)S(1)}, u32[]{:S(2)}, u32[]{:S(2)}) async-start(bf16[32,4,4,512]{3,1,2,0:T(4,128)(2,1)} %bitcast.133), calls=%async_computation | async-start | bytes 1048576 | tf_op jit(solution)/shard_map/all_to_all | solution.py:97
  24.3 1.7 collective-permute-start.5
  26.0 3.9 %dynamic-slice_bitcast_fusion.1 = (bf16[1792,256]{1,0:T(8,128)(2,1)S(1)}, bf16[1792,256]{1,0:T(8,128)(2,1)S(1)}, bf16[1792,256]{1,0:T(8,128)(2,1)S(1)}, bf16[179...) fusion(bf16[1,7168,256]{2,1,0:T(8,128)(2,1)} %param.22, s32[]{:T(128)S(6)} %select_n.275, ...), kind=kLoop, calls=%fused_computation.53 | loop fusion | bytes 11010060 | tf_op jit(solution)/shard_map/dynamic_slice | solution.py:103
  35.1 3.6 %all-to-all-done = bf16[32,4,4,512]{3,1,2,0:T(4,128)(2,1)S(1)} async-done(((bf16[32,4,4,512]{3,1,2,0:T(4,128)(2,1)}), bf16[32,4,4,512]{3,1,2,0:T(4,128)(2,1)S(1)}, u32[]{:S(2)}, u32[]{:S(2)}) %all-to-all-start) | async-done | bytes 524320 | tf_op jit(solution)/shard_map/all_to_all | solution.py:97
  39.4 2.6 %collective-permute-start.7 = (bf16[32,4,4,128]{3,0,1,2:T(8,128)(2,1)S(1)}, bf16[32,4,4,128]{3,0,1,2:T(8,128)(2,1)S(1)}, u32[]{:S(2)}, u32[]{:S(2)}) collective-permute-start(bf16[32,4,4,128]{3,0,1,2:T(8,128)(2,1)S(1)} %fusion.35), channel_id=1, source_target_pairs={{0,2},{1,3},{2,0},{3,1},{4,6},{5,7},{6,4},{7,5},{8,10},{9,11},{10,... | collective-permute-start | bytes 393224 | tf_op jit(solution)/shard_map/ppermute | solution.py:20
  47.3 4.1 %collective-permute-start.9 = (bf16[32,16,512]{2,1,0:T(8,128)(2,1)S(1)}, bf16[32,16,512]{2,1,0:T(8,128)(2,1)S(1)}, u32[]{:S(2)}, u32[]{:S(2)}) collective-permute-start(bf16[32,16,512]{2,1,0:T(8,128)(2,1)S(1)} %reshape.325), channel_id=1, source_target_pairs={{0,4},{4,0},{1,5},{5,1},{2,6},{6,2},{3,7},{7,3},{8,12},{12,8},{9,1... | collective-permute-start | bytes 1572872 | tf_op jit(solution)/shard_map/ppermute | solution.py:15
  53.0 2.6 %convolution_convert_fusion = bf16[1024,896]{1,0:T(8,128)(2,1)} fusion(bf16[1024,512]{1,0:T(8,128)(2,1)S(1)} %bitcast.139, bf16[512,896]{1,0:T(8,128)(2,1)S(1)} %copy-done.2), kind=kOutput, calls=%fused_computation.20 | convolution fusion | flops 940441600 | bytes 3801088 | tf_op jit(solution)/shard_map/dot_general | solution.py:142
  55.6 6.7 %all-to-all-start.1 = ((bf16[32,32,896]{2,1,0:T(8,128)(2,1)}), bf16[32,32,896]{2,1,0:T(8,128)(2,1)S(1)}, u32[]{:S(2)}, u32[]{:S(2)}) async-start(bf16[32,32,896]{2,1,0:T(8,128)(2,1)} %bitcast.138), calls=%async_computation.1 | async-start | bytes 3670016 | tf_op jit(solution)/shard_map/all_to_all | solution.py:97
  70.2 35.1 %all-to-all-done.1 = bf16[32,32,896]{2,1,0:T(8,128)(2,1)S(1)} async-done(((bf16[32,32,896]{2,1,0:T(8,128)(2,1)}), bf16[32,32,896]{2,1,0:T(8,128)(2,1)S(1)}, u32[]{:S(2)}, u32[]{:S(2)}) %all-to-all-start.1) | async-done | bytes 1835040 | tf_op jit(solution)/shard_map/all_to_all | solution.py:97
  107.0 7.4 %all-to-all-start.2 = ((bf16[32,16,896]{2,1,0:T(8,128)(2,1)}), bf16[32,16,896]{2,1,0:T(8,128)(2,1)S(1)}, u32[]{:S(2)}, u32[]{:S(2)}) async-start(bf16[32,16,896]{2,1,0:T(8,128)(2,1)} %bitcast.35), calls=%async_computation.2 | async-start | bytes 1835008 | tf_op jit(solution)/shard_map/all_to_all | solution.py:97
  114.4 1.8 collective-permute-start.15
  116.2 20.6 %collective-permute-done.15 = bf16[256,1792]{1,0:T(8,128)(2,1)} collective-permute-done((bf16[256,1792]{1,0:T(8,128)(2,1)S(1)}, bf16[256,1792]{1,0:T(8,128)(2,1)}, u32[]{:S(2)}, u32[]{:S(2)}) %collective-permute-start.15) | collective-permute-done | bytes 917536 | tf_op jit(solution)/shard_map/ppermute | solution.py:20
  136.9 4.7 %collective-permute-start.16 = (bf16[256,896]{1,0:T(8,128)(2,1)S(1)}, bf16[256,896]{1,0:T(8,128)(2,1)}, u32[]{:S(2)}, u32[]{:S(2)}) collective-permute-start(bf16[256,896]{1,0:T(8,128)(2,1)S(1)} %slice_bitcast_fusion.1), channel_id=1, source_target_pairs={{0,4},{4,0},{1,5},{5,1},{2,6},{6,2},{3,7},{7,3},{8,12},{12,8},{9,1... | collective-permute-start | bytes 1376264 | tf_op jit(solution)/shard_map/ppermute | solution.py:15
  141.6 2.8 %dynamic-slice_bitcast_fusion.12 = (bf16[896,256]{1,0:T(8,128)(2,1)}, bf16[896,256]{1,0:T(8,128)(2,1)}, bf16[896,256]{1,0:T(8,128)(2,1)}, bf16[896,256]{1,0:T(8,128)(2,1)}) fusion(bf16[1,7168,256]{2,1,0:T(8,128)(2,1)} %param.22, s32[]{:T(128)S(6)} %select_n.277, s32[]{:T(128)S(6)} %select_n.278, bf16[1,7168,256]{2,1,0:T(8,128)(2,1)} %param.21), kind=kLoop, calls=%fused_computation.91 | loop fusion | bytes 3670024 | tf_op jit(solution)/shard_map/dynamic_slice | solution.py:111
  144.5 1.7 collective-permute-start.19
  147.7 1.9 collective-permute-start.21
  149.6 2.8 %convolution_convert_fusion.3 = bf16[256,512]{1,0:T(8,128)(2,1)} fusion(bf16[1792,512]{1,0:T(8,128)(2,1)} %collective-permute-done.13, bf16[256,896]{1,0:T(8,128)(2,1)S(1)} %get-tuple-element.46, bf16[256,896]{1,0:T(8,128)(2,1)S(1)} %get-tuple-element.45), kind=kOutput, calls=%fused_computation.32 | convolution fusion | flops 471728128 | bytes 3014656 | tf_op jit(solution)/shard_map/dot_general | solution.py:199
  152.4 2.7 %collective-permute-start.17 = (bf16[256,512]{1,0:T(8,128)(2,1)}, bf16[256,512]{1,0:T(8,128)(2,1)}, u32[]{:S(2)}, u32[]{:S(2)}) collective-permute-start(bf16[256,512]{1,0:T(8,128)(2,1)} %convolution_convert_fusion.3), channel_id=1, source_target_pairs={{0,3},{1,0},{2,1},{3,2},{4,7},{5,4},{6,5},{7,6},{8,11},{9,8},{10,9... | collective-permute-start | bytes 786440 | tf_op jit(solution)/shard_map/ppermute | solution.py:20
  155.1 2.8 %convolution_convert_fusion.2 = bf16[256,512]{1,0:T(8,128)(2,1)} fusion(bf16[1792,512]{1,0:T(8,128)(2,1)} %collective-permute-done.14, bf16[256,896]{1,0:T(8,128)(2,1)S(1)} %get-tuple-element.46, bf16[256,896]{1,0:T(8,128)(2,1)S(1)} %get-tuple-element.45), kind=kOutput, calls=%fused_computation.31 | convolution fusion | flops 471728128 | bytes 3014656 | tf_op jit(solution)/shard_map/dot_general | solution.py:199
  157.9 10.0 %collective-permute-done.19 = bf16[32,2,8,896]{3,2,1,0:T(8,128)(2,1)S(1)} collective-permute-done((bf16[32,2,8,896]{3,2,1,0:T(8,128)(2,1)S(1)}, bf16[32,2,8,896]{3,2,1,0:T(8,128)(2,1)S(1)}, u32[]{:S(2)}, u32[]{:S(2)}) %collective-permute-start.19) | collective-permute-done | bytes 917536 | tf_op jit(solution)/shard_map/ppermute | solution.py:20
  169.9 1.8 fusion.37
  174.0 1.8 fusion.32
  179.7 2.1 collective-permute-done.23
  181.8 3.8 %collective-permute-done.25 = bf16[256,256]{1,0:T(8,128)(2,1)S(1)} collective-permute-done((bf16[256,256]{1,0:T(8,128)(2,1)S(1)}, bf16[256,256]{1,0:T(8,128)(2,1)S(1)}, u32[]{:S(2)}, u32[]{:S(2)}) %collective-permute-start.25) | collective-permute-done | bytes 131104 | tf_op jit(solution)/shard_map/ppermute | solution.py:20
  185.7 3.8 %fusion.11 = bf16[32,8,1792]{2,1,0:T(8,128)(2,1)} fusion(bf16[256,1792]{1,0:T(8,128)(2,1)} %collective-permute-done.15, bf16[256,1792]{1,0:T(8,128)(2,1)} %collective-permute-done.2, bf16[256,1792]{1,0:T(8,128)(2,1)} %collective-permute-done.1, bf16[256,1792]{1,0:T(8,128)(2,1)S(1)} %copy-done.5, bf16[256,256]{1,0:T(8,128)(2,1)S(1)} %collective-permute-done.25, ...), kind=kOutput, calls=%fused_computation.12 | convolution fusion | flops 956760064 | bytes 5111808 | tf_op jit(solution)/shard_map/dot_general | solution.py:209
  189.5 6.8 %all-to-all-start.3 = ((bf16[32,8,1792]{2,1,0:T(8,128)(2,1)}), bf16[32,8,1792]{2,1,0:T(8,128)(2,1)S(1)}, u32[]{:S(2)}, u32[]{:S(2)}) async-start(bf16[32,8,1792]{2,1,0:T(8,128)(2,1)} %fusion.11), calls=%async_computation.3 | async-start | bytes 1835008 | tf_op jit(solution)/shard_map/all_to_all | solution.py:97
  196.2 1.6 collective-permute-start.12
  200.3 17.9 %all-to-all-done.3 = bf16[32,8,1792]{2,1,0:T(8,128)(2,1)S(1)} async-done(((bf16[32,8,1792]{2,1,0:T(8,128)(2,1)}), bf16[32,8,1792]{2,1,0:T(8,128)(2,1)S(1)}, u32[]{:S(2)}, u32[]{:S(2)}) %all-to-all-start.3) | async-done | bytes 917536 | tf_op jit(solution)/shard_map/all_to_all | solution.py:97
  218.6 5.1 %collective-permute-start.26 = (f32[16,1792]{1,0:T(8,128)S(1)}, f32[16,1792]{1,0:T(8,128)S(1)}, u32[]{:S(2)}, u32[]{:S(2)}) collective-permute-start(f32[16,1792]{1,0:T(8,128)S(1)} %dynamic-slice_bitcast_fusion.14), channel_id=1, source_target_pairs={{0,4},{4,0},{1,5},{5,1},{2,6},{6,2},{3,7},{7,3},{8,12},{12,8},{9,1... | collective-permute-start | bytes 344072 | tf_op jit(solution)/shard_map/ppermute | solution.py:15
  (164 shorter events, 42.0 us)
Async XLA Ops:
  4.1 31.1 %collective-permute-start.1 = (bf16[256,1792]{1,0:T(8,128)(2,1)}, bf16[256,1792]{1,0:T(8,128)(2,1)}, u32[]{:S(2)}, u32[]{:S(2)}) collective-permute-start(bf16[256,1792]{1,0:T(8,128)(2,1)} %get-tuple-element.43), channel_id=1, source_target_pairs={{0,1},{1,2},{2,3},{3,0},{4,5},{5,6},{6,7},{7,4},{8,9},{9,10},{10,1... | collective-permute-start | bytes 2752520 | tf_op jit(solution)/shard_map/ppermute | solution.py:20
  6.2 28.9 %collective-permute-start.2 = (bf16[256,1792]{1,0:T(8,128)(2,1)}, bf16[256,1792]{1,0:T(8,128)(2,1)}, u32[]{:S(2)}, u32[]{:S(2)}) collective-permute-start(bf16[256,1792]{1,0:T(8,128)(2,1)} %get-tuple-element.42), channel_id=1, source_target_pairs={{0,3},{1,0},{2,1},{3,2},{4,7},{5,4},{6,5},{7,6},{8,11},{9,8},{10,9... | collective-permute-start | bytes 2752520 | tf_op jit(solution)/shard_map/ppermute | solution.py:20
  8.5 24.3 %collective-permute-start.4 = (bf16[256,896]{1,0:T(8,128)(2,1)}, bf16[256,896]{1,0:T(8,128)(2,1)}, u32[]{:S(2)}, u32[]{:S(2)}) collective-permute-start(bf16[256,896]{1,0:T(8,128)(2,1)} %constant_dynamic-slice_fusion), channel_id=1, source_target_pairs={{0,4},{4,0},{1,5},{5,1},{2,6},{6,2},{3,7},{7,3},{8,12},{12,8},{9,1... | collective-permute-start | bytes 1376264 | tf_op jit(solution)/shard_map/ppermute | solution.py:15
  14.6 24.2 %all-to-all-start = ((bf16[32,4,4,512]{3,1,2,0:T(4,128)(2,1)}), bf16[32,4,4,512]{3,1,2,0:T(4,128)(2,1)S(1)}, u32[]{:S(2)}, u32[]{:S(2)}) async-start(bf16[32,4,4,512]{3,1,2,0:T(4,128)(2,1)} %bitcast.133), calls=%async_computation | async-start | bytes 1048576 | tf_op jit(solution)/shard_map/all_to_all | solution.py:97
  23.9 8.8 %collective-permute-start.3 = (bf16[2,512,128]{2,1,0:T(8,128)(2,1)S(1)}, bf16[2,512,128]{2,1,0:T(8,128)(2,1)S(1)}, u32[]{:S(2)}, u32[]{:S(2)}) collective-permute-start(bf16[2,512,128]{2,1,0:T(8,128)(2,1)S(1)} %copy-done.10), channel_id=1, source_target_pairs={{0,4},{4,0},{1,5},{5,1},{2,6},{6,2},{3,7},{7,3},{8,12},{12,8},{9,1... | collective-permute-start | bytes 786440 | tf_op jit(solution)/shard_map/ppermute | solution.py:15
  24.3 10.9 %collective-permute-start.5 = (f32[1792]{0:T(1024)S(1)}, f32[1792]{0:T(1024)S(1)}, u32[]{:S(2)}, u32[]{:S(2)}) collective-permute-start(f32[1792]{0:T(1024)S(1)} %copy-done.12), channel_id=1, source_target_pairs={{0,2},{1,3},{2,0},{3,1},{4,6},{5,7},{6,4},{7,5},{8,10},{9,11},{10,... | collective-permute-start | bytes 21512 | tf_op jit(solution)/shard_map/ppermute | solution.py:20
  39.2 5.1 %collective-permute-start.6 = (bf16[32,4,4,128]{3,0,1,2:T(8,128)(2,1)S(1)}, bf16[32,4,4,128]{3,0,1,2:T(8,128)(2,1)S(1)}, u32[]{:S(2)}, u32[]{:S(2)}) collective-permute-start(bf16[32,4,4,128]{3,0,1,2:T(8,128)(2,1)S(1)} %fusion.35), channel_id=1, source_target_pairs={{0,1},{1,2},{2,3},{3,0},{4,5},{5,6},{6,7},{7,4},{8,9},{9,10},{10,1... | collective-permute-start | bytes 393224 | tf_op jit(solution)/shard_map/ppermute | solution.py:20
  39.4 6.4 %collective-permute-start.7 = (bf16[32,4,4,128]{3,0,1,2:T(8,128)(2,1)S(1)}, bf16[32,4,4,128]{3,0,1,2:T(8,128)(2,1)S(1)}, u32[]{:S(2)}, u32[]{:S(2)}) collective-permute-start(bf16[32,4,4,128]{3,0,1,2:T(8,128)(2,1)S(1)} %fusion.35), channel_id=1, source_target_pairs={{0,2},{1,3},{2,0},{3,1},{4,6},{5,7},{6,4},{7,5},{8,10},{9,11},{10,... | collective-permute-start | bytes 393224 | tf_op jit(solution)/shard_map/ppermute | solution.py:20
  42.0 4.6 %collective-permute-start.8 = (bf16[32,4,4,128]{3,0,1,2:T(8,128)(2,1)S(1)}, bf16[32,4,4,128]{3,0,1,2:T(8,128)(2,1)S(1)}, u32[]{:S(2)}, u32[]{:S(2)}) collective-permute-start(bf16[32,4,4,128]{3,0,1,2:T(8,128)(2,1)S(1)} %fusion.35), channel_id=1, source_target_pairs={{0,3},{1,0},{2,1},{3,2},{4,7},{5,4},{6,5},{7,6},{8,11},{9,8},{10,9... | collective-permute-start | bytes 393224 | tf_op jit(solution)/shard_map/ppermute | solution.py:20
  47.3 5.6 %collective-permute-start.9 = (bf16[32,16,512]{2,1,0:T(8,128)(2,1)S(1)}, bf16[32,16,512]{2,1,0:T(8,128)(2,1)S(1)}, u32[]{:S(2)}, u32[]{:S(2)}) collective-permute-start(bf16[32,16,512]{2,1,0:T(8,128)(2,1)S(1)} %reshape.325), channel_id=1, source_target_pairs={{0,4},{4,0},{1,5},{5,1},{2,6},{6,2},{3,7},{7,3},{8,12},{12,8},{9,1... | collective-permute-start | bytes 1572872 | tf_op jit(solution)/shard_map/ppermute | solution.py:15
  55.6 49.8 %all-to-all-start.1 = ((bf16[32,32,896]{2,1,0:T(8,128)(2,1)}), bf16[32,32,896]{2,1,0:T(8,128)(2,1)S(1)}, u32[]{:S(2)}, u32[]{:S(2)}) async-start(bf16[32,32,896]{2,1,0:T(8,128)(2,1)} %bitcast.138), calls=%async_computation.1 | async-start | bytes 3670016 | tf_op jit(solution)/shard_map/all_to_all | solution.py:97
  63.0 6.4 %collective-permute-start = (bf16[16,896]{1,0:T(8,128)(2,1)}, bf16[16,896]{1,0:T(8,128)(2,1)S(1)}, u32[]{:S(2)}, u32[]{:S(2)}) collective-permute-start(bf16[16,896]{1,0:T(8,128)(2,1)} %constant_dynamic-slice_fusion.1), channel_id=1, source_target_pairs={{0,4},{4,0},{1,5},{5,1},{2,6},{6,2},{3,7},{7,3},{8,12},{12,8},{9,1... | collective-permute-start | bytes 86024 | tf_op jit(solution)/shard_map/ppermute | solution.py:15
  63.6 1.2 collective-permute-start.11
  65.7 48.7 %collective-permute-start.13 = (bf16[1792,512]{1,0:T(8,128)(2,1)}, bf16[1792,512]{1,0:T(8,128)(2,1)}, u32[]{:S(2)}, u32[]{:S(2)}) collective-permute-start(bf16[1792,512]{1,0:T(8,128)(2,1)} %pad_maximum_fusion), channel_id=1, source_target_pairs={{0,1},{1,2},{2,3},{3,0},{4,5},{5,6},{6,7},{7,4},{8,9},{9,10},{10,1... | collective-permute-start | bytes 5505032 | tf_op jit(solution)/shard_map/ppermute | solution.py:20
  66.9 47.5 %collective-permute-start.14 = (bf16[1792,512]{1,0:T(8,128)(2,1)}, bf16[1792,512]{1,0:T(8,128)(2,1)}, u32[]{:S(2)}, u32[]{:S(2)}) collective-permute-start(bf16[1792,512]{1,0:T(8,128)(2,1)} %pad_maximum_fusion.1), channel_id=1, source_target_pairs={{0,3},{1,0},{2,1},{3,2},{4,7},{5,4},{6,5},{7,6},{8,11},{9,8},{10,9... | collective-permute-start | bytes 5505032 | tf_op jit(solution)/shard_map/ppermute | solution.py:20
  107.0 29.8 %all-to-all-start.2 = ((bf16[32,16,896]{2,1,0:T(8,128)(2,1)}), bf16[32,16,896]{2,1,0:T(8,128)(2,1)S(1)}, u32[]{:S(2)}, u32[]{:S(2)}) async-start(bf16[32,16,896]{2,1,0:T(8,128)(2,1)} %bitcast.35), calls=%async_computation.2 | async-start | bytes 1835008 | tf_op jit(solution)/shard_map/all_to_all | solution.py:97
  114.4 22.4 %collective-permute-start.15 = (bf16[256,1792]{1,0:T(8,128)(2,1)S(1)}, bf16[256,1792]{1,0:T(8,128)(2,1)}, u32[]{:S(2)}, u32[]{:S(2)}) collective-permute-start(bf16[256,1792]{1,0:T(8,128)(2,1)S(1)} %copy-done.6), channel_id=1, source_target_pairs={{0,2},{1,3},{2,0},{3,1},{4,6},{5,7},{6,4},{7,5},{8,10},{9,11},{10,... | collective-permute-start | bytes 2752520 | tf_op jit(solution)/shard_map/ppermute | solution.py:20
  136.9 9.3 %collective-permute-start.16 = (bf16[256,896]{1,0:T(8,128)(2,1)S(1)}, bf16[256,896]{1,0:T(8,128)(2,1)}, u32[]{:S(2)}, u32[]{:S(2)}) collective-permute-start(bf16[256,896]{1,0:T(8,128)(2,1)S(1)} %slice_bitcast_fusion.1), channel_id=1, source_target_pairs={{0,4},{4,0},{1,5},{5,1},{2,6},{6,2},{3,7},{7,3},{8,12},{12,8},{9,1... | collective-permute-start | bytes 1376264 | tf_op jit(solution)/shard_map/ppermute | solution.py:15
  144.5 23.5 %collective-permute-start.19 = (bf16[32,2,8,896]{3,2,1,0:T(8,128)(2,1)S(1)}, bf16[32,2,8,896]{3,2,1,0:T(8,128)(2,1)S(1)}, u32[]{:S(2)}, u32[]{:S(2)}) collective-permute-start(bf16[32,2,8,896]{3,2,1,0:T(8,128)(2,1)S(1)} %bitcast.136), channel_id=1, source_target_pairs={{0,2},{1,3},{2,0},{3,1},{4,6},{5,7},{6,4},{7,5},{8,10},{9,11},{10,... | collective-permute-start | bytes 2752520 | tf_op jit(solution)/shard_map/ppermute | solution.py:20
  147.7 24.2 %collective-permute-start.21 = (f32[256]{0:T(256)S(1)}, f32[256]{0:T(256)S(1)}, u32[]{:S(2)}, u32[]{:S(2)}) collective-permute-start(f32[256]{0:T(256)S(1)} %multiply_reduce_fusion), channel_id=1, source_target_pairs={{0,3},{1,0},{2,1},{3,2},{4,7},{5,4},{6,5},{7,6},{8,11},{9,8},{10,9... | collective-permute-start | bytes 3080 | tf_op jit(solution)/shard_map/ppermute | solution.py:20
  149.6 22.4 %collective-permute-start.22 = (f32[256]{0:T(256)S(1)}, f32[256]{0:T(256)S(1)}, u32[]{:S(2)}, u32[]{:S(2)}) collective-permute-start(f32[256]{0:T(256)S(1)} %multiply_reduce_fusion), channel_id=1, source_target_pairs={{0,1},{1,2},{2,3},{3,0},{4,5},{5,6},{6,7},{7,4},{8,9},{9,10},{10,1... | collective-permute-start | bytes 3080 | tf_op jit(solution)/shard_map/ppermute | solution.py:20
  152.4 21.3 %collective-permute-start.17 = (bf16[256,512]{1,0:T(8,128)(2,1)}, bf16[256,512]{1,0:T(8,128)(2,1)}, u32[]{:S(2)}, u32[]{:S(2)}) collective-permute-start(bf16[256,512]{1,0:T(8,128)(2,1)} %convolution_convert_fusion.3), channel_id=1, source_target_pairs={{0,3},{1,0},{2,1},{3,2},{4,7},{5,4},{6,5},{7,6},{8,11},{9,8},{10,9... | collective-permute-start | bytes 786440 | tf_op jit(solution)/shard_map/ppermute | solution.py:20
  157.9 16.1 %collective-permute-start.18 = (bf16[256,512]{1,0:T(8,128)(2,1)}, bf16[256,512]{1,0:T(8,128)(2,1)}, u32[]{:S(2)}, u32[]{:S(2)}) collective-permute-start(bf16[256,512]{1,0:T(8,128)(2,1)} %convolution_convert_fusion.2), channel_id=1, source_target_pairs={{0,1},{1,2},{2,3},{3,0},{4,5},{5,6},{6,7},{7,4},{8,9},{9,10},{10,1... | collective-permute-start | bytes 786440 | tf_op jit(solution)/shard_map/ppermute | solution.py:20
  168.0 3.7 %collective-permute-start.20 = (bf16[256,896]{1,0:T(8,128)(2,1)S(1)}, bf16[256,896]{1,0:T(8,128)(2,1)S(1)}, u32[]{:S(2)}, u32[]{:S(2)}) collective-permute-start(bf16[256,896]{1,0:T(8,128)(2,1)S(1)} %slice_bitcast_fusion), channel_id=1, source_target_pairs={{0,4},{4,0},{1,5},{5,1},{2,6},{6,2},{3,7},{7,3},{8,12},{12,8},{9,1... | collective-permute-start | bytes 1376264 | tf_op jit(solution)/shard_map/ppermute | solution.py:15
  174.0 11.6 %copy-start.5 = (bf16[256,1792]{1,0:T(8,128)(2,1)S(1)}, bf16[256,1792]{1,0:T(8,128)(2,1)}, u32[]{:S(2)}) copy-start(bf16[256,1792]{1,0:T(8,128)(2,1)} %get-tuple-element.41) | copy-start | bytes 2752516
  176.0 5.8 %collective-permute-start.23 = (bf16[256,256]{1,0:T(8,128)(2,1)S(1)}, bf16[256,256]{1,0:T(8,128)(2,1)S(1)}, u32[]{:S(2)}, u32[]{:S(2)}) collective-permute-start(bf16[256,256]{1,0:T(8,128)(2,1)S(1)} %fusion.63), channel_id=1, source_target_pairs={{0,1},{1,2},{2,3},{3,0},{4,5},{5,6},{6,7},{7,4},{8,9},{9,10},{10,1... | collective-permute-start | bytes 393224 | tf_op jit(solution)/shard_map/ppermute | solution.py:20
  177.2 4.6 %collective-permute-start.24 = (bf16[256,256]{1,0:T(8,128)(2,1)S(1)}, bf16[256,256]{1,0:T(8,128)(2,1)S(1)}, u32[]{:S(2)}, u32[]{:S(2)}) collective-permute-start(bf16[256,256]{1,0:T(8,128)(2,1)S(1)} %fusion.63), channel_id=1, source_target_pairs={{0,3},{1,0},{2,1},{3,2},{4,7},{5,4},{6,5},{7,6},{8,11},{9,8},{10,9... | collective-permute-start | bytes 393224 | tf_op jit(solution)/shard_map/ppermute | solution.py:20
  178.7 6.9 %collective-permute-start.25 = (bf16[256,256]{1,0:T(8,128)(2,1)S(1)}, bf16[256,256]{1,0:T(8,128)(2,1)S(1)}, u32[]{:S(2)}, u32[]{:S(2)}) collective-permute-start(bf16[256,256]{1,0:T(8,128)(2,1)S(1)} %fusion.63), channel_id=1, source_target_pairs={{0,2},{1,3},{2,0},{3,1},{4,6},{5,7},{6,4},{7,5},{8,10},{9,11},{10,... | collective-permute-start | bytes 393224 | tf_op jit(solution)/shard_map/ppermute | solution.py:20
  189.5 28.8 %all-to-all-start.3 = ((bf16[32,8,1792]{2,1,0:T(8,128)(2,1)}), bf16[32,8,1792]{2,1,0:T(8,128)(2,1)S(1)}, u32[]{:S(2)}, u32[]{:S(2)}) async-start(bf16[32,8,1792]{2,1,0:T(8,128)(2,1)} %fusion.11), calls=%async_computation.3 | async-start | bytes 1835008 | tf_op jit(solution)/shard_map/all_to_all | solution.py:97
  196.2 2.5 %collective-permute-start.12 = (bf16[16,8]{1,0:T(8,128)(2,1)S(1)}, bf16[16,8]{1,0:T(8,128)(2,1)S(1)}, u32[]{:S(2)}, u32[]{:S(2)}) collective-permute-start(bf16[16,8]{1,0:T(8,128)(2,1)S(1)} %bitcast.148), channel_id=1, source_target_pairs={{0,4},{4,0},{1,5},{5,1},{2,6},{6,2},{3,7},{7,3},{8,12},{12,8},{9,1... | collective-permute-start | bytes 776 | tf_op jit(solution)/shard_map/ppermute | solution.py:15
  199.0 1.3 collective-permute-start.10
  218.6 6.1 %collective-permute-start.26 = (f32[16,1792]{1,0:T(8,128)S(1)}, f32[16,1792]{1,0:T(8,128)S(1)}, u32[]{:S(2)}, u32[]{:S(2)}) collective-permute-start(f32[16,1792]{1,0:T(8,128)S(1)} %dynamic-slice_bitcast_fusion.14), channel_id=1, source_target_pairs={{0,4},{4,0},{1,5},{5,1},{2,6},{6,2},{3,7},{7,3},{8,12},{12,8},{9,1... | collective-permute-start | bytes 344072 | tf_op jit(solution)/shard_map/ppermute | solution.py:15
  (17 other events, 120.4 us)
